TPU v7x, 32 devices: a whole 2x2x4 slice. The times are simulated.
32 devices in a mesh: dp: 8 (over z, x), mp: 4 (over y, core).
Axes of the slice: x: 2, y: 2, z: 4, core: 2. Of those that a mesh axis runs over, the one named last changes fastest.
Arguments:
- inputs: bfloat16 [8192, 768], P('dp'), may hold values from -6 to 6
- page_feat: bfloat16 [8, 8, 768], P('dp'), may hold values from -6 to 6
- page_onehot: int32 [8192, 8], P('dp'), may hold values from 0 to 1, as said below
- lengths: int32 [8], P('dp'), may hold values from 256 to 1024, as said below
- hor_pos: int32 [8192], P('dp'), may hold values from 0 to 999
- ver_pos: int32 [8192], P('dp'), may hold values from 0 to 999
- norm1_gain: bfloat16 [768], replicated, may hold values from 0.099609375 to 1.8984375
- w_query: bfloat16 [768, 768], P(None, 'mp'), may hold values from -0.21875 to 0.21875
- w_key: bfloat16 [768, 768], P(None, 'mp'), may hold values from -0.21875 to 0.21875
- w_value: bfloat16 [768, 768], P(None, 'mp'), may hold values from -0.21875 to 0.21875
- rel_table: bfloat16 [12, 32], P('mp'), may hold values from -4 to 4
- hor_table: bfloat16 [12, 32], P('mp'), may hold values from -4 to 4
- ver_table: bfloat16 [12, 32], P('mp'), may hold values from -4 to 4
- w_output: bfloat16 [768, 768], P('mp'), may hold values from -0.875 to 0.875
- norm2_gain: bfloat16 [768], replicated, may hold values from 0.099609375 to 1.8984375
- w_up: bfloat16 [768, 3072], P(None, 'mp'), may hold values from -0.21875 to 0.21875
- w_down: bfloat16 [3072, 768], P('mp'), may hold values from -0.15625 to 0.15625
- cotangent: bfloat16 [8192, 768], P('dp'), may hold values from -6 to 6
Outputs:
- output: bfloat16 [8192, 768], P('dp')
- grad_inputs: float32 [8192, 768], P('dp')
- grad_page_feat: float32 [8, 8, 768], P('dp')
- grad_norm1_gain: float32 [768], P('dp')
- grad_w_query: float32 [768, 768], P('dp', 'mp')
- grad_w_key: float32 [768, 768], P('dp', 'mp')
- grad_w_value: float32 [768, 768], P('dp', 'mp')
- grad_rel_table: float32 [12, 32], P('mp')
- grad_hor_table: float32 [12, 32], P('mp')
- grad_ver_table: float32 [12, 32], P('mp')
- grad_w_output: float32 [768, 768], P('mp', 'dp')
- grad_norm2_gain: float32 [768], P('dp')
- grad_w_up: float32 [768, 3072], P('dp', 'mp')
- grad_w_down: float32 [3072, 768], P('mp', 'dp')
Inputs may be any that keep to these rules, and one draw needn't show every extreme that they name: `lengths`: keys at or past a sequence's length are padding; in every draw some sequence uses all 1024 slots. `page_onehot`: each row has exactly one 1; within a sequence the page number never falls from one token to the next.
All inputs are finite; a program needn't handle non-finite values.
Results may differ from a plain program's by a relative error of at most 0.012.
Values may be sent and summed in bfloat16 or wider, within the bound.
No kernel may reach another device: no remote copies, remote signals or barrier semaphores. Data moves between devices by JAX's collectives and lax.ppermute only.
A program may use at most 192 MiB of HBM per device.

v0:
```python
import jax
import jax.numpy as jnp
from jax import lax
from jax.sharding import PartitionSpec as P

EPS = 1e-06
THRESHOLDS = (12, 16, 23, 32, 46, 64, 91)


def bucket(delta):
    magnitude = jnp.abs(delta)
    coarse = 8 + sum(((magnitude >= limit).astype(jnp.int32) for limit in THRESHOLDS))
    return jnp.where(magnitude < 8, magnitude, coarse) + 16 * (delta > 0).astype(jnp.int32)


def unit_rows(field):
    factor = lax.rsqrt(jnp.mean(field * field, axis=-1, keepdims=True) + EPS)
    return (field * factor, factor)


def norm_back(grad_normed, unit, factor, gain_row):
    scaled = grad_normed * gain_row
    grad_field = factor * (scaled - unit * jnp.mean(scaled * unit, axis=-1, keepdims=True))
    return (grad_field, jnp.sum(grad_normed * unit, axis=0))


def pair_ids(start, count, hor_seq, ver_seq):
    positions = jnp.arange(hor_seq.shape[0], dtype=jnp.int32)
    rel_ids = bucket(positions[None, :] - positions[start : start + count, None])
    hor_ids = bucket(hor_seq[None, :] - hor_seq[start : start + count, None])
    ver_ids = bucket(ver_seq[None, :] - ver_seq[start : start + count, None])
    return (rel_ids, hor_ids, ver_ids)


def one_hot_ids(table_ids, bucket_count):
    return (
        table_ids[None, :, :] == jnp.arange(bucket_count, dtype=jnp.int32)[:, None, None]
    ).astype(jnp.bfloat16)


def block_scores(query_block, key_heads, tables, ids, valid):
    scores = (
        jnp.einsum("qhd,khd->hqk", query_block, key_heads, preferred_element_type=jnp.float32)
        * 0.125
    )
    bias_sum = None
    for table, table_ids in zip(tables, ids):
        term = jnp.einsum(
            "ngo,sn->sgo",
            one_hot_ids(table_ids, table.shape[1]),
            table,
            preferred_element_type=jnp.float32,
        )
        bias_sum = term if bias_sum is None else bias_sum + term
    return jnp.where(valid[None, None, :], scores + bias_sum, -1e30)


def attend(queries, key_rows, value_rows, tables, hor_seq, ver_seq, length, head_count):
    seq_len, width = queries.shape
    head_size = width // head_count
    block_rows = min(512, seq_len)
    key_heads = key_rows.reshape(seq_len, head_count, head_size)
    value_heads = value_rows.reshape(seq_len, head_count, head_size)
    valid = jnp.arange(seq_len) < length
    pieces, log_parts = ([], [])
    for start in range(0, seq_len, block_rows):
        query_block = queries[start : start + block_rows].reshape(block_rows, head_count, head_size)
        ids = pair_ids(start, block_rows, hor_seq, ver_seq)
        scores = block_scores(query_block, key_heads, tables, ids, valid)
        peak = jnp.max(scores, axis=-1, keepdims=True)
        expo = jnp.exp(scores - peak)
        norm_sum = jnp.sum(expo, axis=-1, keepdims=True)
        probs = (expo / norm_sum).astype(jnp.bfloat16)
        block_out = jnp.einsum(
            "hqk,khd->qhd", probs, value_heads, preferred_element_type=jnp.float32
        )
        pieces.append(block_out.reshape(block_rows, width))
        log_parts.append(peak + jnp.log(norm_sum))
    return (
        jnp.concatenate(pieces, axis=0).astype(jnp.bfloat16),
        jnp.concatenate(log_parts, axis=1),
    )


def attend_back(
    queries,
    key_rows,
    value_rows,
    tables,
    hor_seq,
    ver_seq,
    length,
    head_count,
    log_totals,
    grad_attended,
):
    seq_len, width = queries.shape
    head_size = width // head_count
    block_rows = min(512, seq_len)
    key_heads = key_rows.reshape(seq_len, head_count, head_size)
    value_heads = value_rows.reshape(seq_len, head_count, head_size)
    valid = jnp.arange(seq_len) < length
    grad_key = jnp.zeros((seq_len, head_count, head_size), jnp.float32)
    grad_value = jnp.zeros((seq_len, head_count, head_size), jnp.float32)
    grad_tables = [jnp.zeros(table.shape, jnp.float32) for table in tables]
    query_parts = []
    for start in range(0, seq_len, block_rows):
        query_block = queries[start : start + block_rows].reshape(block_rows, head_count, head_size)
        grad_block = grad_attended[start : start + block_rows].reshape(
            block_rows, head_count, head_size
        )
        ids = pair_ids(start, block_rows, hor_seq, ver_seq)
        scores = block_scores(query_block, key_heads, tables, ids, valid)
        probs = jnp.exp(scores - log_totals[:, start : start + block_rows])
        grad_probs = jnp.einsum(
            "qhd,khd->hqk", grad_block, value_heads, preferred_element_type=jnp.float32
        )
        inner = jnp.sum(probs * grad_probs, axis=-1, keepdims=True)
        grad_scores = (probs * (grad_probs - inner)).astype(jnp.bfloat16)
        query_part = (
            jnp.einsum("hqk,khd->qhd", grad_scores, key_heads, preferred_element_type=jnp.float32)
            * 0.125
        )
        query_parts.append(query_part.reshape(block_rows, width))
        grad_key = (
            grad_key
            + jnp.einsum(
                "hqk,qhd->khd", grad_scores, query_block, preferred_element_type=jnp.float32
            )
            * 0.125
        )
        grad_value = grad_value + jnp.einsum(
            "hqk,qhd->khd",
            probs.astype(jnp.bfloat16),
            grad_block,
            preferred_element_type=jnp.float32,
        )
        for which in range(len(tables)):
            grad_tables[which] = grad_tables[which] + jnp.einsum(
                "pkm,fkm->pf",
                grad_scores,
                one_hot_ids(ids[which], tables[which].shape[1]),
                preferred_element_type=jnp.float32,
            )
    grad_queries = jnp.concatenate(query_parts, axis=0).astype(jnp.bfloat16)
    return (
        grad_queries,
        grad_key.reshape(seq_len, width).astype(jnp.bfloat16),
        grad_value.reshape(seq_len, width).astype(jnp.bfloat16),
        grad_tables,
    )


def local(
    inputs,
    page_feat,
    page_onehot,
    lengths,
    hor_pos,
    ver_pos,
    norm1_gain,
    w_query,
    w_key,
    w_value,
    rel_table,
    hor_table,
    ver_table,
    w_output,
    norm2_gain,
    w_up,
    w_down,
    cotangent,
):
    head_count = rel_table.shape[0]
    tables = (rel_table, hor_table, ver_table)
    gain_one = norm1_gain.astype(jnp.float32)
    gain_two = norm2_gain.astype(jnp.float32)
    index = 0
    onehot = page_onehot.astype(jnp.bfloat16)
    hidden_x = inputs.astype(jnp.float32) + jnp.dot(
        onehot, page_feat[index], preferred_element_type=jnp.float32
    )
    unit_one, factor_one = unit_rows(hidden_x)
    normed1 = (unit_one * gain_one).astype(jnp.bfloat16)
    queries = jnp.dot(normed1, w_query, preferred_element_type=jnp.float32).astype(jnp.bfloat16)
    key_rows = jnp.dot(normed1, w_key, preferred_element_type=jnp.float32).astype(jnp.bfloat16)
    value_rows = jnp.dot(normed1, w_value, preferred_element_type=jnp.float32).astype(jnp.bfloat16)
    hor_seq = hor_pos
    ver_seq = ver_pos
    attended, log_totals = attend(
        queries, key_rows, value_rows, tables, hor_seq, ver_seq, lengths[index], head_count
    )
    attn_terms = jnp.dot(attended, w_output, preferred_element_type=jnp.float32)
    mixed = hidden_x + lax.psum(attn_terms, "mp")
    unit_two, factor_two = unit_rows(mixed)
    normed2 = (unit_two * gain_two).astype(jnp.bfloat16)
    upward = jnp.dot(normed2, w_up, preferred_element_type=jnp.float32)
    activated = jax.nn.gelu(upward).astype(jnp.bfloat16)
    ffn_terms = jnp.dot(activated, w_down, preferred_element_type=jnp.float32)
    result = mixed + lax.psum(ffn_terms, "mp")
    outputs = result.astype(jnp.bfloat16)
    kept_up = upward
    saved = [
        (
            onehot,
            unit_one,
            factor_one,
            normed1,
            queries,
            key_rows,
            value_rows,
            hor_seq,
            ver_seq,
            attended,
            log_totals,
            unit_two,
            factor_two,
            normed2,
            kept_up,
        )
    ]
    index = 0
    (
        onehot,
        unit_one,
        factor_one,
        normed1,
        queries,
        key_rows,
        value_rows,
        hor_seq,
        ver_seq,
        attended,
        log_totals,
        unit_two,
        factor_two,
        normed2,
        kept_up,
    ) = saved[index]
    upward = kept_up
    activated, gelu_back = jax.vjp(jax.nn.gelu, upward)
    grad_activated = jnp.einsum("td,fd->tf", cotangent, w_down, preferred_element_type=jnp.float32)
    grad_up = gelu_back(grad_activated)[0].astype(jnp.bfloat16)
    grad_w_down = jnp.einsum(
        "tf,td->fd", activated.astype(jnp.bfloat16), cotangent, preferred_element_type=jnp.float32
    )
    grad_w_up = jnp.einsum("td,tf->df", normed2, grad_up, preferred_element_type=jnp.float32)
    normed_terms = jnp.einsum("tf,df->td", grad_up, w_up, preferred_element_type=jnp.float32)
    grad_normed2 = lax.psum(normed_terms, "mp")
    grad_field, gain_part = norm_back(grad_normed2, unit_two, factor_two, gain_two)
    grad_gain_two = gain_part
    mixed_grads = [cotangent.astype(jnp.float32) + grad_field]
    table_sums = [jnp.zeros(table.shape, jnp.float32) for table in tables]
    index = 0
    (
        onehot,
        unit_one,
        factor_one,
        normed1,
        queries,
        key_rows,
        value_rows,
        hor_seq,
        ver_seq,
        attended,
        log_totals,
        unit_two,
        factor_two,
        normed2,
        kept_up,
    ) = saved[index]
    grad_mixed = mixed_grads[index]
    mixed_low = grad_mixed.astype(jnp.bfloat16)
    grad_w_output = jnp.einsum("tc,td->cd", attended, mixed_low, preferred_element_type=jnp.float32)
    grad_attended = jnp.einsum(
        "td,cd->tc", mixed_low, w_output, preferred_element_type=jnp.float32
    ).astype(jnp.bfloat16)
    grad_queries, grad_keys, grad_values, table_parts = attend_back(
        queries,
        key_rows,
        value_rows,
        tables,
        hor_seq,
        ver_seq,
        lengths[index],
        head_count,
        log_totals,
        grad_attended,
    )
    for which in range(len(tables)):
        table_sums[which] = table_parts[which]
    grad_w_query = jnp.einsum(
        "td,tc->dc", normed1, grad_queries, preferred_element_type=jnp.float32
    )
    grad_w_key = jnp.einsum("td,tc->dc", normed1, grad_keys, preferred_element_type=jnp.float32)
    grad_w_value = jnp.einsum("td,tc->dc", normed1, grad_values, preferred_element_type=jnp.float32)
    normed_terms = jnp.einsum(
        "tc,dc->td", grad_queries, w_query, preferred_element_type=jnp.float32
    )
    normed_terms = normed_terms + jnp.einsum(
        "tc,dc->td", grad_keys, w_key, preferred_element_type=jnp.float32
    )
    normed_terms = normed_terms + jnp.einsum(
        "tc,dc->td", grad_values, w_value, preferred_element_type=jnp.float32
    )
    grad_normed1 = lax.psum(normed_terms.astype(jnp.bfloat16), "mp").astype(jnp.float32)
    grad_field, gain_part = norm_back(grad_normed1, unit_one, factor_one, gain_one)
    grad_rows = grad_mixed + grad_field
    feat_grads = [jnp.dot(onehot.astype(jnp.float32).T, grad_rows, precision=lax.Precision.HIGHEST)]
    (
        sent_query,
        sent_key,
        sent_value,
        sent_output,
        sent_gain_one,
        sent_up,
        sent_down,
        sent_gain_two,
    ) = (
        lax.psum_scatter(grad_w_query, "dp", scatter_dimension=0, tiled=True),
        lax.psum_scatter(grad_w_key, "dp", scatter_dimension=0, tiled=True),
        lax.psum_scatter(grad_w_value, "dp", scatter_dimension=0, tiled=True),
        lax.psum_scatter(grad_w_output, "dp", scatter_dimension=1, tiled=True),
        lax.psum_scatter(gain_part, "dp", scatter_dimension=0, tiled=True),
        lax.psum_scatter(grad_w_up, "dp", scatter_dimension=0, tiled=True),
        lax.psum_scatter(grad_w_down, "dp", scatter_dimension=1, tiled=True),
        lax.psum_scatter(grad_gain_two, "dp", scatter_dimension=0, tiled=True),
    )
    sent_rel, sent_hor, sent_ver = lax.psum((table_sums[0], table_sums[1], table_sums[2]), "dp")
    return (
        outputs,
        grad_rows,
        jnp.stack(feat_grads, axis=0),
        sent_gain_one,
        sent_query,
        sent_key,
        sent_value,
        sent_rel,
        sent_hor,
        sent_ver,
        sent_output,
        sent_gain_two,
        sent_up,
        sent_down,
    )


def solution(mesh):
    return jax.shard_map(
        local,
        mesh=mesh,
        in_specs=(
            P("dp", None),
            P("dp", None, None),
            P("dp", None),
            P("dp"),
            P("dp"),
            P("dp"),
            P(),
            P(None, "mp"),
            P(None, "mp"),
            P(None, "mp"),
            P("mp", None),
            P("mp", None),
            P("mp", None),
            P("mp", None),
            P(),
            P(None, "mp"),
            P("mp", None),
            P("dp", None),
        ),
        out_specs=(
            P("dp", None),
            P("dp", None),
            P("dp", None, None),
            P("dp"),
            P("dp", "mp"),
            P("dp", "mp"),
            P("dp", "mp"),
            P("mp", None),
            P("mp", None),
            P("mp", None),
            P("mp", "dp"),
            P("dp"),
            P("dp", "mp"),
            P("mp", "dp"),
        ),
        check_vma=False,
    )
```

profile of v0, /device:TPU:0, one launch (start us, length us, event | category | flops | bytes accessed | tf_op | source)
XLA Modules:
  0.0 844.7 jit_solution(3242733492916511745)
XLA Ops:
  15.4 5.3 fusion.87
  20.8 11.7 %fusion.7 = f32[512,1024,3]{1,2,0:T(4,128)} fusion(s32[512,1024]{1,0:T(8,128)S(1)} %get-tuple-element.65, bf16[3,32]{1,0:T(4,128)(2,1)S(1)} %copy-done.67), kind=kOutput, calls=%fused_computation.11 | convolution fusion | flops 117440512 | bytes 8388800 | tf_op jit(solution)/shard_map/ngo,sn->sgo/dot_general | solution.py:48
  32.4 11.5 %fusion.1 = f32[512,1024,3]{1,2,0:T(4,128)S(1)} fusion(s32[512,1024]{1,0:T(8,128)} %get-tuple-element.66, bf16[3,32]{1,0:T(4,128)(2,1)S(1)} %copy-done.67), kind=kOutput, calls=%fused_computation.2 | convolution fusion | flops 117440512 | bytes 8388800 | tf_op jit(solution)/shard_map/ngo,sn->sgo/dot_general | solution.py:48
  43.9 5.5 fusion.86
  49.5 12.7 %fusion.9 = f32[512,1024,3]{1,2,0:T(4,128)} fusion(s32[512,1024]{1,0:T(8,128)} %get-tuple-element.61, bf16[3,32]{1,0:T(4,128)(2,1)S(1)} %copy-done.68), kind=kOutput, calls=%fused_computation.14 | convolution fusion | flops 117440512 | bytes 8388800 | tf_op jit(solution)/shard_map/ngo,sn->sgo/dot_general | solution.py:48
  62.2 13.1 %fusion.3 = f32[512,1024,3]{1,2,0:T(4,128)} fusion(s32[512,1024]{1,0:T(8,128)} %get-tuple-element.62, bf16[3,32]{1,0:T(4,128)(2,1)S(1)} %copy-done.68), kind=kOutput, calls=%fused_computation.5 | convolution fusion | flops 117440512 | bytes 8388800 | tf_op jit(solution)/shard_map/ngo,sn->sgo/dot_general | solution.py:48
  78.8 11.7 %fusion.11 = f32[512,1024,3]{1,2,0:T(4,128)} fusion(s32[512,1024]{1,0:T(8,128)S(1)} %fusion.85, bf16[3,32]{1,0:T(4,128)(2,1)S(1)} %copy-done.69), kind=kOutput, calls=%fused_computation.17 | convolution fusion | flops 117440512 | bytes 8388800 | tf_op jit(solution)/shard_map/ngo,sn->sgo/dot_general | solution.py:48
  90.5 12.7 %fusion.5 = f32[512,1024,3]{1,2,0:T(4,128)} fusion(s32[512,1024]{1,0:T(8,128)} %fusion.88, bf16[3,32]{1,0:T(4,128)(2,1)S(1)} %copy-done.69), kind=kOutput, calls=%fused_computation.8 | convolution fusion | flops 117440512 | bytes 8388800 | tf_op jit(solution)/shard_map/ngo,sn->sgo/dot_general | solution.py:48
  103.2 20.1 %fusion.175 = (f32[3,512]{1,0:T(4,128)S(1)}, f32[3,512,1024]{2,1,0:T(8,128)S(1)}) fusion(f32[512,1024,3]{1,2,0:T(4,128)} %fusion.7, f32[512,1024,3]{1,2,0:T(4,128)} %fusion.9, f32[512,1024,3]{1,2,0:T(4,128)} %fusion.11, bf16[512,3,64]{0,2,1:T(8,128)(2,1)S(1)} %bitcast.145, bf16[1024,3,64]{0,2,1:T(8,128)(2,1)S(1)} %bitcast.131, ...), kind=kOutput, calls=%fused_computation.222 | convolution fusion | flops 210762240 | bytes 25762816 | tf_op jit(solution)/shard_map/qhd,khd->hqk/dot_general | solution.py:43
  127.7 17.1 %fusion.174 = (f32[3,512]{1,0:T(4,128)S(1)}, f32[3,512,1024]{2,1,0:T(8,128)S(1)}) fusion(f32[512,1024,3]{1,2,0:T(4,128)S(1)} %fusion.1, f32[512,1024,3]{1,2,0:T(4,128)} %fusion.3, f32[512,1024,3]{1,2,0:T(4,128)} %fusion.5, bf16[512,3,64]{0,2,1:T(8,128)(2,1)S(1)} %bitcast.143, bf16[1024,3,64]{0,2,1:T(8,128)(2,1)S(1)} %bitcast.132, ...), kind=kOutput, calls=%fused_computation.221 | convolution fusion | flops 210762240 | bytes 25762816 | tf_op jit(solution)/shard_map/qhd,khd->hqk/dot_general | solution.py:43
  152.6 4.8 fusion.176
  157.4 66.0 %all-reduce.8.cloned.1.call-done = f32[1024,768]{0,1:T(8,128)} async-done(((f32[1024,768]{0,1:T(8,128)}), f32[1024,768]{0,1:T(8,128)}) %all-reduce.8.cloned.1.call-update) | async-done | bytes 3145744 | tf_op jit(solution)/shard_map/psum | solution.py:194
  223.4 4.1 multiply_reduce_fusion.4
  240.4 117.1 %all-reduce.12.cloned.1.call-done = (f32[1024,768]{0,1:T(8,128)}, f32[1024,768]{0,1:T(8,128)}) async-done(((f32[1024,768]{0,1:T(8,128)}, f32[1024,768]{0,1:T(8,128)}), (f32[1024,768]{0,1:T(8,128)}, f32[1024,768]{0,1:T(8,128)})) %all-reduce.12.cloned.1.call-update) | async-done | bytes 6291472 | tf_op jit(solution)/shard_map/psum | solution.py:200
  357.5 4.4 multiply_reduce_fusion.2
  362.2 4.8 multiply_add_fusion
  396.7 5.3 fusion.166
  403.3 5.7 fusion.168
  409.0 16.0 %fusion.127 = f32[3,32]{1,0:T(4,128)S(1)} fusion(s32[512,1024]{1,0:T(8,128)S(1)} %copy-done.22, bf16[3,512,1024]{2,1,0:T(8,128)(2,1)} %copy-done.8), kind=kOutput, calls=%fused_computation.179 | convolution fusion | flops 117440512 | bytes 5243264 | tf_op jit(solution)/shard_map/pkm,fkm->pf/dot_general | solution.py:139
  425.0 14.5 %fusion.124 = f32[3,32]{1,0:T(4,128)S(1)} fusion(s32[512,1024]{1,0:T(8,128)S(1)} %copy-done.23, bf16[3,512,1024]{2,1,0:T(8,128)(2,1)S(1)} %copy-done.9), kind=kOutput, calls=%fused_computation.178 | convolution fusion | flops 117440512 | bytes 5243264 | tf_op jit(solution)/shard_map/pkm,fkm->pf/dot_general | solution.py:139
  439.6 14.7 %fusion.121 = f32[3,32]{1,0:T(4,128)S(1)} fusion(s32[512,1024]{1,0:T(8,128)S(1)} %copy-done.18, bf16[3,512,1024]{2,1,0:T(8,128)(2,1)S(1)} %copy-done.9), kind=kOutput, calls=%fused_computation.177 | convolution fusion | flops 117440512 | bytes 5243264 | tf_op jit(solution)/shard_map/pkm,fkm->pf/dot_general | solution.py:139
  455.8 16.2 %fusion.139 = f32[3,32]{1,0:T(4,128)S(1)} fusion(f32[3,32]{1,0:T(4,128)S(1)} %fusion.127, s32[512,1024]{1,0:T(8,128)} %get-tuple-element.66, bf16[3,512,1024]{2,1,0:T(8,128)(2,1)} %copy-done.6), kind=kOutput, calls=%fused_computation.183 | convolution fusion | flops 117440608 | bytes 5243648 | tf_op jit(solution)/shard_map/pkm,fkm->pf/dot_general | solution.py:139
  472.1 14.7 %fusion.142 = f32[3,32]{1,0:T(4,128)S(1)} fusion(f32[3,32]{1,0:T(4,128)S(1)} %fusion.124, s32[512,1024]{1,0:T(8,128)S(1)} %copy-done.20, bf16[3,512,1024]{2,1,0:T(8,128)(2,1)S(1)} %copy-done.7), kind=kOutput, calls=%fused_computation.184 | convolution fusion | flops 117440608 | bytes 5243648 | tf_op jit(solution)/shard_map/pkm,fkm->pf/dot_general | solution.py:139
  486.8 14.7 %fusion.145 = f32[3,32]{1,0:T(4,128)S(1)} fusion(f32[3,32]{1,0:T(4,128)S(1)} %fusion.121, s32[512,1024]{1,0:T(8,128)S(1)} %copy-done.19, bf16[3,512,1024]{2,1,0:T(8,128)(2,1)S(1)} %copy-done.7), kind=kOutput, calls=%fused_computation.185 | convolution fusion | flops 117440608 | bytes 5243648 | tf_op jit(solution)/shard_map/pkm,fkm->pf/dot_general | solution.py:139
  505.2 37.1 %all-reduce.2 = (f32[768]{0:T(1024)S(1)}, f32[3,32]{1,0:T(4,128)}, f32[3,32]{1,0:T(4,128)}, f32[3,32]{1,0:T(4,128)}, f32[768]{0:T(1024)S(1)}) all-reduce(f32[768]{0:T(1024)S(1)} %get-tuple-element.44, f32[3,32]{1,0:T(4,128)S(1)} %fusion.145, f32[3,32]{1,0:T(4,128)S(1)} %fusion.142, ...), channel_id=2, replica_groups=mesh['dp'=8,'mp'=4] {'dp'}, use_global_device_ids=true, to_apply=%region_15.16.clone | all-reduce | flops 1824 | bytes 14592
  543.5 5.2 fusion.40
  552.3 4.0 convolution_bitcast_fusion.1
  558.0 4.5 reduce-scatter.13.cloned.1.call-done
  562.5 65.2 %reduce-scatter.9.cloned.1.call-done = f32[96,192]{1,0:T(8,128)} async-done(((f32[768,192]{1,0:T(8,128)}), f32[96,192]{1,0:T(8,128)}) %reduce-scatter.9.cloned.1.call-update) | async-done | bytes 73744 | tf_op jit(solution)/shard_map/reduce_scatter | solution.py:320
  627.7 65.8 %reduce-scatter.11.cloned.1.call-done = f32[96,192]{1,0:T(8,128)} async-done(((f32[768,192]{1,0:T(8,128)}), f32[96,192]{1,0:T(8,128)}) %reduce-scatter.11.cloned.1.call-update) | async-done | bytes 73744 | tf_op jit(solution)/shard_map/reduce_scatter | solution.py:321
  693.5 72.1 %reduce-scatter.15.cloned.1.call-done = f32[96,768]{1,0:T(8,128)} async-done(((f32[768,768]{1,0:T(8,128)}), f32[96,768]{1,0:T(8,128)}) %reduce-scatter.15.cloned.1.call-update) | async-done | bytes 294928 | tf_op jit(solution)/shard_map/reduce_scatter | solution.py:325
  765.6 72.1 %reduce-scatter.17.cloned.1.call-done = f32[768,96]{0,1:T(8,128)} async-done(((f32[768,768]{0,1:T(8,128)}), f32[768,96]{0,1:T(8,128)}) %reduce-scatter.17.cloned.1.call-update) | async-done | bytes 294928 | tf_op jit(solution)/shard_map/reduce_scatter | solution.py:326
  (237 shorter events, 77.6 us)
Async XLA Ops:
  7.2 220.4 %copy-start = (bf16[768,768]{1,0:T(8,128)(2,1)S(1)}, bf16[768,768]{1,0:T(8,128)(2,1)}, u32[]{:S(2)}) copy-start(bf16[768,768]{1,0:T(8,128)(2,1)} %param.33) | copy-start | bytes 3538948
  7.2 216.2 %all-reduce.8.cloned.1.call-start = ((), (), s32[]{:S(2)}) async-start(), calls=%async_computation.6 | async-start | bytes 6291456 | tf_op jit(solution)/shard_map/psum | solution.py:194
  12.0 91.2 %copy-start.24 = (bf16[512,192]{0,1:T(8,128)(2,1)}, bf16[512,192]{0,1:T(8,128)(2,1)S(1)}, u32[]{:S(2)}) copy-start(bf16[512,192]{0,1:T(8,128)(2,1)S(1)} %get-tuple-element.59) | copy-start | bytes 589828
  12.0 115.6 %copy-start.15 = (bf16[512,192]{0,1:T(8,128)(2,1)}, bf16[512,192]{0,1:T(8,128)(2,1)S(1)}, u32[]{:S(2)}) copy-start(bf16[512,192]{0,1:T(8,128)(2,1)S(1)} %get-tuple-element.60) | copy-start | bytes 589828
  14.3 64.5 %copy-start.17 = (s32[512,1024]{1,0:T(8,128)}, s32[512,1024]{1,0:T(8,128)S(1)}, u32[]{:S(2)}) copy-start(s32[512,1024]{1,0:T(8,128)S(1)} %fusion.85) | copy-start | bytes 6291460
  14.9 5.8 copy-start.67
  20.7 11.7 %copy-start.21 = (s32[512,1024]{1,0:T(8,128)}, s32[512,1024]{1,0:T(8,128)S(1)}, u32[]{:S(2)}) copy-start(s32[512,1024]{1,0:T(8,128)S(1)} %get-tuple-element.65) | copy-start | bytes 6291460
  62.2 16.7 %copy-start.69 = (bf16[3,32]{1,0:T(4,128)(2,1)S(1)}, bf16[3,32]{1,0:T(4,128)(2,1)}, u32[]{:S(2)}) copy-start(bf16[3,32]{1,0:T(4,128)(2,1)} %param.28) | copy-start | bytes 580
  127.6 21.4 %copy-start.34 = (bf16[3,64,512]{2,1,0:T(8,128)(2,1)}, bf16[3,64,512]{2,1,0:T(8,128)(2,1)S(1)}, u32[]{:S(2)}) copy-start(bf16[3,64,512]{2,1,0:T(8,128)(2,1)S(1)} %fusion.120) | copy-start | bytes 589828
  152.1 205.4 %all-reduce.12.cloned.1.call-start = ((), (), s32[]{:S(2)}) async-start(), calls=%async_computation.14 | async-start | bytes 12582912 | tf_op jit(solution)/shard_map/psum | solution.py:200
  152.6 75.0 %copy-start.50 = (f32[768]{0:T(1024)}, f32[768]{0:T(1024)S(1)}, u32[]{:S(2)}) copy-start(f32[768]{0:T(1024)S(1)} %convert_element_type.536) | copy-start | bytes 9220
  237.5 120.0 %copy-start.51 = (f32[768]{0:T(1024)S(1)}, f32[768]{0:T(1024)}, u32[]{:S(2)}) copy-start(f32[768]{0:T(1024)} %copy-done.50) | copy-start | bytes 9220
  237.5 120.0 %copy-start.54 = (f32[1024]{0:T(1024)S(1)}, f32[1024]{0:T(1024)}, u32[]{:S(2)}) copy-start(f32[1024]{0:T(1024)} %copy-done.53) | copy-start | bytes 12292
  237.5 264.1 %all-reduce.10.cloned.1.call-start = ((), (), s32[]{:S(2)}) async-start(), calls=%async_computation.7 | async-start | bytes 3145728 | tf_op jit(solution)/shard_map/psum | solution.py:306
  379.4 6.1 copy-start.38
  388.0 168.4 %reduce-scatter.19.cloned.1.call-start = ((), (), s32[]{:S(2)}) async-start(), calls=%async_computation.13 | async-start | bytes 884736
  391.4 171.1 %reduce-scatter.13.cloned.1.call-start = ((), (), s32[]{:S(2)}) async-start(), calls=%async_computation.10 | async-start | bytes 884736 | tf_op jit(solution)/shard_map/reduce_scatter | solution.py:322
  393.4 234.2 %reduce-scatter.9.cloned.1.call-start = ((), (), s32[]{:S(2)}) async-start(), calls=%async_computation.8 | async-start | bytes 884736 | tf_op jit(solution)/shard_map/reduce_scatter | solution.py:320
  395.0 298.5 %reduce-scatter.11.cloned.1.call-start = ((), (), s32[]{:S(2)}) async-start(), calls=%async_computation.9 | async-start | bytes 884736 | tf_op jit(solution)/shard_map/reduce_scatter | solution.py:321
  396.6 369.0 %reduce-scatter.15.cloned.1.call-start = ((), (), s32[]{:S(2)}) async-start(), calls=%async_computation.11 | async-start | bytes 2654208 | tf_op jit(solution)/shard_map/reduce_scatter | solution.py:325
  402.0 435.7 %reduce-scatter.17.cloned.1.call-start = ((), (), s32[]{:S(2)}) async-start(), calls=%async_computation.12 | async-start | bytes 2654208 | tf_op jit(solution)/shard_map/reduce_scatter | solution.py:326
  409.0 16.0 %copy-start.9 = (bf16[3,512,1024]{2,1,0:T(8,128)(2,1)S(1)}, bf16[3,512,1024]{2,1,0:T(8,128)(2,1)}, u32[]{:S(2)}) copy-start(bf16[3,512,1024]{2,1,0:T(8,128)(2,1)} %copy-done.8) | copy-start | bytes 9437188
  409.0 16.0 %copy-start.23 = (s32[512,1024]{1,0:T(8,128)S(1)}, s32[512,1024]{1,0:T(8,128)}, u32[]{:S(2)}) copy-start(s32[512,1024]{1,0:T(8,128)} %get-tuple-element.61) | copy-start | bytes 6291460
  425.0 14.5 %copy-start.18 = (s32[512,1024]{1,0:T(8,128)S(1)}, s32[512,1024]{1,0:T(8,128)}, u32[]{:S(2)}) copy-start(s32[512,1024]{1,0:T(8,128)} %copy-done.17) | copy-start | bytes 6291460
  439.6 14.7 %copy-start.14 = (bf16[1024,768]{0,1:T(8,128)(2,1)S(1)}, bf16[1024,768]{0,1:T(8,128)(2,1)}, u32[]{:S(2)}) copy-start(bf16[1024,768]{0,1:T(8,128)(2,1)} %get-tuple-element.56) | copy-start | bytes 4718596
  455.8 16.2 %copy-start.7 = (bf16[3,512,1024]{2,1,0:T(8,128)(2,1)S(1)}, bf16[3,512,1024]{2,1,0:T(8,128)(2,1)}, u32[]{:S(2)}) copy-start(bf16[3,512,1024]{2,1,0:T(8,128)(2,1)} %copy-done.6) | copy-start | bytes 9437188
  455.8 16.2 %copy-start.20 = (s32[512,1024]{1,0:T(8,128)S(1)}, s32[512,1024]{1,0:T(8,128)}, u32[]{:S(2)}) copy-start(s32[512,1024]{1,0:T(8,128)} %get-tuple-element.62) | copy-start | bytes 6291460
  472.1 14.8 %copy-start.19 = (s32[512,1024]{1,0:T(8,128)S(1)}, s32[512,1024]{1,0:T(8,128)}, u32[]{:S(2)}) copy-start(s32[512,1024]{1,0:T(8,128)} %fusion.88) | copy-start | bytes 6291460
  486.8 14.8 %copy-start.47 = (f32[1024]{0:T(1024)S(1)}, f32[1024]{0:T(1024)}, u32[]{:S(2)}) copy-start(f32[1024]{0:T(1024)} %copy-done.46) | copy-start | bytes 12292
  486.8 14.8 %copy-start.49 = (f32[768]{0:T(1024)S(1)}, f32[768]{0:T(1024)}, u32[]{:S(2)}) copy-start(f32[768]{0:T(1024)} %copy-done.48) | copy-start | bytes 9220
  501.6 41.9 %copy-start.13 = (bf16[1024,768]{0,1:T(8,128)(2,1)S(1)}, bf16[1024,768]{0,1:T(8,128)(2,1)}, u32[]{:S(2)}) copy-start(bf16[1024,768]{0,1:T(8,128)(2,1)} %all-reduce.10.cloned.1.call-done) | copy-start | bytes 4718596
  548.7 289.0 %copy-start.1 = (bf16[768,768]{1,0:T(8,128)(2,1)S(1)}, bf16[768,768]{1,0:T(8,128)(2,1)}, u32[]{:S(2)}) copy-start(bf16[768,768]{1,0:T(8,128)(2,1)} %param.33) | copy-start | bytes 3538948
  (55 other events, 147.4 us)
Sparse Core Ops, SparseCore 0:
  152.2 71.1 all-reduce.7
  237.6 119.8 all-reduce.11
  388.1 43.0 all-reduce.9
  434.3 62.5 reduce-scatter.18
  500.9 61.5 reduce-scatter.12
  566.2 61.4 reduce-scatter.8
  631.9 61.5 reduce-scatter.10
  697.6 67.9 reduce-scatter.14
  769.6 67.9 reduce-scatter.16
where the time goes:
time: 853 us; the launch traced here: 845 us
  waiting for transfers between devices  463 us (54%)
  matrix products  261 us (31%)
  other arithmetic  46.8 us (5%)
  blocking collectives  37.1 us (4%)
  local copies, waits for them, and re-layouts  18.3 us (2%)
  between operations  16.7 us (2%)
    psum x1, waiting for transfers between devices, local(): result = mixed + lax.psum(ffn_terms, 'mp')  117 us
    dot_general x6, matrix products, attend_back(): jnp.einsum('pkm,fkm->pf', grad_scores, one_hot_ids(ids[which], tables[whi...  90.9 us
    dot_general x6, matrix products, block_scores(): jnp.einsum('ngo,sn->sgo', one_hot_ids(table_ids, table.shape[1]), table,...  73.3 us
    reduce_scatter x1, waiting for transfers between devices, local(): lax.psum_scatter(grad_w_down, 'dp', scatter_dimension=1, tiled=True)  72.1 us
    reduce_scatter x1, waiting for transfers between devices, local(): lax.psum_scatter(grad_w_up, 'dp', scatter_dimension=0, tiled=True)  72.1 us
    psum x1, waiting for transfers between devices, local(): mixed = hidden_x + lax.psum(attn_terms, 'mp')  66 us
    reduce_scatter x1, waiting for transfers between devices, local(): lax.psum_scatter(grad_w_key, 'dp', scatter_dimension=0, tiled=True)  65.8 us
    reduce_scatter x1, waiting for transfers between devices, local(): lax.psum_scatter(grad_w_query, 'dp', scatter_dimension=0, tiled=True)  65.2 us
  transfers between devices with their start and end apart: 9, of which 7 were waited for; matrix products, arithmetic and copies ran while one was open for 16% of the time, Pallas kernels for 0%

commit v1 on v0

v1 whole, which is shorter than its diff:
```python
import functools

import jax
import jax.numpy as jnp
import numpy as np
from jax import lax
from jax.experimental import pallas as pl
from jax.experimental.pallas import tpu as pltpu
from jax.sharding import PartitionSpec as P

EPS = 1e-06
THRESHOLDS = (12, 16, 23, 32, 46, 64, 91)
FAR = 91
HEADS = 3
HD = 64
PAD = 128
MARKS = 72
NEAR = 40
TILES = NEAR + 2
SPAN = 384
LOW = 92
TOP = 311
BF = jnp.bfloat16
F32 = jnp.float32
I32 = jnp.int32
FEED_PARTS = 3
GELU_C = float(np.sqrt(2.0 / np.pi))


def dot(left, right, dims=((1,), (0,))):
    return lax.dot_general(left, right, (dims, ((), ())), preferred_element_type=F32)


def bucket(delta):
    magnitude = jnp.abs(delta)
    coarse = 8 + sum((magnitude >= limit).astype(I32) for limit in THRESHOLDS)
    return jnp.where(magnitude < 8, magnitude, coarse) + 16 * (delta > 0).astype(I32)


def params(mib):
    return pltpu.CompilerParams(vmem_limit_bytes=mib * 2**20)


def cost(flops, nbytes):
    return pl.CostEstimate(flops=int(flops), bytes_accessed=int(nbytes), transcendentals=0)


def shape(dims, dtype):
    return jax.ShapeDtypeStruct(dims, dtype)


def whole(dims):
    return pl.BlockSpec(dims, lambda *a: (0,) * len(dims))


def hidden_rows(inputs, pages, feats):
    return inputs.astype(F32) + dot(pages.astype(F32).astype(BF), feats, ((0,), (0,)))


def unit_rows(field):
    factor = lax.rsqrt(jnp.mean(field * field, axis=-1, keepdims=True) + EPS)
    return field * factor, factor


def project_kernel(ids, x_ref, page_ref, feat_ref, gain_ref, wq_ref, wk_ref, wv_ref, n_ref, q_ref, k_ref, v_ref):
    step = pl.program_id(0)
    rows = x_ref.shape[0]
    unit, _ = unit_rows(hidden_rows(x_ref[...], page_ref[...], feat_ref[...]))
    normed = (unit * gain_ref[...].astype(F32)).astype(BF)
    n_ref[...] = normed
    lane = lax.broadcasted_iota(I32, (rows, PAD), 1)
    row = lax.broadcasted_iota(I32, (rows, PAD), 0) + step * rows
    masked = jnp.where((lane == HD) & (row >= ids[8]), -1e30, 0.0)
    block = lane - MARKS
    far_left = (block >= 0) & (block < 8) & (row < 128 * block - 96)
    far_right = (block >= 8) & (block < 16) & (row >= 128 * (block - 8) + 224)
    masked = jnp.where(far_left | far_right, 1.0, masked)
    query_extra = jnp.where(lane == HD, 1.0, 0.0)
    value_extra = jnp.where((lane == HD) | (lane == HD + 1), 1.0, 0.0)
    for out_ref, w_ref, extra, scale in (
        (q_ref, wq_ref, query_extra, 0.125),
        (k_ref, wk_ref, masked, None),
        (v_ref, wv_ref, value_extra, None),
    ):
        full = dot(normed, w_ref[...], ((1,), (1,)))
        if scale is not None:
            full = full * scale
        pair = full[:, :PAD]
        last = jnp.concatenate([full[:, PAD:], jnp.zeros((rows, PAD - HD), F32)], axis=1)
        heads = (pair, pltpu.roll(pair, HD, 1), last)
        for head in range(HEADS):
            out_ref[:, head * PAD : (head + 1) * PAD] = jnp.where(lane < HD, heads[head], extra).astype(BF)


def project(ids, inputs, onehot, feats, gain, w_query, w_key, w_value):
    seq, width = inputs.shape
    rows = 256
    columns = w_query.shape[0]
    wide = HEADS * PAD
    block = lambda cols: pl.BlockSpec((rows, cols), lambda i, s: (i, 0))
    lanes = lambda n: pl.BlockSpec((n, rows), lambda i, s: (0, i))
    return pl.pallas_call(
        project_kernel,
        grid_spec=pltpu.PrefetchScalarGridSpec(
            num_scalar_prefetch=1,
            grid=(seq // rows,),
            in_specs=[block(width), lanes(onehot.shape[0]), whole(feats.shape), whole(gain.shape)]
            + [whole((columns, width))] * 3,
            out_specs=[block(width), block(wide), block(wide), block(wide)],
        ),
        out_shape=[shape((seq, width), BF)] + [shape((seq, wide), BF)] * 3,
        compiler_params=params(24),
        cost_estimate=cost(2 * seq * width * 3 * columns, 4 * seq * width),
        name="project",
    )(ids, inputs, onehot, feats, gain, w_query, w_key, w_value)


def place(delta):
    magnitude = jnp.abs(delta)
    coarse = jnp.minimum(25 - lax.clz(delta * delta), 7)
    exact = magnitude < 8
    return jnp.where(exact, magnitude, coarse), exact, delta > 0


def look(table_ref, row, where):
    index, exact, after = where
    found = [jnp.take_along_axis(table_ref[row, part], index, axis=0) for part in range(4)]
    return jnp.where(after, jnp.where(exact, found[2], found[3]), jnp.where(exact, found[0], found[1]))


def tile_delta(tile):
    lane = lax.broadcasted_iota(I32, (8, 128), 1)
    sub = lax.broadcasted_iota(I32, (8, 128), 0)
    delta = 8 * (tile - 13) + sub - lane
    if tile == 0:
        delta = jnp.full_like(delta, -1000)
    if tile == TILES - 1:
        delta = jnp.full_like(delta, 1000)
    return delta


def attend_kernel(
    ids, q_ref, k_ref, v_ref, hor_ref, ver_ref, hor_all, ver_all, table_ref,
    e_ref, own_ref, other_ref, inv_ref, out_ref, s_ref, rel_ref, t8_ref, hor_col, ver_col, *, width, chunk,
):
    seq = k_ref.shape[0]
    lanes = width // 128
    step = pl.program_id(0)
    steps = seq // width

    @pl.when(step == 0)
    def _():
        for all_ref, col_ref in ((hor_all, hor_col), (ver_all, ver_col)):
            for b in range(seq // 128):
                cols = slice(128 * b, 128 * b + 128)
                spread = jnp.broadcast_to(all_ref[:, cols].astype(F32), (128, 128))
                col_ref[cols, :] = spread.T.astype(I32)
        for axis in range(3):
            for head in range(HEADS):
                at = axis * HEADS + head
                for part in range(4):
                    t8_ref[at, part] = jnp.broadcast_to(table_ref[8 * part : 8 * part + 8, at : at + 1], (8, 128))
        for tile in range(TILES):
            where = place(tile_delta(tile))
            for head in range(HEADS):
                rel_ref[head, tile] = look(t8_ref, head, where)

    queries = q_ref[...]
    for head in range(HEADS):
        cols = slice(head * PAD, (head + 1) * PAD)
        s_ref[head] = dot(k_ref[:, cols], queries[:, cols], ((1,), (1,)))
    hor = [jnp.broadcast_to(hor_ref[:, 128 * l : 128 * l + 128], (8, 128)) for l in range(lanes)]
    ver = [jnp.broadcast_to(ver_ref[:, 128 * l : 128 * l + 128], (8, 128)) for l in range(lanes)]
    first = ids[9 + step] * lanes

    def add_bias(c, tops):
        tops = list(tops)
        base = pl.multiple_of(c * chunk, chunk)
        for g in range(chunk // 8):
            rows = pl.ds(pl.multiple_of(base + 8 * g, 8), 8)
            hor_keys, ver_keys = hor_col[rows, :], ver_col[rows, :]
            for l in range(lanes):
                cols = pl.ds(128 * l, 128)
                hor_at, ver_at = place(hor_keys - hor[l]), place(ver_keys - ver[l])
                tile = jnp.clip(c * (chunk // 8) + g - 16 * (first + l) + 13, 0, TILES - 1)
                for head in range(HEADS):
                    s = s_ref[head, rows, cols] + rel_ref[head, tile]
                    s = s + (look(t8_ref, HEADS + head, hor_at) + look(t8_ref, 2 * HEADS + head, ver_at))
                    s_ref[head, rows, cols] = s
                    tops[head * lanes + l] = jnp.maximum(tops[head * lanes + l], s)
        return tuple(tops)

    tops = lax.fori_loop(
        0, seq // chunk, add_bias, tuple(jnp.full((8, 128), -1e30, F32) for _ in range(HEADS * lanes))
    )
    peaks = [jnp.broadcast_to(jnp.max(top, axis=0, keepdims=True), (16, 128)) for top in tops]

    def exps(c, carry):
        for g in range(4):
            rows = pl.ds(pl.multiple_of(c * 64 + 16 * g, 16), 16)
            for l in range(lanes):
                cols = pl.ds(128 * l, 128)
                for head in range(HEADS):
                    e_ref[head, rows, cols] = jnp.exp(s_ref[head, rows, cols] - peaks[head * lanes + l]).astype(BF)
        return carry

    lax.fori_loop(0, seq // 64, exps, 0)
    for head in range(HEADS):
        total = dot(v_ref[:, head * PAD : (head + 1) * PAD], e_ref[head], ((0,), (0,)))
        inverse = 1.0 / total[HD : HD + 1, :]
        inv_ref[head : head + 1, :] = inverse
        out_ref[head * HD : (head + 1) * HD, :] = total[:HD] * inverse

    @pl.when(step < steps // 2)
    def _():
        other_ref[...] = out_ref[...].astype(BF)

    @pl.when(step >= steps // 2)
    def _():
        own_ref[...] = out_ref[...].astype(BF)


def attend(ids, queries, keys, values, hor, ver, tables):
    seq, wide = queries.shape
    width = 256
    steps = seq // width
    half = steps // 2
    columns = HEADS * HD
    at = lambda i, s: (0, s[9 + i])
    return pl.pallas_call(
        functools.partial(attend_kernel, width=width, chunk=32),
        grid_spec=pltpu.PrefetchScalarGridSpec(
            num_scalar_prefetch=1,
            grid=(steps,),
            in_specs=[
                pl.BlockSpec((width, wide), lambda i, s: (s[9 + i], 0)),
                whole(keys.shape),
                whole(values.shape),
                pl.BlockSpec((1, width), at),
                pl.BlockSpec((1, width), at),
                whole(hor.shape),
                whole(ver.shape),
                whole(tables.shape),
            ],
            out_specs=[
                pl.BlockSpec((HEADS, seq, width), lambda i, s: (0, 0, s[9 + i])),
                pl.BlockSpec((columns, width), lambda i, s: (0, jnp.maximum(i - half, 0))),
                pl.BlockSpec((columns, width), lambda i, s: (0, jnp.minimum(i, half - 1))),
                pl.BlockSpec((HEADS, width), at),
                pl.BlockSpec((columns, width), at),
            ],
            scratch_shapes=[
                pltpu.VMEM((HEADS, seq, width), F32),
                pltpu.VMEM((HEADS, TILES, 8, 128), F32),
                pltpu.VMEM((3 * HEADS, 4, 8, 128), F32),
                pltpu.VMEM((seq, 128), I32),
                pltpu.VMEM((seq, 128), I32),
            ],
        ),
        out_shape=[
            shape((HEADS, seq, seq), BF),
            shape((columns, seq // 2), BF),
            shape((columns, seq // 2), BF),
            shape((HEADS, seq), F32),
            shape((columns, seq), F32),
        ],
        compiler_params=params(32),
        cost_estimate=cost(25e9, 10e6),
        name="attend",
    )(ids, queries, keys, values, hor, ver, hor, ver, tables)


def feed_kernel(
    ids, x_ref, page_ref, feat_ref, gain_ref, cot_ref, a0, a1, a2, a3, o0, o1, o2, o3, u0, u1, d0, d1,
    act0, act1, up0, up1, n_ref, mixed_ref, grad_ref, ffn_ref, grad_sum, ffn_sum,
):
    step = pl.program_id(0)
    half = pl.num_programs(0) // 2

    @pl.when(step == 0)
    def _():
        mixed = hidden_rows(x_ref[...], page_ref[...], feat_ref[...])
        for a_ref, o_ref in ((a0, o0), (a1, o1), (a2, o2), (a3, o3)):
            mixed = mixed + dot(a_ref[...], o_ref[...], ((0,), (0,)))
        mixed_ref[...] = mixed
        unit, _ = unit_rows(mixed)
        n_ref[...] = (unit * gain_ref[...].astype(F32)).astype(BF)
        grad_sum[...] = jnp.zeros_like(grad_sum)
        ffn_sum[...] = jnp.zeros_like(ffn_sum)

    def part(u_ref, d_ref, act_ref, up_ref):
        upward = dot(n_ref[...], u_ref[...])
        square = upward * upward
        tanh = jnp.tanh(GELU_C * upward * (1.0 + 0.044715 * square))
        lifted = 0.5 * (1.0 + tanh)
        activated = (upward * lifted).astype(BF)
        slope = lifted + 0.5 * upward * (1.0 - tanh * tanh) * (GELU_C * (1.0 + 3 * 0.044715 * square))
        grad_up = (dot(cot_ref[...], d_ref[...], ((1,), (1,))) * slope).astype(BF)
        act_ref[...] = activated
        up_ref[...] = grad_up
        ffn_sum[...] += dot(activated, d_ref[...])
        grad_sum[...] += dot(grad_up, u_ref[...], ((1,), (1,)))

    @pl.when(step < half)
    def _():
        part(u0, d0, act0, up0)

    @pl.when(step >= half)
    def _():
        part(u1, d1, act1, up1)

    @pl.when(step == 2 * half - 1)
    def _():
        grad_ref[...] = grad_sum[...].astype(grad_ref.dtype)
        ffn_ref[...] = ffn_sum[...].astype(ffn_ref.dtype)


def feed(ids, own, inputs, onehot, feats, gain, cotangent, attended, w_outputs, ups, downs):
    seq, width = inputs.shape
    rows = seq // 4
    units = ups[0].shape[1]
    half = FEED_PARTS
    chunk = units // half
    slot = 16 if own else 17
    quarter = lambda cols: pl.BlockSpec((rows, cols), lambda i, s: (s[slot], 0))
    pages = pl.BlockSpec((onehot.shape[0], rows), lambda i, s: (0, s[slot]))
    columns = HEADS * HD
    att = pl.BlockSpec((columns, rows), lambda i, s: (0, s[slot + 2]))
    low = lambda i: jnp.minimum(i, half - 1)
    high = lambda i: jnp.maximum(i - half, 0)
    kept = F32 if own else BF
    flops = 2 * rows * width * (width + 2 * units * 4)
    return pl.pallas_call(
        feed_kernel,
        grid_spec=pltpu.PrefetchScalarGridSpec(
            num_scalar_prefetch=1,
            grid=(2 * half,),
            in_specs=[quarter(width), pages, whole(feats.shape), whole(gain.shape), quarter(width)]
            + [att] * 4
            + [whole((columns, width))] * 4
            + [
                pl.BlockSpec((width, chunk), lambda i, s: (0, low(i))),
                pl.BlockSpec((width, chunk), lambda i, s: (0, high(i))),
                pl.BlockSpec((chunk, width), lambda i, s: (low(i), 0)),
                pl.BlockSpec((chunk, width), lambda i, s: (high(i), 0)),
            ],
            out_specs=[
                pl.BlockSpec((rows, chunk), lambda i, s: (0, low(i))),
                pl.BlockSpec((rows, chunk), lambda i, s: (0, high(i))),
                pl.BlockSpec((rows, chunk), lambda i, s: (0, low(i))),
                pl.BlockSpec((rows, chunk), lambda i, s: (0, high(i))),
                whole((rows, width)),
                whole((rows, width)),
                whole((rows, width)),
                whole((rows, width)),
            ],
            scratch_shapes=[pltpu.VMEM((rows, width), F32), pltpu.VMEM((rows, width), F32)],
        ),
        out_shape=[shape((rows, units), BF)] * 4
        + [shape((rows, width), BF), shape((rows, width), F32), shape((rows, width), kept), shape((rows, width), kept)],
        compiler_params=params(40),
        cost_estimate=cost(flops, 8e6),
        name="feed_own" if own else "feed_other",
    )(ids, inputs, onehot, feats, gain, cotangent, *attended, *w_outputs, *ups, *downs)


def mid_kernel(ids, mine_ref, sent_ref, mixed_ref, gain_ref, cot_ref, o0, o1, o2, o3, grad_ref, low_ref, g0, g1, g2, g3, part_ref):
    grad_normed = mine_ref[...] + sent_ref[...].astype(F32)
    unit, factor = unit_rows(mixed_ref[...])
    scaled = grad_normed * gain_ref[...].astype(F32)
    grad = factor * (scaled - unit * jnp.mean(scaled * unit, axis=-1, keepdims=True))
    grad = cot_ref[...].astype(F32) + grad
    grad_ref[...] = grad
    low = grad.astype(BF)
    low_ref[...] = low
    part_ref[...] = jnp.sum(grad_normed * unit, axis=0, keepdims=True)
    for o_ref, g_ref in ((o0, g0), (o1, g1), (o2, g2), (o3, g3)):
        g_ref[...] = dot(o_ref[...], low, ((1,), (1,))).astype(BF)


def mid(ids, mine, sent, mixed, gain, cotangent, w_outputs):
    rows, width = mine.shape
    columns = HEADS * HD
    full = whole((rows, width))
    return pl.pallas_call(
        mid_kernel,
        grid_spec=pltpu.PrefetchScalarGridSpec(
            num_scalar_prefetch=1,
            grid=(1,),
            in_specs=[full, full, full, whole(gain.shape), pl.BlockSpec((rows, width), lambda i, s: (s[16], 0))]
            + [whole((columns, width))] * 4,
            out_specs=[full, full] + [whole((columns, rows))] * 4 + [whole((1, width))],
        ),
        out_shape=[shape((rows, width), F32), shape((rows, width), BF)]
        + [shape((columns, rows), BF)] * 4
        + [shape((1, width), F32)],
        compiler_params=params(24),
        cost_estimate=cost(2 * rows * width * width, 4e6),
        name="mid",
    )(ids, mine, sent, mixed, gain, cotangent, *w_outputs)


def back_kernel(*refs, first):
    ids, ea_ref, eb_ref, qa_ref, qb_ref, inv_a, inv_b, out_a, out_b, k_ref, v_ref, ga_ref, gb_ref = refs[:13]
    refs = refs[13:]
    if first:
        ds_ref, dqa_ref, dqb_ref, key_ref, value_ref, near_ref, far_ref, x_ref = refs
    else:
        key_in, value_in, near_in, far_in = refs[:4]
        ds_ref, dqa_ref, dqb_ref, keep_ref, send_ref, near_ref, far_ref, x_ref = refs[4:]
    head = pl.program_id(0)
    seq = k_ref.shape[0]
    width = qa_ref.shape[0]
    both = 2 * width
    lanes = width // 128
    base = 0 if first else 2

    sub = lax.broadcasted_iota(I32, (HD, both), 0)
    head_sub = lax.broadcasted_iota(I32, (8, both), 0)
    inverse = jnp.concatenate([inv_a[...], inv_b[...]], axis=1)
    inverse = jnp.sum(jnp.where(head_sub[: inverse.shape[0]] == head, inverse, 0.0), axis=0, keepdims=True)
    grad = jnp.concatenate([ga_ref[...], gb_ref[...]], axis=1).astype(F32)
    grad = (grad * inverse).astype(BF).astype(F32)
    inner = jnp.sum(grad * jnp.concatenate([out_a[...], out_b[...]], axis=1), axis=0, keepdims=True)
    high = inner.astype(BF).astype(F32)
    extra = jnp.where(sub == 0, -high, jnp.where(sub == 1, high - inner, 0.0))
    right = jnp.concatenate([grad, extra], axis=0).astype(BF)
    x_ref[...] = dot(v_ref[...], right)
    value = dot(ea_ref[0], right[:, :width], ((1,), (1,))) + dot(eb_ref[0], right[:, width:], ((1,), (1,)))

    def grad_scores(c, carry):
        rows = pl.ds(pl.multiple_of(c * 64, 64), 64)
        for part, e_ref in enumerate((ea_ref, eb_ref)):
            cols = slice(part * width, part * width + width)
            ds_ref[0, rows, cols] = (e_ref[0, rows, :].astype(F32) * x_ref[rows, cols]).astype(BF)
        return carry

    lax.fori_loop(0, seq // 64, grad_scores, 0)
    grad = ds_ref[0]
    key = dot(grad, jnp.concatenate([qa_ref[...], qb_ref[...]], axis=0))
    query = dot(k_ref[...], grad, ((0,), (0,)))
    dqa_ref[...] = (query[:HD, :width] * 0.125).astype(BF)
    dqb_ref[...] = (query[:HD, width:] * 0.125).astype(BF)

    blocks = [ids[base + l // lanes] * lanes + l % lanes for l in range(2 * lanes)]
    for g in range(NEAR // 2):
        total = None if first else near_in[0, 16 * g : 16 * g + 16]
        for l, block in enumerate(blocks):
            start = 128 * block - 96 + 16 * g
            inside = (start >= 0) & (start < seq)
            rows = pl.ds(pl.multiple_of(jnp.clip(start, 0, seq - 16), 16), 16)
            found = ds_ref[0, rows, 128 * l : 128 * l + 128].astype(F32)
            found = jnp.where(inside, found, 0.0)
            total = found if total is None else total + found
        near_ref[0, 16 * g : 16 * g + 16] = total
    spot = lax.broadcasted_iota(I32, (8, 128), 0)
    for side in range(2):
        total = None if first else far_in[0, 8 * side : 8 * side + 8]
        for l, block in enumerate(blocks):
            marks = query[MARKS + 8 * side : MARKS + 8 * side + 8, 128 * l : 128 * l + 128]
            marks = jnp.where(spot == block, marks, 0.0)
            total = marks if total is None else total + marks
        far_ref[0, 8 * side : 8 * side + 8] = total

    if first:
        key_ref[...] = key
        value_ref[...] = value
    else:
        for part, acc in ((0, key_in[...] + key), (1, value_in[...] + value)):
            turned = acc.T[:HD].astype(BF)
            for k in range(4):
                goal = keep_ref if k % 2 == 0 else send_ref
                for q in range(4):

                    @pl.when(ids[k] == q)
                    def _(goal=goal, k=k, q=q, part=part, turned=turned):
                        goal[k // 2, part] = turned[:, q * width : (q + 1) * width]


def back(ids, e, queries, inverse, out, keys, values, grad_a, grad_b, carried):
    seq, wide = queries.shape
    width = seq // 4
    first = carried is None
    base = 0 if first else 2
    columns = HEADS * HD
    head_cols = pl.BlockSpec((seq, PAD), lambda h, s: (0, h))
    grad_rows = pl.BlockSpec((HD, width), lambda h, s: (h, 0))
    near = pl.BlockSpec((1, 8 * NEAR, 128), lambda h, s: (h, 0, 0))
    far = pl.BlockSpec((1, 16, 128), lambda h, s: (h, 0, 0))
    pieces = pl.BlockSpec((2, 2, HD, width), lambda h, s: (0, 0, h, 0))
    sums = [(shape((seq, wide), F32), head_cols)] * 2
    rel = [(shape((HEADS, 8 * NEAR, 128), F32), near), (shape((HEADS, 16, 128), F32), far)]
    outs = [(shape((HEADS, seq, 2 * width), BF), pl.BlockSpec((1, seq, 2 * width), lambda h, s: (h, 0, 0)))]
    outs += [(shape((columns, width), BF), grad_rows)] * 2
    outs += sums if first else [(shape((2, 2, columns, width), BF), pieces)] * 2
    outs += rel
    specs = []
    for make in (
        lambda q: pl.BlockSpec((1, seq, width), lambda h, s: (h, 0, s[q])),
        lambda q: pl.BlockSpec((width, PAD), lambda h, s: (s[q], h)),
        lambda q: pl.BlockSpec((HEADS, width), lambda h, s: (0, s[q])),
        lambda q: pl.BlockSpec((HD, width), lambda h, s: (h, s[q])),
    ):
        specs += [make(base), make(base + 1)]
    specs += [head_cols, head_cols, grad_rows, grad_rows]
    if not first:
        specs += [spec for _, spec in sums + rel]
    return pl.pallas_call(
        functools.partial(back_kernel, first=first),
        grid_spec=pltpu.PrefetchScalarGridSpec(
            num_scalar_prefetch=1,
            grid=(HEADS,),
            in_specs=specs,
            out_specs=[spec for _, spec in outs],
            scratch_shapes=[pltpu.VMEM((seq, 2 * width), F32)],
        ),
        out_shape=[o for o, _ in outs],
        compiler_params=params(40),
        cost_estimate=cost(6e9, 10e6),
        name="back_first" if first else "back_last",
    )(ids, e, e, queries, queries, inverse, inverse, out, out, keys, values, grad_a, grad_b, *(() if first else carried))


def tables_kernel(ids, s_ref, t_ref, keys_ref, q0, q1, q2, q3, near_ref, far_ref, out_ref, e_ref, y_ref):
    axis, block = pl.program_id(0), pl.program_id(1)
    places, seq = e_ref.shape
    width = s_ref.shape[2]
    groups = places // 128

    @pl.when(block == 0)
    def _():
        spot = lax.broadcasted_iota(I32, (places, seq), 0)
        e_ref[...] = jnp.where(spot == keys_ref[0], 1.0, 0.0).astype(BF)

    def windows(scores_ref, query):
        column = lax.broadcasted_iota(I32, (SPAN, width), 0)
        right = [
            jnp.where(column == jnp.clip(128 * b + TOP - LOW - query, 0, TOP), 1.0, 0.0).astype(BF) for b in range(groups)
        ]
        left = []
        for head in range(HEADS):
            moved = dot(e_ref[...], scores_ref[head]).astype(BF)
            left.append(jnp.concatenate([moved[128 * b : 128 * b + 128] for b in range(groups)], axis=1))
        return dot(jnp.concatenate(left, axis=0), jnp.concatenate(right, axis=1), ((1,), (1,)))

    @pl.when(block == 0)
    def _():
        y_ref[...] = windows(s_ref, jnp.concatenate([q0[0], q1[0]], axis=1))

    @pl.when(block == 1)
    def _():
        y_ref[...] += windows(t_ref, jnp.concatenate([q2[0], q3[0]], axis=1))

    def to_buckets(row, sums, delta):
        found = bucket(delta)
        spot = lax.broadcasted_iota(I32, (32, sums.shape[1]), 0)
        out_ref[row] = jnp.sum(jnp.where(found == spot, sums, 0.0), axis=1, keepdims=True)

    @pl.when(block == 1)
    def _():
        lane = lax.broadcasted_iota(I32, (1, 512), 1)
        for head in range(HEADS):
            grid = jnp.concatenate([y_ref[head * 128 : head * 128 + 128, :], jnp.zeros((128, 512 - SPAN), F32)], axis=1)
            grid = pltpu.roll(grid, 0, 1, stride=1, stride_axis=0)
            sums = jnp.sum(grid, axis=0, keepdims=True)
            to_buckets(head + HEADS * (1 + axis), sums, lane + LOW - TOP)

        @pl.when(axis == 0)
        def _():
            flip = 7 - lax.broadcasted_iota(I32, (8, 128), 0)
            for head in range(HEADS):
                near = [
                    jnp.take_along_axis(near_ref[head, 8 * t : 8 * t + 8], flip, axis=0) for t in reversed(range(NEAR))
                ]
                grid = jnp.concatenate(near, axis=0)
                grid = jnp.concatenate([grid, jnp.zeros((8 * NEAR, 384), F32)], axis=1)
                grid = pltpu.roll(grid, 0, 1, stride=1, stride_axis=0)
                sums = jnp.sum(grid, axis=0, keepdims=True)
                to_buckets(head, sums, 8 * NEAR - 1 - 8 * 12 - lane)
                spot = lax.broadcasted_iota(I32, (32, 1), 0)
                left = jnp.sum(jnp.sum(far_ref[head, :8], axis=0, keepdims=True), axis=1, keepdims=True)
                right = jnp.sum(jnp.sum(far_ref[head, 8:], axis=0, keepdims=True), axis=1, keepdims=True)
                out_ref[head] += jnp.where(spot == 15, left, 0.0) + jnp.where(spot == 31, right, 0.0)


def table_grads(ids, scores_a, scores_b, positions, near, far):
    seq = positions.shape[2]
    width = seq // 4
    places = 1024
    quarter = lambda k: pl.BlockSpec((1, 1, width), lambda a, b, s: (a, 0, s[k]))
    return pl.pallas_call(
        tables_kernel,
        grid_spec=pltpu.PrefetchScalarGridSpec(
            num_scalar_prefetch=1,
            grid=(2, 2),
            in_specs=[
                whole(scores_a.shape),
                whole(scores_b.shape),
                pl.BlockSpec((1, 1, seq), lambda a, b, s: (a, 0, 0)),
                quarter(0),
                quarter(1),
                quarter(2),
                quarter(3),
                whole(near.shape),
                whole(far.shape),
            ],
            out_specs=whole((3 * HEADS, 32, 1)),
            scratch_shapes=[pltpu.VMEM((places, seq), BF), pltpu.VMEM((HEADS * 128, SPAN), F32)],
        ),
        out_shape=shape((3 * HEADS, 32, 1), F32),
        compiler_params=params(48),
        cost_estimate=cost(16e9, 8e6),
        name="table_grads",
    )(ids, scores_a, scores_b, positions, positions, positions, positions, positions, near, far)


def terms_kernel(w0, w1, w2, p0, p1, p2, mine_q, mine_kv, sent_q, sent_kv, out_ref):
    total = None
    for refs, q_ref, kv_ref in (((w0, w1, w2), mine_q, mine_kv), ((p0, p1, p2), sent_q, sent_kv)):
        for w_ref, grad in zip(refs, (q_ref[...], kv_ref[0, 0], kv_ref[0, 1])):
            found = dot(grad, w_ref[...], ((0,), (0,)))
            total = found if total is None else total + found
    out_ref[...] = total.astype(out_ref.dtype)


def terms(own, weights, partner, mine_q, mine_kv, sent_q, sent_kv):
    columns, width = weights[0].shape
    rows = mine_q.shape[1]
    slot = 0 if own else 1
    pieces = pl.BlockSpec((1, 2, columns, rows), lambda i: (slot, 0, 0, 0))
    return pl.pallas_call(
        terms_kernel,
        grid=(1,),
        in_specs=[whole(weights[0].shape)] * 6 + [whole((columns, rows)), pieces] * 2,
        out_specs=whole((rows, width)),
        out_shape=shape((rows, width), F32 if own else BF),
        compiler_params=params(16),
        cost_estimate=cost(2 * rows * width * columns * 6, 3e6),
        name="terms_own" if own else "terms_other",
    )(*weights, *partner, mine_q, mine_kv, sent_q, sent_kv)


def last_kernel(ids, mine_ref, sent_ref, x_ref, page_ref, feat_ref, gain_ref, grad_ref, out_ref, part_ref):
    grad_normed = mine_ref[...] + sent_ref[...].astype(F32)
    unit, factor = unit_rows(hidden_rows(x_ref[...], page_ref[...], feat_ref[...]))
    scaled = grad_normed * gain_ref[...].astype(F32)
    grad = factor * (scaled - unit * jnp.mean(scaled * unit, axis=-1, keepdims=True))
    out_ref[...] = (grad_ref[...] + grad).astype(BF)
    part_ref[...] = jnp.sum(grad_normed * unit, axis=0, keepdims=True)


def last(ids, mine, sent, inputs, onehot, feats, gain, grad_mixed):
    rows, width = mine.shape
    full = whole((rows, width))
    quarter = lambda cols: pl.BlockSpec((rows, cols), lambda i, s: (s[16], 0))
    pages = pl.BlockSpec((onehot.shape[0], rows), lambda i, s: (0, s[16]))
    return pl.pallas_call(
        last_kernel,
        grid_spec=pltpu.PrefetchScalarGridSpec(
            num_scalar_prefetch=1,
            grid=(1,),
            in_specs=[full, full, quarter(width), pages, whole(feats.shape), whole(gain.shape), full],
            out_specs=[full, whole((1, width))],
        ),
        out_shape=[shape((rows, width), BF), shape((1, width), F32)],
        compiler_params=params(16),
        cost_estimate=cost(1e8, 4e6),
        name="last",
    )(ids, mine, sent, inputs, onehot, feats, gain, grad_mixed)


def join_kernel(ids, b0, b1, b2, b3, out_ref):
    for k, b_ref in enumerate((b0, b1, b2, b3)):

        @pl.when(pl.program_id(0) == k)
        def _(b_ref=b_ref):
            out_ref[...] = b_ref[...].astype(out_ref.dtype)


def join_feat_kernel(ids, b0, b1, b2, b3, page_ref, out_ref, feat_ref, all_ref):
    step = pl.program_id(0)
    rows = b0.shape[0]
    for k, b_ref in enumerate((b0, b1, b2, b3)):

        @pl.when(step == k)
        def _(b_ref=b_ref, k=k):
            out_ref[...] = b_ref[...].astype(out_ref.dtype)
            all_ref[pl.ds(pl.multiple_of(ids[k] * rows, rows), rows), :] = b_ref[...]

    @pl.when(step == 3)
    def _():
        feat_ref[...] = dot(page_ref[...].astype(F32).astype(BF), all_ref[...])


def join(ids, blocks, dtype, onehot=None):
    rows, width = blocks[0].shape
    specs = [whole((rows, width))] * 4
    outs, out_specs = [shape((4 * rows, width), dtype)], [pl.BlockSpec((rows, width), lambda i, s: (s[i], 0))]
    extra, scratch = (), []
    if onehot is not None:
        pages = onehot.shape[0]
        specs = specs + [whole(onehot.shape)]
        outs.append(shape((pages, width), F32))
        out_specs.append(whole((pages, width)))
        extra, scratch = (onehot,), [pltpu.VMEM((4 * rows, width), BF)]
    found = pl.pallas_call(
        join_kernel if onehot is None else join_feat_kernel,
        grid_spec=pltpu.PrefetchScalarGridSpec(
            num_scalar_prefetch=1, grid=(4,), in_specs=specs, out_specs=out_specs, scratch_shapes=scratch
        ),
        out_shape=outs,
        compiler_params=params(16),
        cost_estimate=cost(1e6, 6e6),
        name="join_output" if onehot is None else "join_grads",
    )(ids, *blocks, *extra)
    return found[0] if onehot is None else found


def split_rows(ids, total, keep_ref, send_ref, parity):
    groups, size = keep_ref.shape[0], keep_ref.shape[1]
    for g in range(groups):
        mine = pl.multiple_of((2 * g + parity) * size, 8)
        theirs = pl.multiple_of((2 * g + 1 - parity) * size, 8)
        keep_ref[g] = total[pl.ds(mine, size), :].astype(keep_ref.dtype)
        send_ref[g] = total[pl.ds(theirs, size), :].astype(BF)


def feed_grad_kernel(ids, *refs, fast, blocks):
    lefts, rights = refs[:blocks], refs[blocks : 2 * blocks]
    outs = refs[2 * blocks :]
    left = jnp.concatenate([r[...] for r in lefts], axis=0)
    right = jnp.concatenate([r[...] for r in rights], axis=0)
    total = outs[-1]
    total[...] = dot(left, right, ((0,), (0,)))
    if fast:
        split_rows(ids, total, outs[0], outs[1], ids[13])
    else:
        outs[0][...] = total[...]


def feed_grad(ids, lefts, left_places, rights, fast, name):
    blocks = len(rights)
    rows, units = rights[0].shape
    width = lefts[0].shape[1]
    specs = []
    for left, spot in zip(lefts, left_places):
        if spot is None:
            specs.append(whole((rows, width)))
        else:
            specs.append(pl.BlockSpec((rows, width), functools.partial(lambda i, s, spot: (s[spot], 0), spot=spot)))
    specs += [whole((rows, units))] * blocks
    if fast:
        outs = [shape((4, width // 8, units), F32), shape((4, width // 8, units), BF)]
    else:
        outs = [shape((width, units), F32)]
    return pl.pallas_call(
        functools.partial(feed_grad_kernel, fast=fast, blocks=blocks),
        grid_spec=pltpu.PrefetchScalarGridSpec(
            num_scalar_prefetch=1,
            grid=(1,),
            in_specs=specs,
            out_specs=[whole(o.shape) for o in outs],
            scratch_shapes=[pltpu.VMEM((width, units), F32)],
        ),
        out_shape=outs,
        compiler_params=params(32),
        cost_estimate=cost(2 * blocks * rows * width * units, 8e6),
        name=name,
    )(ids, *lefts, *rights)


def head_grad_kernel(ids, n0, n1, n2, n3, q0, q1, q2, q3, keep_kv, send_kv, l0, l1, l2, l3, a0, a1, a2, a3, *outs, fast):
    total, turned = outs[-2:]
    n = q0.shape[0]
    normed = jnp.concatenate([r[...] for r in (n0, n1, n2, n3)], axis=0)
    low = jnp.concatenate([r[...] for r in (l0, l1, l2, l3)], axis=0)
    pieces = [[r[...] for r in (q0, q1, q2, q3)]]
    for part in range(2):
        pieces.append([keep_kv[0, part], send_kv[0, part], keep_kv[1, part], send_kv[1, part]])
    pieces.append([r[...] for r in (a0, a1, a2, a3)])
    for at, piece in enumerate(pieces):
        right = low if at == 3 else normed
        total[at * n : (at + 1) * n, :] = dot(jnp.concatenate(piece, axis=1), right)
    turned[...] = total[...].T
    if fast:
        split_rows(ids, turned, outs[0], outs[1], ids[13])
    else:
        outs[0][...] = turned[...]


def head_grad(ids, normed, grad_q, keep_kv, send_kv, lows, own, other, fast):
    seq, width = normed.shape
    rows = seq // 4
    n = grad_q[0].shape[0]
    quarter = lambda k: pl.BlockSpec((rows, width), lambda i, s: (s[k], 0))
    halves = lambda k: pl.BlockSpec((n, rows), lambda i, s: (0, s[20 + k]))
    specs = [quarter(k) for k in range(4)]
    specs += [whole((n, rows))] * 4 + [whole(keep_kv.shape)] * 2 + [whole((rows, width))] * 4
    specs += [halves(k) for k in range(4)]
    if fast:
        outs = [shape((4, width // 8, 4 * n), F32), shape((4, width // 8, 4 * n), BF)]
    else:
        outs = [shape((width, 4 * n), F32)]
    return pl.pallas_call(
        functools.partial(head_grad_kernel, fast=fast),
        grid_spec=pltpu.PrefetchScalarGridSpec(
            num_scalar_prefetch=1,
            grid=(1,),
            in_specs=specs,
            out_specs=[whole(o.shape) for o in outs],
            scratch_shapes=[pltpu.VMEM((4 * n, width), F32), pltpu.VMEM((width, 4 * n), F32)],
        ),
        out_shape=outs,
        compiler_params=params(32),
        cost_estimate=cost(2 * seq * width * 4 * n, 8e6),
        name="head_grad",
    )(ids, *[normed] * 4, *grad_q, keep_kv, send_kv, *lows, own, other, own, other)


def pair_kernel(ids, keep_ref, got_ref, o0, o1, o2, o3):
    for k, o_ref in enumerate((o0, o1, o2, o3)):
        at = ids[24 + k]
        o_ref[...] = (keep_ref[at] + got_ref[at].astype(F32)).astype(o_ref.dtype)


def pair_sum(ids, keep, got):
    _, size, n = keep.shape
    return pl.pallas_call(
        pair_kernel,
        grid_spec=pltpu.PrefetchScalarGridSpec(
            num_scalar_prefetch=1,
            grid=(1,),
            in_specs=[whole(keep.shape), whole(got.shape)],
            out_specs=[whole((size, n))] * 4,
        ),
        out_shape=[shape((size, n), F32)] + [shape((size, n), BF)] * 3,
        compiler_params=params(16),
        cost_estimate=cost(1e6, 4e6),
        name="pair_sum",
    )(ids, keep, got)


def feed_final_kernel(a0, a1, a2, a3, b0, b1, b2, b3, up_ref, down_ref):
    up_ref[...] = a0[...] + a1[...].astype(F32) + a2[...].astype(F32) + a3[...].astype(F32)
    down_ref[...] = b0[...] + b1[...].astype(F32) + b2[...].astype(F32) + b3[...].astype(F32)


def head_final_kernel(a0, a1, a2, a3, q_ref, k_ref, v_ref, o_ref):
    total = a0[...] + a1[...].astype(F32) + a2[...].astype(F32) + a3[...].astype(F32)
    n = q_ref.shape[1]
    q_ref[...] = total[:, :n]
    k_ref[...] = total[:, n : 2 * n]
    v_ref[...] = total[:, 2 * n : 3 * n]
    o_ref[...] = total[:, 3 * n :].T


def finish(kernel, arrays, outs, name):
    return pl.pallas_call(
        kernel,
        grid=(1,),
        in_specs=[whole(a.shape) for a in arrays],
        out_specs=[whole(o.shape) for o in outs],
        out_shape=outs,
        compiler_params=params(16),
        cost_estimate=cost(1e6, 3e6),
        name=name,
    )(*arrays)


def swap(array, axis, size, bits):
    return lax.ppermute(array, axis, [(i, i ^ bits) for i in range(size)])


def after(arrays, *others):
    return lax.optimization_barrier((tuple(arrays), others))[0]


def local(
    inputs, page_feat, page_onehot, lengths, hor_pos, ver_pos, norm1_gain, w_query, w_key, w_value,
    rel_table, hor_table, ver_table, w_output, norm2_gain, w_up, w_down, cotangent, *, dp,
):
    seq, width = inputs.shape
    fast = dp == 8
    over = functools.partial(swap, axis="mp", size=4)
    m = lax.axis_index("mp").astype(I32)
    d = lax.axis_index("dp").astype(I32)
    k4 = jnp.arange(4, dtype=I32)
    spot = lambda who: (who & 1) * 2 + (who >> 1)
    core, chip = m & 1, m >> 1
    ids = jnp.concatenate([
        spot(m ^ k4),
        k4 * 0,
        lengths[:1],
        (k4 + 2 * (1 - core)) % 4,
        (d & 1)[None],
        (k4 * 0)[:2],
        jnp.stack([spot(m), spot(m ^ 2), chip, 1 - chip]),
        jnp.stack([chip, chip, 1 - chip, 1 - chip]),
        (d >> 1) ^ k4,
    ])
    gain_one, gain_two = norm1_gain[None], norm2_gain[None]
    feats = page_feat[0]
    hor, ver = hor_pos[None], ver_pos[None]
    tables = jnp.concatenate([rel_table, hor_table, ver_table], axis=0).astype(F32).T
    pages = page_onehot.T
    weights = [w_query.T, w_key.T, w_value.T]

    normed1, queries, keys, values = project(ids, inputs, pages, feats, gain_one, *weights)

    own_weights = after([w_output, w_up, w_down, *weights], normed1)
    w_output, w_up, w_down = own_weights[:3]
    wo_y = over(w_output, bits=2)
    w_outputs = [w_output, over(w_output, bits=1), wo_y, over(wo_y, bits=1)]
    ups = [w_up, over(w_up, bits=1)]
    downs = [w_down, over(w_down, bits=1)]
    partner = [over(w, bits=1) for w in own_weights[3:]]

    e, att_own, att_other, inverse, out = attend(ids, queries, keys, values, hor, ver, tables)
    attended = [att_own, over(att_other, bits=1), over(att_own, bits=2), over(att_other, bits=3)]

    feed_args = (inputs, pages, feats, gain_two, cotangent, attended, w_outputs, ups, downs)
    x_act0, x_act1, x_up0, x_up1, x_normed, _, x_grad, x_ffn = feed(ids, False, *feed_args)
    sent_grad = over(x_grad, bits=2)
    m_act0, m_act1, m_up0, m_up1, m_normed, mixed, m_grad, m_ffn = feed(ids, True, *feed_args)
    grad_mixed, low, ga0, ga1, ga2, ga3, gain_two_part = mid(ids, m_grad, sent_grad, mixed, gain_two, cotangent, w_outputs)
    ga1, ga2, ga3 = over(ga1, bits=1), over(ga2, bits=2), over(ga3, bits=3)

    c_act1, c_up1, c_normed = over(m_act1, bits=1), over(m_up1, bits=1), over(m_normed, bits=1)
    cx_act1, cx_up1, cx_normed = over(x_act1, bits=1), over(x_up1, bits=1), over(x_normed, bits=1)
    down_grad = feed_grad(
        ids, [cotangent] * 4, [0, 1, 2, 3], [m_act0, c_act1, x_act0, cx_act1], fast, "down_grad"
    )
    up_grad = feed_grad(
        ids, [m_normed, c_normed, x_normed, cx_normed], [None] * 4, [m_up0, c_up1, x_up0, cx_up1], fast, "up_grad"
    )

    sent_ffn = over(x_ffn, bits=2)
    rows_out = (mixed + m_ffn + sent_ffn.astype(F32)).astype(BF)
    rows_y = over(rows_out, bits=2)
    outputs = join(ids, [rows_out, over(rows_out, bits=1), rows_y, over(rows_y, bits=1)], BF)

    scores_a, dq0, dq1, key_sum, value_sum, near, far = back(
        ids, e, queries, inverse, out, keys, values, ga0, ga1, None
    )
    scores_b, dq2, dq3, keep_kv, send_kv, near, far = back(
        ids, e, queries, inverse, out, keys, values, ga2, ga3, (key_sum, value_sum, near, far)
    )
    got1, got3, got_kv = over(dq1, bits=1), over(dq3, bits=1), over(send_kv, bits=1)
    other_terms = terms(False, weights, partner, dq2, keep_kv, got3, got_kv)
    sent_terms = over(other_terms, bits=2)
    own_terms = terms(True, weights, partner, dq0, keep_kv, got1, got_kv)

    low_y = over(low, bits=2)
    lows = [low, over(low, bits=1), low_y, over(low_y, bits=1)]
    head_grads = head_grad(ids, normed1, [dq0, dq1, dq2, dq3], keep_kv, send_kv, lows, att_own, att_other, fast)

    grad_rows, gain_one_part = last(ids, own_terms, sent_terms, inputs, pages, feats, gain_one, grad_mixed)
    grad_y = over(grad_rows, bits=2)
    grad_inputs, grad_feats = join(
        ids, [grad_rows, over(grad_rows, bits=1), grad_y, over(grad_y, bits=1)], F32, pages
    )

    positions = jnp.stack([hor, ver])
    scores_b, _ = after([scores_b, scores_a], head_grads[0], own_terms)
    table_sums = table_grads(ids, scores_a, scores_b, positions, near, far)

    gains = jnp.concatenate([gain_one_part, gain_two_part], axis=0)
    gains = gains + over(gains, bits=1)
    gains = gains + over(gains, bits=2)
    small = jnp.concatenate([gains.reshape(-1), table_sums.reshape(-1)])[None]
    size = width // dp
    n = w_query.shape[1]
    if fast:
        around = functools.partial(swap, axis="dp", size=dp)
        for bits in (1, 2, 4):
            small = small + around(small, bits=bits)
        reduced = []
        for keep, send in (down_grad, up_grad, head_grads):
            parts = pair_sum(ids, keep, around(send, bits=1))
            reduced.append([parts[0]] + [around(part, bits=2 * k) for k, part in zip((1, 2, 3), parts[1:])])
        units = w_up.shape[1]
        grad_up, grad_down = finish(
            feed_final_kernel, reduced[1] + reduced[0], [shape((size, units), F32)] * 2, "feed_final"
        )
        grad_query, grad_key, grad_value, grad_output = finish(
            head_final_kernel, reduced[2], [shape((size, n), F32)] * 3 + [shape((n, size), F32)], "head_final"
        )
    else:
        small = lax.psum(small, "dp")
        scatter = lambda a: lax.psum_scatter(a[0], "dp", scatter_dimension=0, tiled=True)
        grad_up, grad_down, heads = scatter(up_grad), scatter(down_grad), scatter(head_grads)
        grad_query, grad_key, grad_value = heads[:, :n], heads[:, n : 2 * n], heads[:, 2 * n : 3 * n]
        grad_output = heads[:, 3 * n :].T
    gain_sums = small[0, : 2 * width].reshape(2, width)
    mine = lax.dynamic_slice(gain_sums, (0, d * size), (2, size))
    bins = rel_table.shape[1]
    table_sums = small[0, 2 * width :].reshape(3, HEADS, bins)
    return (
        outputs, grad_inputs, grad_feats[None], mine[0], grad_query, grad_key, grad_value,
        table_sums[0], table_sums[1], table_sums[2], grad_output, mine[1], grad_up, grad_down.T,
    )


def solution(mesh):
    return jax.shard_map(
        functools.partial(local, dp=mesh.shape["dp"]),
        mesh=mesh,
        in_specs=(
            P("dp", None),
            P("dp", None, None),
            P("dp", None),
            P("dp"),
            P("dp"),
            P("dp"),
            P(),
            P(None, "mp"),
            P(None, "mp"),
            P(None, "mp"),
            P("mp", None),
            P("mp", None),
            P("mp", None),
            P("mp", None),
            P(),
            P(None, "mp"),
            P("mp", None),
            P("dp", None),
        ),
        out_specs=(
            P("dp", None),
            P("dp", None),
            P("dp", None, None),
            P("dp"),
            P("dp", "mp"),
            P("dp", "mp"),
            P("dp", "mp"),
            P("mp", None),
            P("mp", None),
            P("mp", None),
            P("mp", "dp"),
            P("dp"),
            P("dp", "mp"),
            P("mp", "dp"),
        ),
        check_vma=False,
    )
```

time: 853 us -> 243 us (0.28)
  waiting for transfers between devices: 463 us -> 57.8 us
  matrix products: 261 us -> 0 us
  Pallas kernels: 0 us -> 112 us
  other arithmetic: 46.8 us -> 1.82 us
  blocking collectives: 37.1 us -> 0 us
  starting transfers between devices: 1.36 us -> 36.4 us
  between operations: 16.7 us -> 2.03 us
  local copies, waits for them, and re-layouts: 18.3 us -> 32.2 us
    reduce_scatter x5 -> x0, waiting for transfers between devices: 280 us -> none  [the longest x1 72.1 us: local(): lax.psum_scatter(grad_w_down, 'dp', scatter_dimension=1, tiled=True)]
    dot_general x43 -> x0, matrix products: 258 us -> none  [the longest x6 90.9 us: attend_back(): jnp.einsum('pkm,fkm->pf', grad_scores, one_hot_ids(ids[which], tables[whi...]
    psum x3 -> x0, waiting for transfers between devices: 183 us -> none  [the longest x1 117 us: local(): result = mixed + lax.psum(ffn_terms, 'mp')]
    pallas_call x0 -> x21, Pallas kernels: none -> 112 us  [the longest x1 23.8 us: table_grads(): pl.pallas_call(tables_kernel, grid_spec=pltpu.PrefetchScalarGridSpec(num_...]
    ppermute x0 -> x52, waiting for transfers between devices: none -> 57.8 us  [swap(): return lax.ppermute(array, axis, [(i, i ^ bits) for i in range(size)])]
    unnamed x1 -> x0, blocking collectives: 37.1 us -> none
    ppermute x0 -> x52, starting transfers between devices: none -> 36.4 us  [swap(): return lax.ppermute(array, axis, [(i, i ^ bits) for i in range(size)])]
    add x8 -> x6, other arithmetic: 26.5 us -> 1.45 us  [the longest x3 0.73 us: local(): small = small + around(small, bits=bits)]
  transfers between devices with their start and end apart: 9 -> 52, of which waited for: 7 -> 12; matrix products, arithmetic and copies ran while one was open for 16% -> 2% of each run, Pallas kernels for 0% -> 39%
where the time goes in v1:
time: 243 us; the launch traced here: 242 us
  Pallas kernels  112 us (46%)
  waiting for transfers between devices  57.8 us (24%)
  starting transfers between devices  36.4 us (15%)
  local copies, waits for them, and re-layouts  32.2 us (13%)
    ppermute x52, waiting for transfers between devices, swap(): return lax.ppermute(array, axis, [(i, i ^ bits) for i in range(size)])  57.8 us
    ppermute x52, starting transfers between devices, swap(): return lax.ppermute(array, axis, [(i, i ^ bits) for i in range(size)])  36.4 us
    unnamed x135, local copies, waits for them, and re-layouts  28.7 us
    pallas_call x1, Pallas kernels, table_grads(): pl.pallas_call(tables_kernel, grid_spec=pltpu.PrefetchScalarGridSpec(num_...  23.8 us
    pallas_call x1, Pallas kernels, attend(): pl.pallas_call(functools.partial(attend_kernel, width=width, chunk=32), g...  22.1 us
    pallas_call x2, Pallas kernels, feed(): pl.pallas_call(feed_kernel, grid_spec=pltpu.PrefetchScalarGridSpec(num_sc...  18.7 us
    pallas_call x2, Pallas kernels, back(): pl.pallas_call(functools.partial(back_kernel, first=first), grid_spec=plt...  17.9 us
    pallas_call x2, Pallas kernels, join(): pl.pallas_call(join_kernel if onehot is None else join_feat_kernel, grid_...  6.45 us
  transfers between devices with their start and end apart: 52, of which 12 were waited for; matrix products, arithmetic and copies ran while one was open for 2% of the time, Pallas kernels for 39%

profile of v1, /device:TPU:0, one launch (start us, length us, event | category | flops | bytes accessed | tf_op | source)
XLA Modules:
  0.0 241.8 jit_solution(3888564107883320487)
XLA Ops:
  7.9 4.2 %project.1 = (bf16[1024,768]{1,0:T(8,128)(2,1)S(1)}, bf16[1024,384]{1,0:T(8,128)(2,1)S(1)}, bf16[1024,384]{1,0:T(8,128)(2,1)S(1)}, bf16[1024,384]{1,0:T(8,128)(2,1)S(1)}) custom-call(s32[28]{0:T(128)S(1)} %concatenate.12.ids.refs_0_, bf16[1024,768]{1,0:T(8,128)(2,1)S(1)} %copy-done.1, s32[8,1024]{1,0:T(8,128)S(1)} %bitcast.34, bf16[8,768]{1,0:T(8,128)(2,1)S(1)} %bitcast.39, ...), custom_call_target="tpu_custom_call" | custom-call | flops 905969664 | bytes 3145728 | tf_op jit(solution)/shard_map/project/pallas_call | solution.py:102
  14.0 3.0 %collective-permute-start.4 = (bf16[192,768]{1,0:T(8,128)(2,1)S(1)}, bf16[192,768]{1,0:T(8,128)(2,1)S(1)}, u32[]{:S(2)}, u32[]{:S(2)}) collective-permute-start(bf16[192,768]{1,0:T(8,128)(2,1)S(1)} %copy-done.11), channel_id=1, source_target_pairs={{0,2},{1,3},{2,0},{3,1},{4,6},{5,7},{6,4},{7,5},{8,10},{9,11},{10,... | collective-permute-start | bytes 884744 | tf_op jit(solution)/shard_map/ppermute | solution.py:871
  20.1 22.1 %attend.1 = (bf16[3,1024,1024]{2,1,0:T(8,128)(2,1)S(1)}, bf16[192,512]{1,0:T(8,128)(2,1)S(1)}, bf16[192,512]{1,0:T(8,128)(2,1)S(1)}, f32[3,1024]{1,0:T(4,128)S(1)}, f32[192,1024]{1,0:T(8,128)S(1)}) custom-call(s32[28]{0:T(128)S(1)} %concatenate.12.ids.refs_0_, bf16[1024,384]{1,0:T(8,128)(2,1)S(1)} %get-tuple-element.94.q_ref.refs_3_.refs_4_, ...), custom_call_target="tpu_custom_call" | custom-call | flops 24999999488 | bytes 10000000 | tf_op jit(solution)/shard_map/attend/pallas_call | solution.py:230
  42.2 2.6 %copy-done.41 = bf16[3,1024,1024]{2,1,0:T(8,128)(2,1)} copy-done((bf16[3,1024,1024]{2,1,0:T(8,128)(2,1)}, bf16[3,1024,1024]{2,1,0:T(8,128)(2,1)S(1)}, u32[]{:S(2)}) %copy-start.41) | copy-done | bytes 6291480
  46.8 5.4 %collective-permute-done.1.a2 = bf16[192,512]{1,0:T(8,128)(2,1)S(1)} collective-permute-done((bf16[192,512]{1,0:T(8,128)(2,1)S(1)}, bf16[192,512]{1,0:T(8,128)(2,1)S(1)}, u32[]{:S(2)}, u32[]{:S(2)}) %collective-permute-start.1) | collective-permute-done | bytes 196640 | tf_op jit(solution)/shard_map/ppermute | solution.py:871
  52.1 7.1 %collective-permute-done.2.a3 = bf16[192,512]{1,0:T(8,128)(2,1)S(1)} collective-permute-done((bf16[192,512]{1,0:T(8,128)(2,1)S(1)}, bf16[192,512]{1,0:T(8,128)(2,1)S(1)}, u32[]{:S(2)}, u32[]{:S(2)}) %collective-permute-start.2) | collective-permute-done | bytes 196640 | tf_op jit(solution)/shard_map/ppermute | solution.py:871
  59.3 10.0 %feed_other.1 = (bf16[256,768]{1,0:T(8,128)(2,1)S(1)}, bf16[256,768]{1,0:T(8,128)(2,1)S(1)}, bf16[256,768]{1,0:T(8,128)(2,1)S(1)}, bf16[256,768]{1,0:T(8,128)(2,...) custom-call(s32[28]{0:T(128)S(1)} %concatenate.12.ids.refs_0_, ...), custom_call_target="tpu_custom_call" | custom-call | flops 2717908992 | bytes 8000000 | tf_op jit(solution)/shard_map/feed_other/pallas_call | solution.py:333
  70.1 8.8 %feed_own.1 = (bf16[256,768]{1,0:T(8,128)(2,1)S(1)}, bf16[256,768]{1,0:T(8,128)(2,1)S(1)}, bf16[256,768]{1,0:T(8,128)(2,1)S(1)}, bf16[256,768]{1,0:T(8,128)(2,1)...) custom-call(s32[28]{0:T(128)S(1)} %concatenate.12.ids.refs_0_, ...), custom_call_target="tpu_custom_call" | custom-call | flops 2717908992 | bytes 8000000 | tf_op jit(solution)/shard_map/feed_own/pallas_call | solution.py:333
  78.9 2.2 collective-permute-done.15.sent_ref
  86.4 8.9 %back_first.1 = (bf16[3,1024,512]{2,1,0:T(8,128)(2,1)S(1)}, bf16[192,256]{1,0:T(8,128)(2,1)S(1)}, bf16[192,256]{1,0:T(8,128)(2,1)S(1)}, f32[1024,384]{1,0:T(8,12...) custom-call(s32[28]{0:T(128)S(1)} %concatenate.12.ids.refs_0_, ...), custom_call_target="tpu_custom_call" | custom-call | flops 6000000000 | bytes 10000000 | tf_op jit(solution)/shard_map/back_first/pallas_call | solution.py:508
  98.5 1.7 copy-done.59
  105.8 9.0 %back_last.1 = (bf16[3,1024,512]{2,1,0:T(8,128)(2,1)S(1)}, bf16[192,256]{1,0:T(8,128)(2,1)S(1)}, bf16[192,256]{1,0:T(8,128)(2,1)S(1)}, bf16[2,2,192,256]{3,2,1,0...) custom-call(s32[28]{0:T(128)S(1)} %concatenate.12.ids.refs_0_, ...), custom_call_target="tpu_custom_call" | custom-call | flops 6000000000 | bytes 10000000 | tf_op jit(solution)/shard_map/back_last/pallas_call | solution.py:508
  115.3 1.7 collective-permute-start.29
  117.0 2.1 down_grad.1
  120.7 3.6 %up_grad.1 = (f32[4,96,768]{2,1,0:T(8,128)S(1)}, bf16[4,96,768]{2,1,0:T(8,128)(2,1)S(1)}) custom-call(s32[28]{0:T(128)S(1)} %concatenate.12.ids.refs_0_, bf16[256,768]{1,0:T(8,128)(2,1)S(1)} %copy-done.33, bf16[256,768]{1,0:T(8,128)(2,1)} %collective-permute-done.38.refs_1_, bf16[256,768]{1,0:T(8,128)(2,1)} %get-tuple-element.151.refs_2_, ...), custom_call_target="tpu_custom_call" | custom-call | flops 1207959552 | bytes 8000000 | tf_op jit(solution)/shard_map/up_grad/pallas_call | solution.py:756
  127.4 8.0 %collective-permute-done.29.l2 = bf16[256,768]{1,0:T(8,128)(2,1)S(1)} collective-permute-done((bf16[256,768]{1,0:T(8,128)(2,1)S(1)}, bf16[256,768]{1,0:T(8,128)(2,1)S(1)}, u32[]{:S(2)}, u32[]{:S(2)}) %collective-permute-start.29) | collective-permute-done | bytes 393248 | tf_op jit(solution)/shard_map/ppermute | solution.py:871
  138.2 8.7 %collective-permute-done.42.got_ref = bf16[4,96,768]{2,1,0:T(8,128)(2,1)S(1)} collective-permute-done((bf16[4,96,768]{2,1,0:T(8,128)(2,1)S(1)}, bf16[4,96,768]{2,1,0:T(8,128)(2,1)S(1)}, u32[]{:S(2)}, u32[]{:S(2)}) %collective-permute-start.42) | collective-permute-done | bytes 589856 | tf_op jit(solution)/shard_map/ppermute | solution.py:871
  149.8 2.6 %collective-permute-start.50 = (bf16[96,768]{1,0:T(8,128)(2,1)}, bf16[96,768]{1,0:T(8,128)(2,1)}, u32[]{:S(2)}, u32[]{:S(2)}) collective-permute-start(bf16[96,768]{1,0:T(8,128)(2,1)} %get-tuple-element.170), channel_id=1, source_target_pairs={{0,16},{4,20},{8,24},{12,28},{16,0},{20,4},{24,8},{28,12},{1,17},{... | collective-permute-start | bytes 442376 | tf_op jit(solution)/shard_map/ppermute | solution.py:871
  154.1 2.2 head_grad.1
  157.2 23.8 %table_grads.1 = f32[9,32,1]{2,1,0:T(8,128)S(1)} custom-call(s32[28]{0:T(128)S(1)} %concatenate.12.ids.refs_0_, bf16[3,1024,512]{2,1,0:T(8,128)(2,1)S(1)} %copy-done.60, bf16[3,1024,512]{2,1,0:T(8,128)(2,1)} %copy-done.42, s32[2,1,1024]{2,1,0:T(1,128)S(1)} %pad_add_fusion.keys_ref.q0.q1.q2.q3, s32[2,1,1024]{2,1,0:T(1,128)S(1)} %pad_add_fusion.keys_ref.q0.q1.q2.q3, ...), custom_call_target="tpu_custom_call" | custom-call | flops 16000000000 | bytes 8000000 | tf_op jit(solution)/shard_map/table_grads/pallas_call | solution.py:591
  184.8 3.5 %collective-permute-start.44 = (bf16[96,768]{1,0:T(8,128)(2,1)}, bf16[96,768]{1,0:T(8,128)(2,1)S(1)}, u32[]{:S(2)}, u32[]{:S(2)}) collective-permute-start(bf16[96,768]{1,0:T(8,128)(2,1)} %get-tuple-element.160), channel_id=1, source_target_pairs={{0,16},{4,20},{8,24},{12,28},{16,0},{20,4},{24,8},{28,12},{1,17},{... | collective-permute-start | bytes 442376 | tf_op jit(solution)/shard_map/ppermute | solution.py:871
  190.1 5.5 %collective-permute-done.44.a2 = bf16[96,768]{1,0:T(8,128)(2,1)S(1)} collective-permute-done((bf16[96,768]{1,0:T(8,128)(2,1)}, bf16[96,768]{1,0:T(8,128)(2,1)S(1)}, u32[]{:S(2)}, u32[]{:S(2)}) %collective-permute-start.44) | collective-permute-done | bytes 147488 | tf_op jit(solution)/shard_map/ppermute | solution.py:871
  196.3 3.6 %collective-permute-done.32 = f32[1,1824]{1,0:T(1,128)S(1)} collective-permute-done((f32[1,1824]{1,0:T(1,128)S(1)}, f32[1,1824]{1,0:T(1,128)S(1)}, u32[]{:S(2)}, u32[]{:S(2)}) %collective-permute-start.32) | collective-permute-done | bytes 7328 | tf_op jit(solution)/shard_map/ppermute | solution.py:871
  200.0 2.3 collective-permute-start.45
  202.3 4.9 %collective-permute-done.45.a3 = bf16[96,768]{1,0:T(8,128)(2,1)S(1)} collective-permute-done((bf16[96,768]{1,0:T(8,128)(2,1)}, bf16[96,768]{1,0:T(8,128)(2,1)S(1)}, u32[]{:S(2)}, u32[]{:S(2)}) %collective-permute-start.45) | collective-permute-done | bytes 147488 | tf_op jit(solution)/shard_map/ppermute | solution.py:871
  207.9 2.0 collective-permute-start.33
  213.6 1.9 feed_final.1
  215.6 3.4 %join_output.1 = bf16[1024,768]{1,0:T(8,128)(2,1)} custom-call(s32[28]{0:T(128)S(1)} %concatenate.12.ids.refs_0_, bf16[256,768]{1,0:T(8,128)(2,1)S(1)} %add_convert_fusion.b0, bf16[256,768]{1,0:T(8,128)(2,1)S(1)} %collective-permute-done.9.b1, bf16[256,768]{1,0:T(8,128)(2,1)} %collective-permute-done.10.b2, bf16[256,768]{1,0:T(8,128)(2,1)} %collective-permute-done.11.b3), custom_call_target="tpu_custom_call" | custom-call | flops 1000000 | bytes 6000000 | tf_op jit(solution)/shard_map/join_output/pallas_call | solution.py:706
  225.4 2.1 collective-permute-start.37
  228.1 2.9 %collective-permute-done.35.a1 = bf16[96,768]{1,0:T(8,128)(2,1)S(1)} collective-permute-done((bf16[96,768]{1,0:T(8,128)(2,1)S(1)}, bf16[96,768]{1,0:T(8,128)(2,1)S(1)}, u32[]{:S(2)}, u32[]{:S(2)}) %collective-permute-start.35) | collective-permute-done | bytes 147488 | tf_op jit(solution)/shard_map/ppermute | solution.py:871
  231.0 6.9 %collective-permute-done.36.a2 = bf16[96,768]{1,0:T(8,128)(2,1)S(1)} collective-permute-done((bf16[96,768]{1,0:T(8,128)(2,1)S(1)}, bf16[96,768]{1,0:T(8,128)(2,1)S(1)}, u32[]{:S(2)}, u32[]{:S(2)}) %collective-permute-start.36) | collective-permute-done | bytes 147488 | tf_op jit(solution)/shard_map/ppermute | solution.py:871
  238.7 3.1 %join_grads.1 = (f32[1024,768]{1,0:T(8,128)}, f32[8,768]{1,0:T(8,128)}) custom-call(s32[28]{0:T(128)S(1)} %concatenate.12.ids.refs_0_, bf16[256,768]{1,0:T(8,128)(2,1)S(1)} %copy-done.10, bf16[256,768]{1,0:T(8,128)(2,1)S(1)} %collective-permute-done.23.b1, bf16[256,768]{1,0:T(8,128)(2,1)S(1)} %collective-permute-done.24.b2, ...), custom_call_target="tpu_custom_call" | custom-call | flops 1000000 | bytes 6000000 | tf_op jit(solution)/shard_map/join_grads/pallas_call | solution.py:706
  (257 shorter events, 60.1 us)
Async XLA Ops:
  14.0 32.4 %collective-permute-start.4 = (bf16[192,768]{1,0:T(8,128)(2,1)S(1)}, bf16[192,768]{1,0:T(8,128)(2,1)S(1)}, u32[]{:S(2)}, u32[]{:S(2)}) collective-permute-start(bf16[192,768]{1,0:T(8,128)(2,1)S(1)} %copy-done.11), channel_id=1, source_target_pairs={{0,2},{1,3},{2,0},{3,1},{4,6},{5,7},{6,4},{7,5},{8,10},{9,11},{10,... | collective-permute-start | bytes 884744 | tf_op jit(solution)/shard_map/ppermute | solution.py:871
  16.9 42.3 %collective-permute-start.6 = (bf16[768,768]{1,0:T(8,128)(2,1)}, bf16[768,768]{1,0:T(8,128)(2,1)}, u32[]{:S(2)}, u32[]{:S(2)}) collective-permute-start(bf16[768,768]{1,0:T(8,128)(2,1)} %u0.1), channel_id=1, source_target_pairs={{0,1},{1,0},{2,3},{3,2},{4,5},{5,4},{6,7},{7,6},{8,9},{9,8},{10,11... | collective-permute-start | bytes 3538952 | tf_op jit(solution)/shard_map/ppermute | solution.py:871
  16.9 42.3 %collective-permute-start.7 = (bf16[768,768]{1,0:T(8,128)(2,1)}, bf16[768,768]{1,0:T(8,128)(2,1)}, u32[]{:S(2)}, u32[]{:S(2)}) collective-permute-start(bf16[768,768]{1,0:T(8,128)(2,1)} %d0.1), channel_id=1, source_target_pairs={{0,1},{1,0},{2,3},{3,2},{4,5},{5,4},{6,7},{7,6},{8,9},{9,8},{10,11... | collective-permute-start | bytes 3538952 | tf_op jit(solution)/shard_map/ppermute | solution.py:871
  70.1 13.7 %collective-permute-start.12 = (bf16[192,768]{1,0:T(8,128)(2,1)S(1)}, bf16[192,768]{1,0:T(8,128)(2,1)S(1)}, u32[]{:S(2)}, u32[]{:S(2)}) collective-permute-start(bf16[192,768]{1,0:T(8,128)(2,1)S(1)} %bitcast.23), channel_id=1, source_target_pairs={{0,1},{1,0},{2,3},{3,2},{4,5},{5,4},{6,7},{7,6},{8,9},{9,8},{10,11... | collective-permute-start | bytes 884744 | tf_op jit(solution)/shard_map/ppermute | solution.py:871
  82.8 17.4 %collective-permute-start.13 = (bf16[192,768]{1,0:T(8,128)(2,1)S(1)}, bf16[192,768]{1,0:T(8,128)(2,1)S(1)}, u32[]{:S(2)}, u32[]{:S(2)}) collective-permute-start(bf16[192,768]{1,0:T(8,128)(2,1)S(1)} %bitcast.27), channel_id=1, source_target_pairs={{0,1},{1,0},{2,3},{3,2},{4,5},{5,4},{6,7},{7,6},{8,9},{9,8},{10,11... | collective-permute-start | bytes 884744 | tf_op jit(solution)/shard_map/ppermute | solution.py:871
  83.3 17.6 %collective-permute-start.14 = (bf16[192,768]{1,0:T(8,128)(2,1)S(1)}, bf16[192,768]{1,0:T(8,128)(2,1)S(1)}, u32[]{:S(2)}, u32[]{:S(2)}) collective-permute-start(bf16[192,768]{1,0:T(8,128)(2,1)S(1)} %bitcast.31), channel_id=1, source_target_pairs={{0,1},{1,0},{2,3},{3,2},{4,5},{5,4},{6,7},{7,6},{8,9},{9,8},{10,11... | collective-permute-start | bytes 884744 | tf_op jit(solution)/shard_map/ppermute | solution.py:871
  83.3 17.6 %collective-permute-start.46 = (bf16[256,768]{1,0:T(8,128)(2,1)S(1)}, bf16[256,768]{1,0:T(8,128)(2,1)S(1)}, u32[]{:S(2)}, u32[]{:S(2)}) collective-permute-start(bf16[256,768]{1,0:T(8,128)(2,1)S(1)} %get-tuple-element.163), channel_id=1, source_target_pairs={{0,1},{1,0},{2,3},{3,2},{4,5},{5,4},{6,7},{7,6},{8,9},{9,8},{10,11... | collective-permute-start | bytes 1179656 | tf_op jit(solution)/shard_map/ppermute | solution.py:871
  83.8 17.6 %collective-permute-start.17 = (bf16[192,256]{1,0:T(8,128)(2,1)S(1)}, bf16[192,256]{1,0:T(8,128)(2,1)S(1)}, u32[]{:S(2)}, u32[]{:S(2)}) collective-permute-start(bf16[192,256]{1,0:T(8,128)(2,1)S(1)} %get-tuple-element.117), channel_id=1, source_target_pairs={{0,2},{1,3},{2,0},{3,1},{4,6},{5,7},{6,4},{7,5},{8,10},{9,11},{10,... | collective-permute-start | bytes 294920 | tf_op jit(solution)/shard_map/ppermute | solution.py:871
  84.1 17.4 %collective-permute-start.18 = (bf16[192,256]{1,0:T(8,128)(2,1)S(1)}, bf16[192,256]{1,0:T(8,128)(2,1)S(1)}, u32[]{:S(2)}, u32[]{:S(2)}) collective-permute-start(bf16[192,256]{1,0:T(8,128)(2,1)S(1)} %get-tuple-element.118), channel_id=1, source_target_pairs={{0,3},{1,2},{2,1},{3,0},{4,7},{5,6},{6,5},{7,4},{8,11},{9,10},{10,... | collective-permute-start | bytes 294920 | tf_op jit(solution)/shard_map/ppermute | solution.py:871
  100.2 14.6 %collective-permute-start.47 = (bf16[256,768]{1,0:T(8,128)(2,1)S(1)}, bf16[256,768]{1,0:T(8,128)(2,1)S(1)}, u32[]{:S(2)}, u32[]{:S(2)}) collective-permute-start(bf16[256,768]{1,0:T(8,128)(2,1)S(1)} %get-tuple-element.165), channel_id=1, source_target_pairs={{0,1},{1,0},{2,3},{3,2},{4,5},{5,4},{6,7},{7,6},{8,9},{9,8},{10,11... | collective-permute-start | bytes 1179656 | tf_op jit(solution)/shard_map/ppermute | solution.py:871
  100.9 14.0 %collective-permute-start.38 = (bf16[256,768]{1,0:T(8,128)(2,1)S(1)}, bf16[256,768]{1,0:T(8,128)(2,1)}, u32[]{:S(2)}, u32[]{:S(2)}) collective-permute-start(bf16[256,768]{1,0:T(8,128)(2,1)S(1)} %get-tuple-element.150.refs_0_), channel_id=1, source_target_pairs={{0,1},{1,0},{2,3},{3,2},{4,5},{5,4},{6,7},{7,6},{8,9},{9,8},{10,11... | collective-permute-start | bytes 1179656 | tf_op jit(solution)/shard_map/ppermute | solution.py:871
  101.0 14.3 %collective-permute-start.40 = (bf16[256,768]{1,0:T(8,128)(2,1)S(1)}, bf16[256,768]{1,0:T(8,128)(2,1)}, u32[]{:S(2)}, u32[]{:S(2)}) collective-permute-start(bf16[256,768]{1,0:T(8,128)(2,1)S(1)} %get-tuple-element.153), channel_id=1, source_target_pairs={{0,1},{1,0},{2,3},{3,2},{4,5},{5,4},{6,7},{7,6},{8,9},{9,8},{10,11... | collective-permute-start | bytes 1179656 | tf_op jit(solution)/shard_map/ppermute | solution.py:871
  101.4 17.7 %collective-permute-start.39 = (bf16[256,768]{1,0:T(8,128)(2,1)}, bf16[256,768]{1,0:T(8,128)(2,1)}, u32[]{:S(2)}, u32[]{:S(2)}) collective-permute-start(bf16[256,768]{1,0:T(8,128)(2,1)} %get-tuple-element.151.refs_2_), channel_id=1, source_target_pairs={{0,1},{1,0},{2,3},{3,2},{4,5},{5,4},{6,7},{7,6},{8,9},{9,8},{10,11... | collective-permute-start | bytes 1179656 | tf_op jit(solution)/shard_map/ppermute | solution.py:871
  101.5 19.2 %collective-permute-start.41 = (bf16[256,768]{1,0:T(8,128)(2,1)}, bf16[256,768]{1,0:T(8,128)(2,1)}, u32[]{:S(2)}, u32[]{:S(2)}) collective-permute-start(bf16[256,768]{1,0:T(8,128)(2,1)} %get-tuple-element.155), channel_id=1, source_target_pairs={{0,1},{1,0},{2,3},{3,2},{4,5},{5,4},{6,7},{7,6},{8,9},{9,8},{10,11... | collective-permute-start | bytes 1179656 | tf_op jit(solution)/shard_map/ppermute | solution.py:871
  115.3 20.2 %collective-permute-start.29 = (bf16[256,768]{1,0:T(8,128)(2,1)S(1)}, bf16[256,768]{1,0:T(8,128)(2,1)S(1)}, u32[]{:S(2)}, u32[]{:S(2)}) collective-permute-start(bf16[256,768]{1,0:T(8,128)(2,1)S(1)} %get-tuple-element.136.l0), channel_id=1, source_target_pairs={{0,2},{1,3},{2,0},{3,1},{4,6},{5,7},{6,4},{7,5},{8,10},{9,11},{10,... | collective-permute-start | bytes 1179656 | tf_op jit(solution)/shard_map/ppermute | solution.py:871
  119.1 17.3 %collective-permute-start.48 = (bf16[4,96,768]{2,1,0:T(8,128)(2,1)S(1)}, bf16[4,96,768]{2,1,0:T(8,128)(2,1)S(1)}, u32[]{:S(2)}, u32[]{:S(2)}) collective-permute-start(bf16[4,96,768]{2,1,0:T(8,128)(2,1)S(1)} %get-tuple-element.167), channel_id=1, source_target_pairs={{0,4},{4,0},{8,12},{12,8},{16,20},{20,16},{24,28},{28,24},{1,5},{5... | collective-permute-start | bytes 1769480 | tf_op jit(solution)/shard_map/ppermute | solution.py:871
  124.3 22.6 %collective-permute-start.42 = (bf16[4,96,768]{2,1,0:T(8,128)(2,1)S(1)}, bf16[4,96,768]{2,1,0:T(8,128)(2,1)S(1)}, u32[]{:S(2)}, u32[]{:S(2)}) collective-permute-start(bf16[4,96,768]{2,1,0:T(8,128)(2,1)S(1)} %get-tuple-element.157), channel_id=1, source_target_pairs={{0,4},{4,0},{8,12},{12,8},{16,20},{20,16},{24,28},{28,24},{1,5},{5... | collective-permute-start | bytes 1769480 | tf_op jit(solution)/shard_map/ppermute | solution.py:871
  127.1 22.8 %collective-permute-start.22 = (bf16[256,768]{1,0:T(8,128)(2,1)S(1)}, bf16[256,768]{1,0:T(8,128)(2,1)S(1)}, u32[]{:S(2)}, u32[]{:S(2)}) collective-permute-start(bf16[256,768]{1,0:T(8,128)(2,1)S(1)} %terms_other.1), channel_id=1, source_target_pairs={{0,2},{1,3},{2,0},{3,1},{4,6},{5,7},{6,4},{7,5},{8,10},{9,11},{10,... | collective-permute-start | bytes 1179656 | tf_op jit(solution)/shard_map/ppermute | solution.py:871
  127.4 26.3 %collective-permute-start.28 = (bf16[256,768]{1,0:T(8,128)(2,1)S(1)}, bf16[256,768]{1,0:T(8,128)(2,1)S(1)}, u32[]{:S(2)}, u32[]{:S(2)}) collective-permute-start(bf16[256,768]{1,0:T(8,128)(2,1)S(1)} %get-tuple-element.136.l0), channel_id=1, source_target_pairs={{0,1},{1,0},{2,3},{3,2},{4,5},{5,4},{6,7},{7,6},{8,9},{9,8},{10,11... | collective-permute-start | bytes 1179656 | tf_op jit(solution)/shard_map/ppermute | solution.py:871
  135.5 18.6 %collective-permute-start.30 = (bf16[256,768]{1,0:T(8,128)(2,1)S(1)}, bf16[256,768]{1,0:T(8,128)(2,1)S(1)}, u32[]{:S(2)}, u32[]{:S(2)}) collective-permute-start(bf16[256,768]{1,0:T(8,128)(2,1)S(1)} %collective-permute-done.29.l2), channel_id=1, source_target_pairs={{0,1},{1,0},{2,3},{3,2},{4,5},{5,4},{6,7},{7,6},{8,9},{9,8},{10,11... | collective-permute-start | bytes 1179656 | tf_op jit(solution)/shard_map/ppermute | solution.py:871
  136.5 46.2 %collective-permute-start.10 = (bf16[256,768]{1,0:T(8,128)(2,1)S(1)}, bf16[256,768]{1,0:T(8,128)(2,1)}, u32[]{:S(2)}, u32[]{:S(2)}) collective-permute-start(bf16[256,768]{1,0:T(8,128)(2,1)S(1)} %add_convert_fusion.b0), channel_id=1, source_target_pairs={{0,2},{1,3},{2,0},{3,1},{4,6},{5,7},{6,4},{7,5},{8,10},{9,11},{10,... | collective-permute-start | bytes 1179656 | tf_op jit(solution)/shard_map/ppermute | solution.py:871
  146.9 37.3 %collective-permute-start.49 = (bf16[96,768]{1,0:T(8,128)(2,1)}, bf16[96,768]{1,0:T(8,128)(2,1)}, u32[]{:S(2)}, u32[]{:S(2)}) collective-permute-start(bf16[96,768]{1,0:T(8,128)(2,1)} %get-tuple-element.169), channel_id=1, source_target_pairs={{0,8},{4,12},{8,0},{12,4},{16,24},{20,28},{24,16},{28,20},{1,9},{5... | collective-permute-start | bytes 442376 | tf_op jit(solution)/shard_map/ppermute | solution.py:871
  149.8 34.5 %collective-permute-start.50 = (bf16[96,768]{1,0:T(8,128)(2,1)}, bf16[96,768]{1,0:T(8,128)(2,1)}, u32[]{:S(2)}, u32[]{:S(2)}) collective-permute-start(bf16[96,768]{1,0:T(8,128)(2,1)} %get-tuple-element.170), channel_id=1, source_target_pairs={{0,16},{4,20},{8,24},{12,28},{16,0},{20,4},{24,8},{28,12},{1,17},{... | collective-permute-start | bytes 442376 | tf_op jit(solution)/shard_map/ppermute | solution.py:871
  153.8 31.0 %collective-permute-start.51 = (bf16[96,768]{1,0:T(8,128)(2,1)}, bf16[96,768]{1,0:T(8,128)(2,1)}, u32[]{:S(2)}, u32[]{:S(2)}) collective-permute-start(bf16[96,768]{1,0:T(8,128)(2,1)} %get-tuple-element.171), channel_id=1, source_target_pairs={{0,24},{4,28},{8,16},{12,20},{16,8},{20,12},{24,0},{28,4},{1,25},{... | collective-permute-start | bytes 442376 | tf_op jit(solution)/shard_map/ppermute | solution.py:871
  156.4 24.8 %collective-permute-start.27 = (f32[2,768]{1,0:T(2,128)S(1)}, f32[2,768]{1,0:T(2,128)S(1)}, u32[]{:S(2)}, u32[]{:S(2)}) collective-permute-start(f32[2,768]{1,0:T(2,128)S(1)} %fusion.1), channel_id=1, source_target_pairs={{0,2},{1,3},{2,0},{3,1},{4,6},{5,7},{6,4},{7,5},{8,10},{9,11},{10,... | collective-permute-start | bytes 18440 | tf_op jit(solution)/shard_map/ppermute | solution.py:871
  184.3 31.3 %collective-permute-start.9 = (bf16[256,768]{1,0:T(8,128)(2,1)S(1)}, bf16[256,768]{1,0:T(8,128)(2,1)S(1)}, u32[]{:S(2)}, u32[]{:S(2)}) collective-permute-start(bf16[256,768]{1,0:T(8,128)(2,1)S(1)} %add_convert_fusion.b0), channel_id=1, source_target_pairs={{0,1},{1,0},{2,3},{3,2},{4,5},{5,4},{6,7},{7,6},{8,9},{9,8},{10,11... | collective-permute-start | bytes 1179656 | tf_op jit(solution)/shard_map/ppermute | solution.py:871
  184.3 31.3 %collective-permute-start.11 = (bf16[256,768]{1,0:T(8,128)(2,1)}, bf16[256,768]{1,0:T(8,128)(2,1)}, u32[]{:S(2)}, u32[]{:S(2)}) collective-permute-start(bf16[256,768]{1,0:T(8,128)(2,1)} %collective-permute-done.10.b2), channel_id=1, source_target_pairs={{0,1},{1,0},{2,3},{3,2},{4,5},{5,4},{6,7},{7,6},{8,9},{9,8},{10,11... | collective-permute-start | bytes 1179656 | tf_op jit(solution)/shard_map/ppermute | solution.py:871
  188.3 34.1 %collective-permute-start.34 = (bf16[4,96,768]{2,1,0:T(8,128)(2,1)}, bf16[4,96,768]{2,1,0:T(8,128)(2,1)S(1)}, u32[]{:S(2)}, u32[]{:S(2)}) collective-permute-start(bf16[4,96,768]{2,1,0:T(8,128)(2,1)} %copy-done.31), channel_id=1, source_target_pairs={{0,4},{4,0},{8,12},{12,8},{16,20},{20,16},{24,28},{28,24},{1,5},{5... | collective-permute-start | bytes 1769480 | tf_op jit(solution)/shard_map/ppermute | solution.py:871
  189.0 30.7 %collective-permute-start.24 = (bf16[256,768]{1,0:T(8,128)(2,1)S(1)}, bf16[256,768]{1,0:T(8,128)(2,1)S(1)}, u32[]{:S(2)}, u32[]{:S(2)}) collective-permute-start(bf16[256,768]{1,0:T(8,128)(2,1)S(1)} %copy-done.10), channel_id=1, source_target_pairs={{0,2},{1,3},{2,0},{3,1},{4,6},{5,7},{6,4},{7,5},{8,10},{9,11},{10,... | collective-permute-start | bytes 1179656 | tf_op jit(solution)/shard_map/ppermute | solution.py:871
  219.0 19.8 %collective-permute-start.23 = (bf16[256,768]{1,0:T(8,128)(2,1)S(1)}, bf16[256,768]{1,0:T(8,128)(2,1)S(1)}, u32[]{:S(2)}, u32[]{:S(2)}) collective-permute-start(bf16[256,768]{1,0:T(8,128)(2,1)S(1)} %copy-done.10), channel_id=1, source_target_pairs={{0,1},{1,0},{2,3},{3,2},{4,5},{5,4},{6,7},{7,6},{8,9},{9,8},{10,11... | collective-permute-start | bytes 1179656 | tf_op jit(solution)/shard_map/ppermute | solution.py:871
  219.7 19.0 %collective-permute-start.25 = (bf16[256,768]{1,0:T(8,128)(2,1)S(1)}, bf16[256,768]{1,0:T(8,128)(2,1)S(1)}, u32[]{:S(2)}, u32[]{:S(2)}) collective-permute-start(bf16[256,768]{1,0:T(8,128)(2,1)S(1)} %collective-permute-done.24.b2), channel_id=1, source_target_pairs={{0,1},{1,0},{2,3},{3,2},{4,5},{5,4},{6,7},{7,6},{8,9},{9,8},{10,11... | collective-permute-start | bytes 1179656 | tf_op jit(solution)/shard_map/ppermute | solution.py:871
  224.0 13.9 %collective-permute-start.36 = (bf16[96,768]{1,0:T(8,128)(2,1)S(1)}, bf16[96,768]{1,0:T(8,128)(2,1)S(1)}, u32[]{:S(2)}, u32[]{:S(2)}) collective-permute-start(bf16[96,768]{1,0:T(8,128)(2,1)S(1)} %get-tuple-element.144), channel_id=1, source_target_pairs={{0,16},{4,20},{8,24},{12,28},{16,0},{20,4},{24,8},{28,12},{1,17},{... | collective-permute-start | bytes 442376 | tf_op jit(solution)/shard_map/ppermute | solution.py:871
  (86 other events, 675.3 us)

commit v2 on v1

v2 whole, which is shorter than its diff:
```python
import functools

import jax
import jax.numpy as jnp
import numpy as np
from jax import lax
from jax.experimental import pallas as pl
from jax.experimental.pallas import tpu as pltpu
from jax.sharding import PartitionSpec as P

EPS = 1e-06
THRESHOLDS = (12, 16, 23, 32, 46, 64, 91)
FAR = 91
HEADS = 3
HD = 64
PAD = 128
MARKS = 72
NEAR = 40
TILES = NEAR + 2
SPAN = 384
LOW = 92
TOP = 311
BF = jnp.bfloat16
F32 = jnp.float32
I32 = jnp.int32
FEED_PARTS = 3
GELU_C = float(np.sqrt(2.0 / np.pi))


def dot(left, right, dims=((1,), (0,))):
    return lax.dot_general(left, right, (dims, ((), ())), preferred_element_type=F32)


def bucket(delta):
    magnitude = jnp.abs(delta)
    coarse = 8 + sum((magnitude >= limit).astype(I32) for limit in THRESHOLDS)
    return jnp.where(magnitude < 8, magnitude, coarse) + 16 * (delta > 0).astype(I32)


def params(mib):
    return pltpu.CompilerParams(vmem_limit_bytes=mib * 2**20)


def cost(microseconds):
    return pl.CostEstimate(flops=int(1.15e9 * microseconds), bytes_accessed=1, transcendentals=0)


def shape(dims, dtype):
    return jax.ShapeDtypeStruct(dims, dtype)


def whole(dims):
    return pl.BlockSpec(dims, lambda *a: (0,) * len(dims))


def hidden_rows(inputs, pages, feats):
    return inputs.astype(F32) + dot(pages.astype(F32).astype(BF), feats, ((0,), (0,)))


def unit_rows(field):
    factor = lax.rsqrt(jnp.mean(field * field, axis=-1, keepdims=True) + EPS)
    return field * factor, factor


def project_kernel(ids, x_ref, page_ref, feat_ref, gain_ref, wq_ref, wk_ref, wv_ref, n_ref, q_ref, k_ref, v_ref):
    step = pl.program_id(0)
    rows = x_ref.shape[0]
    unit, _ = unit_rows(hidden_rows(x_ref[...], page_ref[...], feat_ref[...]))
    normed = (unit * gain_ref[...].astype(F32)).astype(BF)
    n_ref[...] = normed
    lane = lax.broadcasted_iota(I32, (rows, PAD), 1)
    row = lax.broadcasted_iota(I32, (rows, PAD), 0) + step * rows
    masked = jnp.where((lane == HD) & (row >= ids[8]), -1e30, 0.0)
    block = lane - MARKS
    far_left = (block >= 0) & (block < 8) & (row < 128 * block - 96)
    far_right = (block >= 8) & (block < 16) & (row >= 128 * (block - 8) + 224)
    masked = jnp.where(far_left | far_right, 1.0, masked)
    query_extra = jnp.where(lane == HD, 1.0, 0.0)
    value_extra = jnp.where((lane == HD) | (lane == HD + 1), 1.0, 0.0)
    for out_ref, w_ref, extra, scale in (
        (q_ref, wq_ref, query_extra, 0.125),
        (k_ref, wk_ref, masked, None),
        (v_ref, wv_ref, value_extra, None),
    ):
        full = dot(normed, w_ref[...], ((1,), (1,)))
        if scale is not None:
            full = full * scale
        pair = full[:, :PAD]
        last = jnp.concatenate([full[:, PAD:], jnp.zeros((rows, PAD - HD), F32)], axis=1)
        heads = (pair, pltpu.roll(pair, HD, 1), last)
        for head in range(HEADS):
            out_ref[:, head * PAD : (head + 1) * PAD] = jnp.where(lane < HD, heads[head], extra).astype(BF)


def project(ids, inputs, onehot, feats, gain, w_query, w_key, w_value):
    seq, width = inputs.shape
    rows = 256
    columns = w_query.shape[0]
    wide = HEADS * PAD
    block = lambda cols: pl.BlockSpec((rows, cols), lambda i, s: (i, 0))
    lanes = lambda n: pl.BlockSpec((n, rows), lambda i, s: (0, i))
    return pl.pallas_call(
        project_kernel,
        grid_spec=pltpu.PrefetchScalarGridSpec(
            num_scalar_prefetch=1,
            grid=(seq // rows,),
            in_specs=[block(width), lanes(onehot.shape[0]), whole(feats.shape), whole(gain.shape)]
            + [whole((columns, width))] * 3,
            out_specs=[block(width), block(wide), block(wide), block(wide)],
        ),
        out_shape=[shape((seq, width), BF)] + [shape((seq, wide), BF)] * 3,
        compiler_params=params(16),
        cost_estimate=cost(7),
        name="project",
    )(ids, inputs, onehot, feats, gain, w_query, w_key, w_value)


def place(delta):
    magnitude = jnp.abs(delta)
    coarse = jnp.minimum(25 - lax.clz(delta * delta), 7)
    exact = magnitude < 8
    return jnp.where(exact, magnitude, coarse), exact, delta > 0


def look(table_ref, row, where):
    index, exact, after = where
    found = [jnp.take_along_axis(table_ref[row, part], index, axis=0) for part in range(4)]
    return jnp.where(after, jnp.where(exact, found[2], found[3]), jnp.where(exact, found[0], found[1]))


def tile_delta(tile):
    lane = lax.broadcasted_iota(I32, (8, 128), 1)
    sub = lax.broadcasted_iota(I32, (8, 128), 0)
    delta = 8 * (tile - 13) + sub - lane
    if tile == 0:
        delta = jnp.full_like(delta, -1000)
    if tile == TILES - 1:
        delta = jnp.full_like(delta, 1000)
    return delta


def attend_kernel(*refs, first, width, chunk):
    ids, q_ref, k_ref, v_ref, hor_ref, ver_ref = refs[:6]
    if first:
        hor_all, ver_all, rel_table, hor_table, ver_table, e_ref, att0, att1, inv_ref, out_ref = refs[6:16]
        rel_ref, t8_ref, hor_col, ver_col, s_ref = refs[16:]
    else:
        rel_ref, t8_ref, hor_col, ver_col, e_ref, att0, att1, inv_ref, out_ref, s_ref = refs[6:]
    seq = k_ref.shape[0]
    lanes = width // 128
    step = pl.program_id(0)

    if first:

        @pl.when(step == 0)
        def _():
            for all_ref, col_ref in ((hor_all, hor_col), (ver_all, ver_col)):
                for b in range(seq // 128):
                    cols = slice(128 * b, 128 * b + 128)
                    spread = jnp.broadcast_to(all_ref[:, cols].astype(F32), (128, 128))
                    col_ref[cols, :] = spread.T.astype(I32)
            lane = lax.broadcasted_iota(I32, (8, 32), 1)
            sub = lax.broadcasted_iota(I32, (8, 32), 0)
            for axis, table_ref in enumerate((rel_table, hor_table, ver_table)):
                table = table_ref[...].astype(F32)
                for head in range(HEADS):
                    row = jnp.broadcast_to(table[head : head + 1], (8, 32))
                    for part in range(4):
                        entries = jnp.sum(jnp.where(lane == sub + 8 * part, row, 0.0), axis=1, keepdims=True)
                        t8_ref[axis * HEADS + head, part] = jnp.broadcast_to(entries, (8, 128))
            for tile in range(TILES):
                where = place(tile_delta(tile))
                for head in range(HEADS):
                    rel_ref[head, tile] = look(t8_ref, head, where)

    queries = q_ref[...]
    for head in range(HEADS):
        cols = slice(head * PAD, (head + 1) * PAD)
        s_ref[head] = dot(k_ref[:, cols], queries[:, cols], ((1,), (1,)))
    hor = [jnp.broadcast_to(hor_ref[:, 128 * l : 128 * l + 128], (8, 128)) for l in range(lanes)]
    ver = [jnp.broadcast_to(ver_ref[:, 128 * l : 128 * l + 128], (8, 128)) for l in range(lanes)]
    block = ids[(0 if first else 2) + step] * lanes

    def add_bias(c, tops):
        tops = list(tops)
        base = pl.multiple_of(c * chunk, chunk)
        for g in range(chunk // 8):
            rows = pl.ds(pl.multiple_of(base + 8 * g, 8), 8)
            hor_keys, ver_keys = hor_col[rows, :], ver_col[rows, :]
            for l in range(lanes):
                cols = pl.ds(128 * l, 128)
                hor_at, ver_at = place(hor_keys - hor[l]), place(ver_keys - ver[l])
                tile = jnp.clip(c * (chunk // 8) + g - 16 * (block + l) + 13, 0, TILES - 1)
                for head in range(HEADS):
                    s = s_ref[head, rows, cols] + rel_ref[head, tile]
                    s = s + (look(t8_ref, HEADS + head, hor_at) + look(t8_ref, 2 * HEADS + head, ver_at))
                    s_ref[head, rows, cols] = s
                    tops[head * lanes + l] = jnp.maximum(tops[head * lanes + l], s)
        return tuple(tops)

    tops = lax.fori_loop(
        0, seq // chunk, add_bias, tuple(jnp.full((8, 128), -1e30, F32) for _ in range(HEADS * lanes))
    )
    peaks = [jnp.broadcast_to(jnp.max(top, axis=0, keepdims=True), (16, 128)) for top in tops]

    def exps(c, carry):
        for g in range(4):
            rows = pl.ds(pl.multiple_of(c * 64 + 16 * g, 16), 16)
            for l in range(lanes):
                cols = pl.ds(128 * l, 128)
                for head in range(HEADS):
                    e_ref[head, rows, cols] = jnp.exp(s_ref[head, rows, cols] - peaks[head * lanes + l]).astype(BF)
        return carry

    lax.fori_loop(0, seq // 64, exps, 0)
    for head in range(HEADS):
        total = dot(v_ref[:, head * PAD : (head + 1) * PAD], e_ref[head], ((0,), (0,)))
        inverse = 1.0 / total[HD : HD + 1, :]
        inv_ref[head : head + 1, :] = inverse
        out_ref[head * HD : (head + 1) * HD, :] = total[:HD] * inverse

    for k, att_ref in enumerate((att0, att1)):

        @pl.when(step == k)
        def _(att_ref=att_ref):
            att_ref[...] = out_ref[...].astype(BF)


def attend(ids, queries, keys, values, hor, ver, tables, lookups):
    seq, wide = queries.shape
    width = seq // 4
    first = lookups is None
    base = 0 if first else 2
    columns = HEADS * HD
    at = pl.BlockSpec((1, width), lambda i, s: (0, s[base + i]))
    made = [
        shape((HEADS, TILES, 8, 128), F32), shape((3 * HEADS, 4, 8, 128), F32), shape((seq, 128), I32), shape((seq, 128), I32)
    ]
    extra = (hor, ver, *tables) if first else tuple(lookups)
    outs = [
        (shape((HEADS, seq, 2 * width), BF), pl.BlockSpec((HEADS, seq, width), lambda i, s: (0, 0, i))),
        (shape((columns, width), BF), whole((columns, width))),
        (shape((columns, width), BF), whole((columns, width))),
        (shape((HEADS, 2 * width), F32), pl.BlockSpec((HEADS, width), lambda i, s: (0, i))),
        (shape((columns, 2 * width), F32), pl.BlockSpec((columns, width), lambda i, s: (0, i))),
    ]
    if first:
        outs += [(m, whole(m.shape)) for m in made]
    found = pl.pallas_call(
        functools.partial(attend_kernel, first=first, width=width, chunk=32),
        grid_spec=pltpu.PrefetchScalarGridSpec(
            num_scalar_prefetch=1,
            grid=(2,),
            in_specs=[
                pl.BlockSpec((width, wide), lambda i, s: (s[base + i], 0)),
                whole(keys.shape),
                whole(values.shape),
                at,
                at,
            ]
            + [whole(a.shape) for a in extra],
            out_specs=[spec for _, spec in outs],
            scratch_shapes=[pltpu.VMEM((HEADS, seq, width), F32)],
        ),
        out_shape=[o for o, _ in outs],
        compiler_params=params(18),
        cost_estimate=cost(14),
        name="attend_first" if first else "attend_last",
    )(ids, queries, keys, values, hor, ver, *extra)
    return found[:5], found[5:]


def feed_kernel(
    ids, x_ref, page_ref, feat_ref, gain_ref, cot_ref, a0, a1, a2, a3, o0, o1, o2, o3, u0, u1, d0, d1,
    keep_ref, send_ref, mixed_ref, grad_ref, ffn_ref, grad_sum, ffn_sum,
):
    step = pl.program_id(0)
    half = pl.num_programs(0) // 2
    chunk = u0.shape[1]

    @pl.when(step == 0)
    def _():
        mixed = hidden_rows(x_ref[...], page_ref[...], feat_ref[...])
        for a_ref, o_ref in ((a0, o0), (a1, o1), (a2, o2), (a3, o3)):
            mixed = mixed + dot(a_ref[...], o_ref[...], ((0,), (0,)))
        mixed_ref[...] = mixed
        unit, _ = unit_rows(mixed)
        send_ref[2] = (unit * gain_ref[...].astype(F32)).astype(BF)
        grad_sum[...] = jnp.zeros_like(grad_sum)
        ffn_sum[...] = jnp.zeros_like(ffn_sum)

    def part(u_ref, d_ref, goal, at):
        upward = dot(send_ref[2], u_ref[...])
        square = upward * upward
        tanh = jnp.tanh(GELU_C * upward * (1.0 + 0.044715 * square))
        lifted = 0.5 * (1.0 + tanh)
        activated = (upward * lifted).astype(BF)
        slope = lifted + 0.5 * upward * (1.0 - tanh * tanh) * (GELU_C * (1.0 + 3 * 0.044715 * square))
        grad_up = (dot(cot_ref[...], d_ref[...], ((1,), (1,))) * slope).astype(BF)
        cols = pl.ds(pl.multiple_of(at * chunk, 128), chunk)
        goal[0, :, cols] = activated
        goal[1, :, cols] = grad_up
        ffn_sum[...] += dot(activated, d_ref[...])
        grad_sum[...] += dot(grad_up, u_ref[...], ((1,), (1,)))

    @pl.when(step < half)
    def _():
        part(u0, d0, keep_ref, step)

    @pl.when(step >= half)
    def _():
        part(u1, d1, send_ref, step - half)

    @pl.when(step == 2 * half - 1)
    def _():
        grad_ref[...] = grad_sum[...].astype(grad_ref.dtype)
        ffn_ref[...] = ffn_sum[...].astype(ffn_ref.dtype)


def feed(ids, own, inputs, onehot, feats, gain, cotangent, attended, w_outputs, ups, downs):
    seq, width = inputs.shape
    rows = seq // 4
    units = ups[0].shape[1]
    half = FEED_PARTS
    chunk = units // half
    slot = 0 if own else 2
    quarter = lambda cols: pl.BlockSpec((rows, cols), lambda i, s: (s[slot], 0))
    pages = pl.BlockSpec((onehot.shape[0], rows), lambda i, s: (0, s[slot]))
    columns = HEADS * HD
    low = lambda i: jnp.minimum(i, half - 1)
    high = lambda i: jnp.maximum(i - half, 0)
    kept = F32 if own else BF
    outs = [
        shape((2, rows, units), BF), shape((3, rows, width), BF), shape((rows, width), F32),
        shape((rows, width), kept), shape((rows, width), kept),
    ]
    return pl.pallas_call(
        feed_kernel,
        grid_spec=pltpu.PrefetchScalarGridSpec(
            num_scalar_prefetch=1,
            grid=(2 * half,),
            in_specs=[quarter(width), pages, whole(feats.shape), whole(gain.shape), quarter(width)]
            + [whole((columns, rows))] * 4
            + [whole((columns, width))] * 4
            + [
                pl.BlockSpec((width, chunk), lambda i, s: (0, low(i))),
                pl.BlockSpec((width, chunk), lambda i, s: (0, high(i))),
                pl.BlockSpec((chunk, width), lambda i, s: (low(i), 0)),
                pl.BlockSpec((chunk, width), lambda i, s: (high(i), 0)),
            ],
            out_specs=[whole(o.shape) for o in outs],
            scratch_shapes=[pltpu.VMEM((rows, width), F32), pltpu.VMEM((rows, width), F32)],
        ),
        out_shape=outs,
        compiler_params=params(20),
        cost_estimate=cost(20 if own else 10),
        name="feed_own" if own else "feed_other",
    )(ids, inputs, onehot, feats, gain, cotangent, *attended, *w_outputs, *ups, *downs)


def mid_kernel(
    ids, mine_ref, sent_ref, mixed_ref, gain_ref, cot_ref, o0, o1, o2, o3,
    grad_ref, own_ref, core_ref, chip_ref, far_ref, part_ref,
):
    grad_normed = mine_ref[...] + sent_ref[...].astype(F32)
    unit, factor = unit_rows(mixed_ref[...])
    scaled = grad_normed * gain_ref[...].astype(F32)
    grad = factor * (scaled - unit * jnp.mean(scaled * unit, axis=-1, keepdims=True))
    grad = cot_ref[...].astype(F32) + grad
    grad_ref[...] = grad
    low = grad.astype(BF)
    rows = low.shape[0]
    core_ref[:rows] = low
    chip_ref[:rows] = low
    part_ref[...] = jnp.sum(grad_normed * unit, axis=0, keepdims=True)
    for o_ref, goal, at in ((o0, own_ref, 0), (o1, core_ref, rows), (o2, chip_ref, rows), (o3, far_ref, 0)):
        found = dot(o_ref[...], low, ((1,), (1,))).astype(BF)
        for head in range(HEADS):
            goal[at : at + HD, head * rows : (head + 1) * rows] = found[head * HD : (head + 1) * HD]


def mid(ids, mine, sent, mixed, gain, cotangent, w_outputs):
    rows, width = mine.shape
    columns = HEADS * HD
    full = whole((rows, width))
    outs = [
        shape((rows, width), F32), shape((HD, width), BF), shape((rows + HD, width), BF), shape((rows + HD, width), BF),
        shape((HD, width), BF), shape((1, width), F32),
    ]
    return pl.pallas_call(
        mid_kernel,
        grid_spec=pltpu.PrefetchScalarGridSpec(
            num_scalar_prefetch=1,
            grid=(1,),
            in_specs=[full, full, full, whole(gain.shape), pl.BlockSpec((rows, width), lambda i, s: (s[0], 0))]
            + [whole((columns, width))] * 4,
            out_specs=[whole(o.shape) for o in outs],
        ),
        out_shape=outs,
        compiler_params=params(24),
        cost_estimate=cost(2),
        name="mid",
    )(ids, mine, sent, mixed, gain, cotangent, *w_outputs)


def back_kernel(*refs, first):
    ids, e_ref, qa_ref, qb_ref, inv_ref, o_ref, k_ref, v_ref, ga_ref, gb_ref = refs[:10]
    refs = refs[10:]
    if first:
        ds_ref, dqa_ref, dqb_ref, key_ref, value_ref, near_ref, far_ref, x_ref = refs
    else:
        key_in, value_in, near_in, far_in, dqa_in, dqb_in = refs[:6]
        ds_ref, all_ref, near_ref, far_ref, x_ref = refs[6:]
    head = pl.program_id(0)
    seq = k_ref.shape[0]
    width = qa_ref.shape[0]
    both = 2 * width
    lanes = width // 128
    base = 0 if first else 2

    sub = lax.broadcasted_iota(I32, (HD, both), 0)
    head_sub = lax.broadcasted_iota(I32, (8, both), 0)
    inverse = jnp.sum(jnp.where(head_sub[:HEADS] == head, inv_ref[...], 0.0), axis=0, keepdims=True)
    grad = jnp.concatenate([ga_ref[...], gb_ref[...]], axis=1).astype(F32)
    grad = (grad * inverse).astype(BF).astype(F32)
    inner = jnp.sum(grad * o_ref[...], axis=0, keepdims=True)
    high = inner.astype(BF).astype(F32)
    extra = jnp.where(sub == 0, -high, jnp.where(sub == 1, high - inner, 0.0))
    right = jnp.concatenate([grad, extra], axis=0).astype(BF)
    x_ref[...] = dot(v_ref[...], right)
    value = dot(e_ref[0], right, ((1,), (1,)))

    def grad_scores(c, carry):
        rows = pl.ds(pl.multiple_of(c * 64, 64), 64)
        ds_ref[0, rows, :] = (e_ref[0, rows, :].astype(F32) * x_ref[rows, :]).astype(BF)
        return carry

    lax.fori_loop(0, seq // 64, grad_scores, 0)
    grad = ds_ref[0]
    key = dot(grad, jnp.concatenate([qa_ref[...], qb_ref[...]], axis=0))
    query = dot(k_ref[...], grad, ((0,), (0,)))
    query_a = (query[:HD, :width] * 0.125).astype(BF)
    query_b = (query[:HD, width:] * 0.125).astype(BF)

    blocks = [ids[base + l // lanes] * lanes + l % lanes for l in range(2 * lanes)]
    for g in range(NEAR // 2):
        total = None if first else near_in[0, 16 * g : 16 * g + 16]
        for l, block in enumerate(blocks):
            start = 128 * block - 96 + 16 * g
            inside = (start >= 0) & (start < seq)
            rows = pl.ds(pl.multiple_of(jnp.clip(start, 0, seq - 16), 16), 16)
            found = ds_ref[0, rows, 128 * l : 128 * l + 128].astype(F32)
            found = jnp.where(inside, found, 0.0)
            total = found if total is None else total + found
        near_ref[0, 16 * g : 16 * g + 16] = total
    spot = lax.broadcasted_iota(I32, (8, 128), 0)
    for side in range(2):
        total = None if first else far_in[0, 8 * side : 8 * side + 8]
        for l, block in enumerate(blocks):
            marks = query[MARKS + 8 * side : MARKS + 8 * side + 8, 128 * l : 128 * l + 128]
            marks = jnp.where(spot == block, marks, 0.0)
            total = marks if total is None else total + marks
        far_ref[0, 8 * side : 8 * side + 8] = total

    if first:
        key_ref[...] = key
        value_ref[...] = value
        dqa_ref[...] = query_a
        dqb_ref[...] = query_b
    else:
        for k, found in enumerate((dqa_in[...], dqb_in[...], query_a, query_b)):
            all_ref[k, 0] = found
        for part, acc in ((1, key_in[...] + key), (2, value_in[...] + value)):
            turned = acc.T[:HD].astype(BF)
            for k in range(4):
                for q in range(4):

                    @pl.when(ids[k] == q)
                    def _(k=k, q=q, part=part, turned=turned):
                        all_ref[k, part] = turned[:, q * width : (q + 1) * width]


def back(ids, e, queries, inverse, out, keys, values, grad_a, grad_b, carried):
    seq, wide = queries.shape
    width = seq // 4
    first = carried is None
    base = 0 if first else 2
    columns = HEADS * HD
    head_cols = pl.BlockSpec((seq, PAD), lambda h, s: (0, h))
    grad_rows = pl.BlockSpec((HD, width), lambda h, s: (h, 0))
    sent = lambda at: pl.BlockSpec((HD, width), lambda h, s: (at, h))
    starts = (0, width // HD) if first else (width // HD, 0)
    near = pl.BlockSpec((1, 8 * NEAR, 128), lambda h, s: (h, 0, 0))
    far = pl.BlockSpec((1, 16, 128), lambda h, s: (h, 0, 0))
    queried = [(shape((columns, width), BF), grad_rows)] * 2
    sums = [(shape((seq, wide), F32), head_cols)] * 2
    rel = [(shape((HEADS, 8 * NEAR, 128), F32), near), (shape((HEADS, 16, 128), F32), far)]
    outs = [(shape((HEADS, seq, 2 * width), BF), pl.BlockSpec((1, seq, 2 * width), lambda h, s: (h, 0, 0)))]
    if first:
        outs += queried + sums
    else:
        outs += [(shape((4, 3, columns, width), BF), pl.BlockSpec((4, 3, HD, width), lambda h, s: (0, 0, h, 0)))]
    outs += rel
    part = lambda q: pl.BlockSpec((width, PAD), lambda h, s: (s[base + q], h))
    specs = [
        pl.BlockSpec((1, seq, 2 * width), lambda h, s: (h, 0, 0)),
        part(0),
        part(1),
        whole(inverse.shape),
        pl.BlockSpec((HD, 2 * width), lambda h, s: (h, 0)),
    ]
    specs += [head_cols, head_cols, sent(starts[0]), sent(starts[1])]
    if not first:
        specs += [spec for _, spec in sums + rel + queried]
    return pl.pallas_call(
        functools.partial(back_kernel, first=first),
        grid_spec=pltpu.PrefetchScalarGridSpec(
            num_scalar_prefetch=1,
            grid=(HEADS,),
            in_specs=specs,
            out_specs=[spec for _, spec in outs],
            scratch_shapes=[pltpu.VMEM((seq, 2 * width), F32)],
        ),
        out_shape=[o for o, _ in outs],
        compiler_params=params(20),
        cost_estimate=cost(10 if first else 0.1),
        name="back_first" if first else "back_last",
    )(ids, e, queries, queries, inverse, out, keys, values, grad_a, grad_b, *(() if first else carried))


def tables_kernel(ids, s_ref, keys_ref, qa_ref, qb_ref, *refs):
    diagonals = refs[:-3]
    out_ref, e_ref, left_ref = refs[-3:]
    head = pl.program_id(0)
    places, seq = e_ref.shape
    width = s_ref.shape[2]
    groups = places // 128

    @pl.when(head == 0)
    def _():
        spot = lax.broadcasted_iota(I32, (places, seq), 0)
        e_ref[...] = jnp.where(spot == keys_ref[...], 1.0, 0.0).astype(BF)

    moved = dot(e_ref[...], s_ref[0]).astype(BF)
    rows = pl.ds(pl.multiple_of(head * 128, 128), 128)
    for b in range(groups):
        left_ref[rows, b * width : (b + 1) * width] = moved[128 * b : 128 * b + 128]

    def to_buckets(sums, delta):
        spot = lax.broadcasted_iota(I32, (32, sums.shape[1]), 0)
        return jnp.sum(jnp.where(bucket(delta) == spot, sums, 0.0), axis=1, keepdims=True)

    @pl.when(head == HEADS - 1)
    def _():
        query = jnp.concatenate([qa_ref[...], qb_ref[...]], axis=1)
        column = lax.broadcasted_iota(I32, (SPAN, width), 0)
        right = [
            jnp.where(column == jnp.clip(128 * b + TOP - LOW - query, 0, TOP), 1.0, 0.0).astype(BF) for b in range(groups)
        ]
        found = dot(left_ref[...], jnp.concatenate(right, axis=1), ((1,), (1,)))
        lane = lax.broadcasted_iota(I32, (1, 512), 1)
        columns = []
        for h in range(HEADS):
            grid = jnp.concatenate([found[h * 128 : h * 128 + 128, :], jnp.zeros((128, 512 - SPAN), F32)], axis=1)
            grid = pltpu.roll(grid, 0, 1, stride=1, stride_axis=0)
            columns.append(to_buckets(jnp.sum(grid, axis=0, keepdims=True), lane + LOW - TOP))
        if diagonals:
            near_ref, far_ref = diagonals
            flip = 7 - lax.broadcasted_iota(I32, (8, 128), 0)
            spot = lax.broadcasted_iota(I32, (32, 1), 0)
            for h in range(HEADS):
                near = [jnp.take_along_axis(near_ref[h, 8 * t : 8 * t + 8], flip, axis=0) for t in reversed(range(NEAR))]
                grid = jnp.concatenate(near, axis=0)
                grid = jnp.concatenate([grid, jnp.zeros((8 * NEAR, 384), F32)], axis=1)
                grid = pltpu.roll(grid, 0, 1, stride=1, stride_axis=0)
                found = to_buckets(jnp.sum(grid, axis=0, keepdims=True), 8 * NEAR - 1 - 8 * 12 - lane)
                left = jnp.sum(jnp.sum(far_ref[h, :8], axis=0, keepdims=True), axis=1, keepdims=True)
                right = jnp.sum(jnp.sum(far_ref[h, 8:], axis=0, keepdims=True), axis=1, keepdims=True)
                columns.append(found + jnp.where(spot == 15, left, 0.0) + jnp.where(spot == 31, right, 0.0))
        spread = lax.broadcasted_iota(I32, (32, 128), 1)
        total = sum(jnp.where(spread == at, column, 0.0) for at, column in enumerate(columns))
        out_ref[...] = total.T[:8]


def table_grads(ids, first, scores, positions, sums):
    seq = positions.shape[1]
    width = seq // 4
    places = 1024
    base = 0 if first else 2
    quarter = lambda k: pl.BlockSpec((1, width), lambda h, s: (0, s[base + k]))
    return pl.pallas_call(
        tables_kernel,
        grid_spec=pltpu.PrefetchScalarGridSpec(
            num_scalar_prefetch=1,
            grid=(HEADS,),
            in_specs=[
                pl.BlockSpec((1,) + scores.shape[1:], lambda h, s: (h, 0, 0)), whole((1, seq)), quarter(0), quarter(1),
            ]
            + [whole(a.shape) for a in sums],
            out_specs=whole((8, 32)),
            scratch_shapes=[
                pltpu.VMEM((places, seq), BF),
                pltpu.VMEM((HEADS * 128, places // 128 * 2 * width), BF),
            ],
        ),
        out_shape=shape((8, 32), F32),
        compiler_params=params(24),
        cost_estimate=cost(10 if sums else 0.01),
        name="table_grads",
    )(ids, scores, *[positions] * 3, *sums)


def terms_of(grads, weights):
    total = None
    for part, w_ref in enumerate(weights):
        found = dot(grads[part], w_ref[...], ((0,), (0,)))
        total = found if total is None else total + found
    return total


def terms_send_kernel(w0, w1, w2, grads_ref, out_ref):
    out_ref[0] = terms_of(grads_ref[0], (w0, w1, w2)).astype(BF)


def terms_keep_kernel(w0, w1, w2, grads_ref, got_ref, own_ref, other_ref):
    total = terms_of(grads_ref[0], (w0, w1, w2)) + got_ref[0].astype(F32)

    @pl.when(pl.program_id(0) == 0)
    def _():
        other_ref[...] = total.astype(BF)

    @pl.when(pl.program_id(0) == 1)
    def _():
        own_ref[...] = total


def terms_send(weights, grads):
    columns, width = weights[0].shape
    rows = grads.shape[3]
    return pl.pallas_call(
        terms_send_kernel,
        grid=(2,),
        in_specs=[whole(weights[0].shape)] * 3 + [pl.BlockSpec((1, 3, columns, rows), lambda i: (2 * i + 1, 0, 0, 0))],
        out_specs=pl.BlockSpec((1, rows, width), lambda i: (i, 0, 0)),
        out_shape=shape((2, rows, width), BF),
        compiler_params=params(16),
        cost_estimate=cost(0.1),
        name="terms_send",
    )(*weights, grads)


def terms_keep(weights, grads, got):
    columns, width = weights[0].shape
    rows = grads.shape[3]
    return pl.pallas_call(
        terms_keep_kernel,
        grid=(2,),
        in_specs=[whole(weights[0].shape)] * 3
        + [
            pl.BlockSpec((1, 3, columns, rows), lambda i: (2 - 2 * i, 0, 0, 0)),
            pl.BlockSpec((1, rows, width), lambda i: (1 - i, 0, 0)),
        ],
        out_specs=[whole((rows, width))] * 2,
        out_shape=[shape((rows, width), F32), shape((rows, width), BF)],
        compiler_params=params(16),
        cost_estimate=cost(0.1),
        name="terms_keep",
    )(*weights, grads, got)


def last_kernel(
    ids, mine_ref, sent_ref, x_ref, page_ref, feat_ref, gain_ref, grad_ref, second_ref, mixed_ref, ffn_ref, got_ref,
    out_ref, part_ref,
):
    grad_normed = mine_ref[...] + sent_ref[...].astype(F32)
    unit, factor = unit_rows(hidden_rows(x_ref[...], page_ref[...], feat_ref[...]))
    scaled = grad_normed * gain_ref[...].astype(F32)
    grad = factor * (scaled - unit * jnp.mean(scaled * unit, axis=-1, keepdims=True))
    out_ref[0] = (mixed_ref[...] + ffn_ref[...] + got_ref[...].astype(F32)).astype(BF)
    out_ref[1] = (grad_ref[...] + grad).astype(BF)
    part_ref[0:1] = jnp.sum(grad_normed * unit, axis=0, keepdims=True)
    part_ref[1:2] = second_ref[...]


def last(ids, mine, sent, inputs, onehot, feats, gain, grad_mixed, second, *ffn):
    rows, width = mine.shape
    full = whole((rows, width))
    quarter = lambda cols: pl.BlockSpec((rows, cols), lambda i, s: (s[0], 0))
    pages = pl.BlockSpec((onehot.shape[0], rows), lambda i, s: (0, s[0]))
    return pl.pallas_call(
        last_kernel,
        grid_spec=pltpu.PrefetchScalarGridSpec(
            num_scalar_prefetch=1,
            grid=(1,),
            in_specs=[full, full, quarter(width), pages, whole(feats.shape), whole(gain.shape), full, whole((1, width))]
            + [full] * 3,
            out_specs=[whole((2, rows, width)), whole((2, width))],
        ),
        out_shape=[shape((2, rows, width), BF), shape((2, width), F32)],
        compiler_params=params(16),
        cost_estimate=cost(0.01),
        name="last",
    )(ids, mine, sent, inputs, onehot, feats, gain, grad_mixed, second, *ffn)


def pack_kernel(gains_ref, got_ref, hor_a, hor_b, ver_a, ver_b, out_ref):
    gains = gains_ref[...] + got_ref[...]
    parts = gains.shape[1] // 128
    for row in range(2):
        for part in range(parts):
            at = row * parts + part
            out_ref[at : at + 1, :] = gains[row : row + 1, part * 128 : part * 128 + 128]
    bins = hor_a.shape[1]
    out_ref[2 * parts :, :] = jnp.zeros((out_ref.shape[0] - 2 * parts, 128), F32)
    at = 2 * parts
    out_ref[at : at + HEADS, :bins] = hor_b[HEADS : 2 * HEADS]
    out_ref[at + HEADS : at + 2 * HEADS, :bins] = hor_a[:HEADS] + hor_b[:HEADS]
    out_ref[at + 2 * HEADS : at + 3 * HEADS, :bins] = ver_a[:HEADS] + ver_b[:HEADS]


def pack(gains, got, *sums):
    rows = gains.shape[1] // 128 * 2 + 3 * HEADS
    rows = -(-rows // 8) * 8
    return pl.pallas_call(
        pack_kernel,
        in_specs=[pl.BlockSpec(memory_space=pltpu.VMEM)] * 6,
        out_specs=pl.BlockSpec(memory_space=pltpu.VMEM),
        out_shape=shape((rows, 128), F32),
        compiler_params=params(16),
        cost_estimate=cost(0.1),
        name="pack",
    )(gains, got, *sums)


def unpack_kernel(a_ref, b_ref, rel_ref, hor_ref, ver_ref, gains_ref):
    total = a_ref[...] + b_ref[...]
    parts = gains_ref.shape[1] // 128
    for row in range(2):
        for part in range(parts):
            at = row * parts + part
            gains_ref[row : row + 1, part * 128 : part * 128 + 128] = total[at : at + 1]
    at, bins = 2 * parts, rel_ref.shape[1]
    for goal in (rel_ref, hor_ref, ver_ref):
        goal[...] = total[at : at + HEADS, :bins]
        at += HEADS


def unpack(one, two, bins, width):
    spec = pl.BlockSpec(memory_space=pltpu.VMEM)
    return pl.pallas_call(
        unpack_kernel,
        in_specs=[spec] * 2,
        out_specs=[spec] * 4,
        out_shape=[shape((HEADS, bins), F32)] * 3 + [shape((2, width), F32)],
        compiler_params=params(16),
        cost_estimate=cost(0.1),
        name="unpack",
    )(one, two)


def join_kernel(ids, b0, b1, b2, b3, out_ref):
    for k, b_ref in enumerate((b0, b1, b2, b3)):

        @pl.when(pl.program_id(0) == k)
        def _(b_ref=b_ref):
            out_ref[...] = b_ref[0].astype(out_ref.dtype)


def join_feat_kernel(ids, b0, b1, b2, b3, page_ref, out_ref, feat_ref, all_ref):
    step = pl.program_id(0)
    rows = b0.shape[1]
    for k, b_ref in enumerate((b0, b1, b2, b3)):

        @pl.when(step == k)
        def _(b_ref=b_ref, k=k):
            out_ref[...] = b_ref[0].astype(out_ref.dtype)
            all_ref[pl.ds(pl.multiple_of(ids[k] * rows, rows), rows), :] = b_ref[0]

    @pl.when(step == 3)
    def _():
        feat_ref[...] = dot(page_ref[...].astype(F32).astype(BF), all_ref[...])


def join(ids, blocks, slot, dtype, onehot=None):
    _, rows, width = blocks[0].shape
    specs = [pl.BlockSpec((1, rows, width), lambda i, s: (slot, 0, 0))] * 4
    outs, out_specs = [shape((4 * rows, width), dtype)], [pl.BlockSpec((rows, width), lambda i, s: (s[i], 0))]
    extra, scratch = (), []
    if onehot is not None:
        pages = onehot.shape[0]
        specs = specs + [whole(onehot.shape)]
        outs.append(shape((pages, width), F32))
        out_specs.append(whole((pages, width)))
        extra, scratch = (onehot,), [pltpu.VMEM((4 * rows, width), BF)]
    found = pl.pallas_call(
        join_kernel if onehot is None else join_feat_kernel,
        grid_spec=pltpu.PrefetchScalarGridSpec(
            num_scalar_prefetch=1, grid=(4,), in_specs=specs, out_specs=out_specs, scratch_shapes=scratch
        ),
        out_shape=outs,
        compiler_params=params(16),
        cost_estimate=cost(10),
        name="join_output" if onehot is None else "join_grads",
    )(ids, *blocks, *extra)
    return found[0] if onehot is None else found


def split_rows(ids, total, keep_ref, send_ref, parity):
    groups, size = keep_ref.shape[0], keep_ref.shape[1]
    for g in range(groups):
        mine = pl.multiple_of((2 * g + parity) * size, 8)
        theirs = pl.multiple_of((2 * g + 1 - parity) * size, 8)
        keep_ref[g] = total[pl.ds(mine, size), :].astype(keep_ref.dtype)
        send_ref[g] = total[pl.ds(theirs, size), :].astype(BF)


def feed_grad_kernel(ids, k0, n0, k1, n1, c0, c1, t0, t1, t2, t3, *outs, fast):
    units = k0.shape[2]
    rows = lambda refs: jnp.concatenate(refs, axis=0)
    total = outs[-1]
    normed = rows([n0[0], c0[2], n1[0], c1[2]])
    total[:, :units] = dot(normed, rows([k0[1], c0[1], k1[1], c1[1]]), ((0,), (0,)))
    cotangent = rows([r[...] for r in (t0, t1, t2, t3)])
    total[:, units:] = dot(cotangent, rows([k0[0], c0[0], k1[0], c1[0]]), ((0,), (0,)))
    if fast:
        split_rows(ids, total, outs[0], outs[1], ids[9])
    else:
        outs[0][...] = total[...]


def feed_grad(ids, own, other, got_own, got_other, cotangent, fast):
    _, rows, units = own[0].shape
    width = cotangent.shape[1]
    quarter = lambda k: pl.BlockSpec((rows, width), lambda i, s: (s[k], 0))
    normed = pl.BlockSpec((1, rows, width), lambda i, s: (2, 0, 0))
    if fast:
        outs = [shape((4, width // 8, 2 * units), F32), shape((4, width // 8, 2 * units), BF)]
    else:
        outs = [shape((width, 2 * units), F32)]
    return pl.pallas_call(
        functools.partial(feed_grad_kernel, fast=fast),
        grid_spec=pltpu.PrefetchScalarGridSpec(
            num_scalar_prefetch=1,
            grid=(1,),
            in_specs=[
                whole(own[0].shape), normed, whole(other[0].shape), normed, whole(got_own.shape), whole(got_other.shape),
            ]
            + [quarter(k) for k in range(4)],
            out_specs=[whole(o.shape) for o in outs],
            scratch_shapes=[pltpu.VMEM((width, 2 * units), F32)],
        ),
        out_shape=outs,
        compiler_params=params(32),
        cost_estimate=cost(7),
        name="feed_grad",
    )(ids, *own, *other, got_own, got_other, *[cotangent] * 4)


def head_grad_kernel(ids, n0, n1, n2, n3, grads_ref, l0, l1, l2, l3, a0, a1, a2, a3, *outs, fast):
    total, turned = outs[-2:]
    n = a0.shape[0]
    normed = jnp.concatenate([r[...] for r in (n0, n1, n2, n3)], axis=0)
    for part in range(3):
        left = jnp.concatenate([grads_ref[k, part] for k in range(4)], axis=1)
        total[part * n : (part + 1) * n, :] = dot(left, normed)
    low = jnp.concatenate([r[...] for r in (l0, l1, l2, l3)], axis=0)
    total[3 * n :, :] = dot(jnp.concatenate([r[...] for r in (a0, a1, a2, a3)], axis=1), low)
    turned[...] = total[...].T
    if fast:
        split_rows(ids, turned, outs[0], outs[1], ids[9])
    else:
        outs[0][...] = turned[...]


def head_grad(ids, normed, grads, lows, attended, fast):
    seq, width = normed.shape
    rows = seq // 4
    n = grads.shape[2]
    quarter = lambda k: pl.BlockSpec((rows, width), lambda i, s: (s[k], 0))
    specs = [quarter(k) for k in range(4)] + [whole(grads.shape)]
    specs += [whole((rows, width))] * 4 + [whole((n, rows))] * 4
    if fast:
        outs = [shape((4, width // 8, 4 * n), F32), shape((4, width // 8, 4 * n), BF)]
    else:
        outs = [shape((width, 4 * n), F32)]
    return pl.pallas_call(
        functools.partial(head_grad_kernel, fast=fast),
        grid_spec=pltpu.PrefetchScalarGridSpec(
            num_scalar_prefetch=1,
            grid=(1,),
            in_specs=specs,
            out_specs=[whole(o.shape) for o in outs],
            scratch_shapes=[pltpu.VMEM((4 * n, width), F32), pltpu.VMEM((width, 4 * n), F32)],
        ),
        out_shape=outs,
        compiler_params=params(32),
        cost_estimate=cost(0.1),
        name="head_grad",
    )(ids, *[normed] * 4, grads, *lows, *attended)


def pair_kernel(ids, keep_ref, got_ref, *outs):
    for k, o_ref in enumerate(outs):
        at = ids[4 + k]
        o_ref[...] = (keep_ref[at] + got_ref[at].astype(F32)).astype(o_ref.dtype)


def pair_sum(ids, keep, got):
    _, size, n = keep.shape
    return pl.pallas_call(
        pair_kernel,
        grid_spec=pltpu.PrefetchScalarGridSpec(
            num_scalar_prefetch=1,
            grid=(1,),
            in_specs=[whole(keep.shape), whole(got.shape)],
            out_specs=[whole((size, n))] * 4,
        ),
        out_shape=[shape((size, n), F32)] + [shape((size, n), BF)] * 3,
        compiler_params=params(20),
        cost_estimate=cost(0.01),
        name="pair_sum",
    )(ids, keep, got)


def feed_final_kernel(a0, a1, a2, a3, up_ref, down_ref):
    total = a0[...] + a1[...].astype(F32) + a2[...].astype(F32) + a3[...].astype(F32)
    units = up_ref.shape[1]
    up_ref[...] = total[:, :units]
    down_ref[...] = total[:, units:]


def head_final_kernel(a0, a1, a2, a3, q_ref, k_ref, v_ref, o_ref):
    total = a0[...] + a1[...].astype(F32) + a2[...].astype(F32) + a3[...].astype(F32)
    n = q_ref.shape[1]
    q_ref[...] = total[:, :n]
    k_ref[...] = total[:, n : 2 * n]
    v_ref[...] = total[:, 2 * n : 3 * n]
    o_ref[...] = total[:, 3 * n :].T


def final(kernel, arrays, done, outs):
    arrays = [after(arrays[0], done)] + arrays[1:]
    return pl.pallas_call(
        kernel,
        grid=(1,),
        in_specs=[whole(a.shape) for a in arrays],
        out_specs=[whole(o.shape) for o in outs],
        out_shape=outs,
        compiler_params=params(16),
        cost_estimate=cost(1),
        name=kernel.__name__[:-7],
    )(*arrays)


def swap(array, axis, size, bits):
    return lax.ppermute(array, axis, [(i, i ^ bits) for i in range(size)])


def after(array, *others):
    return lax.optimization_barrier((array, others))[0]


def local(
    inputs, page_feat, page_onehot, lengths, hor_pos, ver_pos, norm1_gain, w_query, w_key, w_value,
    rel_table, hor_table, ver_table, w_output, norm2_gain, w_up, w_down, cotangent, *, dp,
):
    seq, width = inputs.shape
    fast = dp == 8
    over = functools.partial(swap, axis="mp", size=4)
    m = lax.axis_index("mp").astype(I32)
    d = lax.axis_index("dp").astype(I32)
    k4 = jnp.arange(4, dtype=I32)
    spot = lambda who: (who & 1) * 2 + (who >> 1)
    ids = jnp.concatenate([
        spot(m ^ k4),
        (d >> 1) ^ k4,
        lengths[:1],
        (d & 1)[None],
    ])
    gain_one, gain_two = norm1_gain[None], norm2_gain[None]
    feats = page_feat[0]
    hor, ver = hor_pos[None], ver_pos[None]
    tables = (rel_table, hor_table, ver_table)
    pages = page_onehot.T
    weights = [w_query.T, w_key.T, w_value.T]

    wo_y, wo_core = over(w_output, bits=2), over(w_output, bits=1)
    normed1, queries, keys, values = project(ids, inputs, pages, feats, gain_one, *weights)
    w_outputs = [w_output, wo_core, wo_y, over(after(wo_y, normed1), bits=1)]
    ups = [w_up, over(after(w_up, normed1), bits=1)]
    downs = [w_down, over(after(w_down, normed1), bits=1)]

    (e_a, att0, att1, inverse_a, out_a), lookups = attend(ids, queries, keys, values, hor, ver, tables, None)
    from_y, from_yc, own1 = over(att0, bits=2), over(att1, bits=3), over(att1, bits=1)
    ver_late = after(ver, att0, w_outputs[3], ups[1], downs[1])
    (e_b, att2, att3, inverse_b, out_b), _ = attend(ids, queries, keys, values, hor, ver_late, tables, lookups)
    attended = [att0, att1, att2, att3]
    for_other = [att2, over(att3, bits=1), from_y, from_yc]
    for_own = [att0, own1, over(att2, bits=2), over(att3, bits=3)]

    fixed = (inputs, pages, feats, gain_two, cotangent)
    x_keep, x_send, _, x_grad, x_ffn = feed(ids, False, *fixed, for_other, w_outputs, ups, downs)
    sent_grad, x_got = over(x_grad, bits=2), over(x_send, bits=1)
    for_own[0] = after(att0, x_ffn)
    m_keep, m_send, mixed, m_grad, m_ffn = feed(ids, True, *fixed, for_own, w_outputs, ups, downs)
    m_grad = after(m_grad, x_got)
    grad_mixed, ga0, core_send, chip_send, far_send, gain_two_part = mid(
        ids, m_grad, sent_grad, mixed, gain_two, cotangent, w_outputs
    )
    m_got = over(after(m_send, ga0), bits=1)
    core_got, chip_got, far_got = over(core_send, bits=1), over(chip_send, bits=2), over(far_send, bits=3)

    around = functools.partial(swap, axis="dp", size=dp)
    feed_grads = feed_grad(ids, (m_keep, m_send), (x_keep, x_send), m_got, x_got, cotangent, fast)
    feed_got = around(feed_grads[1], bits=1) if fast else ids

    scores_a, dq0, dq1, key_sum, value_sum, near, far = back(
        ids, e_a, queries, inverse_a, out_a, keys, values, after(ga0, feed_grads[0], far_got), core_got, None
    )
    chip_got = after(chip_got, dq0)
    core_far, sent_ffn = over(chip_got, bits=1), over(after(x_ffn, dq0), bits=2)
    scores_b, grads, near, far = back(
        ids, e_b, queries, inverse_b, out_b, keys, values, chip_got, far_got,
        (key_sum, value_sum, near, far, dq0, dq1),
    )
    to_core = terms_send(weights, after(grads, core_far, sent_ffn))
    got_terms = over(to_core, bits=1)
    lows = [core_send, core_got, chip_got, core_far]
    head_grads = head_grad(ids, normed1, after(grads, to_core, feed_got), lows, attended, fast)
    head_got = around(head_grads[1], bits=1) if fast else ids
    own_terms, other_terms = terms_keep(weights, after(grads, head_grads[0]), got_terms)
    sent_terms = over(other_terms, bits=2)

    to_z = lambda parts: [parts[0]] + [around(part, bits=2 * k) for k, part in zip((1, 2, 3), parts[1:])]
    size = width // dp
    n = w_query.shape[1]
    units = w_up.shape[1]
    done = own_terms
    if fast:
        feed_parts = to_z(pair_sum(ids, after(feed_grads[0], done), feed_got))
        done = feed_parts[0]
    hor_sums = [table_grads(ids, True, scores_a, after(hor, done), ())]
    rows, gains = last(
        ids, after(own_terms, hor_sums[0]), sent_terms, inputs, pages, feats, gain_one, grad_mixed, gain_two_part,
        mixed, m_ffn, sent_ffn,
    )
    rows_y, rows_core = over(rows, bits=2), over(rows, bits=1)
    done = gains
    if fast:
        head_parts = list(pair_sum(ids, after(head_grads[0], done), head_got))
        done = head_parts[0]
    ver_sums = [table_grads(ids, True, scores_a, after(ver, done), ())]
    done = ver_sums[0]
    if fast:
        grad_up, grad_down = final(feed_final_kernel, feed_parts, done, [shape((size, units), F32)] * 2)
        done = grad_up
        head_parts = to_z([head_parts[0]] + [after(part, done) for part in head_parts[1:]])
    gains = after(gains, done) + over(gains, bits=1)
    got_gains = over(gains, bits=2)
    hor_sums.append(table_grads(ids, False, scores_b, after(hor, done, gains), (near, far)))
    rows_far = over(after(rows_y, hor_sums[1]), bits=1)
    ver_sums.append(table_grads(ids, False, scores_b, after(ver, hor_sums[1]), ()))
    small = pack(gains, got_gains, *hor_sums, *ver_sums)
    if fast:
        got = around(small, bits=1)
        grad_query, grad_key, grad_value, grad_output = final(
            head_final_kernel, head_parts, small, [shape((size, n), F32)] * 3 + [shape((n, size), F32)]
        )
        small = after(small, grad_query) + got
        got = around(small, bits=2)
    else:
        small, got = lax.psum(small, "dp"), jnp.zeros_like(small)
        scatter = lambda a: lax.psum_scatter(a[0], "dp", scatter_dimension=0, tiled=True)
        grad_feed, heads = scatter(feed_grads), scatter(head_grads)
        grad_up, grad_down = grad_feed[:, :units], grad_feed[:, units:]
        grad_query, grad_key, grad_value = heads[:, :n], heads[:, n : 2 * n], heads[:, 2 * n : 3 * n]
        grad_output = heads[:, 3 * n :].T
    quarters = [rows, rows_core, rows_y, rows_far]
    outputs = join(ids, [after(rows, small)] + quarters[1:], 0, BF)
    small = [after(small, outputs), got]
    if fast:
        small = small[0] + small[1]
        small = [small, around(small, bits=4)]
    grad_inputs, grad_feats = join(ids, [after(rows, small[0])] + quarters[1:], 1, F32, pages)
    small[0] = after(small[0], grad_feats)
    grad_rel, grad_hor, grad_ver, gain_sums = unpack(*small, rel_table.shape[1], width)
    gain_sums = lax.dynamic_slice(gain_sums, (0, d * size), (2, size))
    return (
        outputs, grad_inputs, grad_feats[None], gain_sums[0], grad_query, grad_key, grad_value,
        grad_rel, grad_hor, grad_ver, grad_output, gain_sums[1], grad_up, grad_down.T,
    )


def solution(mesh):
    return jax.shard_map(
        functools.partial(local, dp=mesh.shape["dp"]),
        mesh=mesh,
        in_specs=(
            P("dp", None),
            P("dp", None, None),
            P("dp", None),
            P("dp"),
            P("dp"),
            P("dp"),
            P(),
            P(None, "mp"),
            P(None, "mp"),
            P(None, "mp"),
            P("mp", None),
            P("mp", None),
            P("mp", None),
            P("mp", None),
            P(),
            P(None, "mp"),
            P("mp", None),
            P("dp", None),
        ),
        out_specs=(
            P("dp", None),
            P("dp", None),
            P("dp", None, None),
            P("dp"),
            P("dp", "mp"),
            P("dp", "mp"),
            P("dp", "mp"),
            P("mp", None),
            P("mp", None),
            P("mp", None),
            P("mp", "dp"),
            P("dp"),
            P("dp", "mp"),
            P("mp", "dp"),
        ),
        check_vma=False,
    )
```

time: 243 us -> 174 us (0.72)
  waiting for transfers between devices: 57.8 us -> 18.8 us
  local copies, waits for them, and re-layouts: 32.2 us -> 9.02 us
  starting transfers between devices: 36.4 us -> 33 us
    ppermute x52 -> x37, waiting for transfers between devices: 57.8 us -> 18.8 us  [swap(): return lax.ppermute(array, axis, [(i, i ^ bits) for i in range(size)])]
    unnamed x135 -> x48, local copies, waits for them, and re-layouts: 28.7 us -> 7.73 us
    pallas_call x2, Pallas kernels: 18.7 us -> 14.5 us  [feed(): pl.pallas_call(feed_kernel, grid_spec=pltpu.PrefetchScalarGridSpec(num_sc...]
    pallas_call x1 -> x4, Pallas kernels: 23.8 us -> 27.3 us  [table_grads(): pl.pallas_call(tables_kernel, grid_spec=pltpu.PrefetchScalarGridSpec(num_...]
    ppermute x52 -> x37, starting transfers between devices: 36.4 us -> 33 us  [swap(): return lax.ppermute(array, axis, [(i, i ^ bits) for i in range(size)])]
    pallas_call x7 -> x9, Pallas kernels: 32.1 us -> 32.6 us  [the longest x2 22.5 us: attend(): pl.pallas_call(functools.partial(attend_kernel, first=first, width=width,...]
  transfers between devices with their start and end apart: 52 -> 37, of which waited for: 12 -> 7; matrix products, arithmetic and copies ran while one was open for 2% -> 0% of each run, Pallas kernels for 39% -> 63%
where the time goes in v2:
time: 174 us; the launch traced here: 173 us
  Pallas kernels  111 us (64%)
  starting transfers between devices  33 us (19%)
  waiting for transfers between devices  18.8 us (11%)
  local copies, waits for them, and re-layouts  9.02 us (5%)
    ppermute x37, starting transfers between devices, swap(): return lax.ppermute(array, axis, [(i, i ^ bits) for i in range(size)])  33 us
    pallas_call x4, Pallas kernels, table_grads(): pl.pallas_call(tables_kernel, grid_spec=pltpu.PrefetchScalarGridSpec(num_...  27.3 us
    pallas_call x2, Pallas kernels, attend(): pl.pallas_call(functools.partial(attend_kernel, first=first, width=width,...  22.5 us
    ppermute x37, waiting for transfers between devices, swap(): return lax.ppermute(array, axis, [(i, i ^ bits) for i in range(size)])  18.8 us
    pallas_call x2, Pallas kernels, back(): pl.pallas_call(functools.partial(back_kernel, first=first), grid_spec=plt...  15.9 us
    pallas_call x2, Pallas kernels, feed(): pl.pallas_call(feed_kernel, grid_spec=pltpu.PrefetchScalarGridSpec(num_sc...  14.5 us
    pallas_call x2, Pallas kernels, join(): pl.pallas_call(join_kernel if onehot is None else join_feat_kernel, grid_...  8.04 us
    unnamed x48, local copies, waits for them, and re-layouts  7.73 us
  transfers between devices with their start and end apart: 37, of which 7 were waited for; matrix products, arithmetic and copies ran while one was open for 0% of the time, Pallas kernels for 63%

profile of v2, /device:TPU:0, one launch (start us, length us, event | category | flops | bytes accessed | tf_op | source)
XLA Modules:
  0.0 173.4 jit_solution(2198949467881881727)
XLA Ops:
  1.2 2.6 %collective-permute-start = (bf16[192,768]{1,0:T(8,128)(2,1)}, bf16[192,768]{1,0:T(8,128)(2,1)S(1)}, u32[]{:S(2)}, u32[]{:S(2)}) collective-permute-start(bf16[192,768]{1,0:T(8,128)(2,1)} %o0.5), channel_id=1, source_target_pairs={{0,2},{1,3},{2,0},{3,1},{4,6},{5,7},{6,4},{7,5},{8,10},{9,11},{10,... | collective-permute-start | bytes 884744 | tf_op jit(solution)/shard_map/ppermute | solution.py:956
  11.0 4.2 %project.1 = (bf16[1024,768]{1,0:T(8,128)(2,1)S(1)}, bf16[1024,384]{1,0:T(8,128)(2,1)S(1)}, bf16[1024,384]{1,0:T(8,128)(2,1)S(1)}, bf16[1024,384]{1,0:T(8,128)(2,1)S(1)}) custom-call(s32[10]{0:T(128)S(1)} %pad_add_fusion.ids.refs_0_, bf16[1024,768]{1,0:T(8,128)(2,1)S(1)} %copy-done, s32[8,1024]{1,0:T(8,128)S(1)} %bitcast.41, bf16[8,768]{1,0:T(8,128)(2,1)S(1)} %bitcast.46, ...), custom_call_target="tpu_custom_call" | custom-call | flops 8049999872 | bytes 1 | tf_op jit(solution)/shard_map/project/pallas_call | solution.py:102
  16.0 11.5 %attend_first.1 = (bf16[3,1024,512]{2,1,0:T(8,128)(2,1)S(1)}, bf16[192,256]{1,0:T(8,128)(2,1)S(1)}, bf16[192,256]{1,0:T(8,128)(2,1)S(1)}, f32[3,512]{1,0:T(4,128...) custom-call(s32[10]{0:T(128)S(1)} %pad_add_fusion.ids.refs_0_, ...), custom_call_target="tpu_custom_call" | custom-call | flops 16099999744 | bytes 1 | tf_op jit(solution)/shard_map/attend_first/pallas_call | solution.py:249
  27.6 1.9 %collective-permute-start.5 = (bf16[192,256]{1,0:T(8,128)(2,1)S(1)}, bf16[192,256]{1,0:T(8,128)(2,1)S(1)}, u32[]{:S(2)}, u32[]{:S(2)}) collective-permute-start(bf16[192,256]{1,0:T(8,128)(2,1)S(1)} %get-tuple-element.138.a0), channel_id=1, source_target_pairs={{0,2},{1,3},{2,0},{3,1},{4,6},{5,7},{6,4},{7,5},{8,10},{9,11},{10,... | collective-permute-start | bytes 294920 | tf_op jit(solution)/shard_map/ppermute | solution.py:956
  29.6 11.1 %attend_last.1 = (bf16[3,1024,512]{2,1,0:T(8,128)(2,1)S(1)}, bf16[192,256]{1,0:T(8,128)(2,1)S(1)}, bf16[192,256]{1,0:T(8,128)(2,1)S(1)}, f32[3,512]{1,0:T(4,128)S(1)}, f32[192,512]{1,0:T(8,128)S(1)}) custom-call(s32[10]{0:T(128)S(1)} %pad_add_fusion.ids.refs_0_, bf16[1024,384]{1,0:T(8,128)(2,1)S(1)} %get-tuple-element.118.refs_1_.refs_2_.refs_3_, ...), custom_call_target="tpu_custom_call" | custom-call | flops 16099999744 | bytes 1 | tf_op jit(solution)/shard_map/attend_last/pallas_call | solution.py:249
  41.4 1.7 collective-permute-start.9
  43.1 7.6 %feed_other.1 = (bf16[2,256,768]{2,1,0:T(8,128)(2,1)S(1)}, bf16[3,256,768]{2,1,0:T(8,128)(2,1)S(1)}, f32[256,768]{1,0:T(8,128)}, bf16[256,768]{1,0:T(8,128)(2,1)S(1)}, bf16[256,768]{1,0:T(8,128)(2,1)S(1)}) custom-call(s32[10]{0:T(128)S(1)} %pad_add_fusion.ids.refs_0_, bf16[1024,768]{1,0:T(8,128)(2,1)S(1)} %copy-done.1, s32[8,1024]{1,0:T(8,128)S(1)} %bitcast.42, ...), custom_call_target="tpu_custom_call" | custom-call | flops 11500000256 | bytes 1 | tf_op jit(solution)/shard_map/feed_other/pallas_call | solution.py:337
  51.1 6.9 %feed_own.1 = (bf16[2,256,768]{2,1,0:T(8,128)(2,1)S(1)}, bf16[3,256,768]{2,1,0:T(8,128)(2,1)S(1)}, f32[256,768]{1,0:T(8,128)S(1)}, f32[256,768]{1,0:T(8,128)S(1)}, f32[256,768]{1,0:T(8,128)S(1)}) custom-call(s32[10]{0:T(128)S(1)} %pad_add_fusion.ids.refs_0_, bf16[1024,768]{1,0:T(8,128)(2,1)S(1)} %copy-done.1, s32[8,1024]{1,0:T(8,128)S(1)} %bitcast.43, ...), custom_call_target="tpu_custom_call" | custom-call | flops 23000000512 | bytes 1 | tf_op jit(solution)/shard_map/feed_own/pallas_call | solution.py:337
  58.0 3.9 %collective-permute-done.12.sent_ref = bf16[256,768]{1,0:T(8,128)(2,1)S(1)} collective-permute-done((bf16[256,768]{1,0:T(8,128)(2,1)S(1)}, bf16[256,768]{1,0:T(8,128)(2,1)S(1)}, u32[]{:S(2)}, u32[]{:S(2)}) %collective-permute-start.12) | collective-permute-done | bytes 393248 | tf_op jit(solution)/shard_map/ppermute | solution.py:956
  61.9 1.6 mid.1
  64.0 1.7 %collective-permute-start.13 = (bf16[320,768]{1,0:T(8,128)(2,1)S(1)}, bf16[320,768]{1,0:T(8,128)(2,1)S(1)}, u32[]{:S(2)}, u32[]{:S(2)}) collective-permute-start(bf16[320,768]{1,0:T(8,128)(2,1)S(1)} %get-tuple-element.144), channel_id=1, source_target_pairs={{0,2},{1,3},{2,0},{3,1},{4,6},{5,7},{6,4},{7,5},{8,10},{9,11},{10,... | collective-permute-start | bytes 1474568 | tf_op jit(solution)/shard_map/ppermute | solution.py:956
  66.4 4.5 %feed_grad.1 = (f32[4,96,1536]{2,1,0:T(8,128)S(1)}, bf16[4,96,1536]{2,1,0:T(8,128)(2,1)}) custom-call(s32[10]{0:T(128)S(1)} %pad_add_fusion.ids.refs_0_, bf16[2,256,768]{2,1,0:T(8,128)(2,1)S(1)} %get-tuple-element.149.k0, bf16[3,256,768]{2,1,0:T(8,128)(2,1)S(1)} %get-tuple-element.152.n0, bf16[2,256,768]{2,1,0:T(8,128)(2,1)S(1)} %get-tuple-element.151.k1, ...), custom_call_target="tpu_custom_call" | custom-call | flops 8049999872 | bytes 1 | tf_op jit(solution)/shard_map/feed_grad/pallas_call | solution.py:840
  72.3 1.9 %copy-done.22 = bf16[3,1024,512]{2,1,0:T(8,128)(2,1)S(1)} copy-done((bf16[3,1024,512]{2,1,0:T(8,128)(2,1)S(1)}, bf16[3,1024,512]{2,1,0:T(8,128)(2,1)}, u32[]{:S(2)}) %copy-start.22) | copy-done | bytes 3145752
  74.2 8.0 %back_first.1 = (bf16[3,1024,512]{2,1,0:T(8,128)(2,1)S(1)}, bf16[192,256]{1,0:T(8,128)(2,1)S(1)}, bf16[192,256]{1,0:T(8,128)(2,1)S(1)}, f32[1024,384]{1,0:T(8,12...) custom-call(s32[10]{0:T(128)S(1)} %pad_add_fusion.ids.refs_0_, ...), custom_call_target="tpu_custom_call" | custom-call | flops 11500000256 | bytes 1 | tf_op jit(solution)/shard_map/back_first/pallas_call | solution.py:515
  82.8 8.0 %back_last.1 = (bf16[3,1024,512]{2,1,0:T(8,128)(2,1)S(1)}, bf16[4,3,192,256]{3,2,1,0:T(8,128)(2,1)S(1)}, f32[3,320,128]{2,1,0:T(8,128)S(1)}, f32[3,16,128]{2,1,0:T(8,128)S(1)}) custom-call(s32[10]{0:T(128)S(1)} %pad_add_fusion.ids.refs_0_, bf16[3,1024,512]{2,1,0:T(8,128)(2,1)S(1)} %get-tuple-element.131.refs_1_, ...), custom_call_target="tpu_custom_call" | custom-call | flops 115000000 | bytes 1 | tf_op jit(solution)/shard_map/back_last/pallas_call | solution.py:515
  90.8 3.0 %collective-permute-done.18.got_ref = bf16[256,768]{1,0:T(8,128)(2,1)S(1)} collective-permute-done((bf16[256,768]{1,0:T(8,128)(2,1)S(1)}, bf16[256,768]{1,0:T(8,128)(2,1)S(1)}, u32[]{:S(2)}, u32[]{:S(2)}) %collective-permute-start.18) | collective-permute-done | bytes 393248 | tf_op jit(solution)/shard_map/ppermute | solution.py:956
  95.0 4.1 %collective-permute-done.19.got_ref = bf16[4,96,1536]{2,1,0:T(8,128)(2,1)S(1)} collective-permute-done((bf16[4,96,1536]{2,1,0:T(8,128)(2,1)}, bf16[4,96,1536]{2,1,0:T(8,128)(2,1)S(1)}, u32[]{:S(2)}, u32[]{:S(2)}) %collective-permute-start.19) | collective-permute-done | bytes 1179680 | tf_op jit(solution)/shard_map/ppermute | solution.py:956
  99.1 2.2 %head_grad.1 = (f32[4,96,768]{2,1,0:T(8,128)S(1)}, bf16[4,96,768]{2,1,0:T(8,128)(2,1)S(1)}) custom-call(s32[10]{0:T(128)S(1)} %pad_add_fusion.ids.refs_0_, bf16[1024,768]{1,0:T(8,128)(2,1)S(1)} %get-tuple-element.122.n0.n1.n2.n3, bf16[1024,768]{1,0:T(8,128)(2,1)S(1)} %get-tuple-element.122.n0.n1.n2.n3, bf16[1024,768]{1,0:T(8,128)(2,1)S(1)} %get-tuple-element.122.n0.n1.n2.n3, ...), custom_call_target="tpu_custom_call" | custom-call | flops 115000000 | bytes 1 | tf_op jit(solution)/shard_map/head_grad/pallas_call | solution.py:886
  101.3 1.6 collective-permute-start.22
  105.3 1.7 collective-permute-start.23
  106.9 2.6 %collective-permute-start.24 = (bf16[96,1536]{1,0:T(8,128)(2,1)S(1)}, bf16[96,1536]{1,0:T(8,128)(2,1)S(1)}, u32[]{:S(2)}, u32[]{:S(2)}) collective-permute-start(bf16[96,1536]{1,0:T(8,128)(2,1)S(1)} %get-tuple-element.189), channel_id=1, source_target_pairs={{0,16},{4,20},{8,24},{12,28},{16,0},{20,4},{24,8},{28,12},{1,17},{... | collective-permute-start | bytes 884744 | tf_op jit(solution)/shard_map/ppermute | solution.py:956
  109.7 7.0 %table_grads.4.hor_a = f32[8,32]{1,0:T(8,128)S(1)} custom-call(s32[10]{0:T(128)S(1)} %pad_add_fusion.ids.refs_0_, bf16[3,1024,512]{2,1,0:T(8,128)(2,1)S(1)} %get-tuple-element.172.s_ref, s32[1,1024]{1,0:T(1,128)S(1)} %bitcast.35, s32[1,1024]{1,0:T(1,128)S(1)} %bitcast.36, s32[1,1024]{1,0:T(1,128)S(1)} %bitcast.37), custom_call_target="tpu_custom_call" | custom-call | flops 11500000 | bytes 1 | tf_op jit(solution)/shard_map/table_grads/pallas_call | solution.py:591
  116.7 2.4 %last.1 = (bf16[2,256,768]{2,1,0:T(8,128)(2,1)}, f32[2,768]{1,0:T(2,128)S(1)}) custom-call(s32[10]{0:T(128)S(1)} %pad_add_fusion.ids.refs_0_, f32[256,768]{1,0:T(8,128)S(1)} %get-tuple-element.176.mine_ref, bf16[256,768]{1,0:T(8,128)(2,1)S(1)} %collective-permute-done.21.sent_ref, bf16[1024,768]{1,0:T(8,128)(2,1)S(1)} %copy-done.1, s32[8,1024]{1,0:T(8,128)S(1)} %bitcast.44, ...), custom_call_target="tpu_custom_call" | custom-call | flops 11500000 | bytes 1 | tf_op jit(solution)/shard_map/last/pallas_call | solution.py:690
  122.0 6.8 %table_grads.5.ver_a = f32[8,32]{1,0:T(8,128)S(1)} custom-call(s32[10]{0:T(128)S(1)} %pad_add_fusion.ids.refs_0_, bf16[3,1024,512]{2,1,0:T(8,128)(2,1)S(1)} %get-tuple-element.172.s_ref, s32[1,1024]{1,0:T(1,128)S(1)} %bitcast.26, s32[1,1024]{1,0:T(1,128)S(1)} %bitcast.27, s32[1,1024]{1,0:T(1,128)S(1)} %bitcast.28), custom_call_target="tpu_custom_call" | custom-call | flops 11500000 | bytes 1 | tf_op jit(solution)/shard_map/table_grads/pallas_call | solution.py:591
  131.3 6.8 %table_grads.6.hor_b = f32[8,32]{1,0:T(8,128)S(1)} custom-call(s32[10]{0:T(128)S(1)} %pad_add_fusion.ids.refs_0_, bf16[3,1024,512]{2,1,0:T(8,128)(2,1)S(1)} %get-tuple-element.193.s_ref, s32[1,1024]{1,0:T(1,128)S(1)} %bitcast.38, s32[1,1024]{1,0:T(1,128)S(1)} %bitcast.39, s32[1,1024]{1,0:T(1,128)S(1)} %bitcast.40, ...), custom_call_target="tpu_custom_call" | custom-call | flops 11500000256 | bytes 1 | tf_op jit(solution)/shard_map/table_grads/pallas_call | solution.py:591
  140.9 3.2 %collective-permute-start.28 = (bf16[96,768]{1,0:T(8,128)(2,1)}, bf16[96,768]{1,0:T(8,128)(2,1)}, u32[]{:S(2)}, u32[]{:S(2)}) collective-permute-start(bf16[96,768]{1,0:T(8,128)(2,1)} %get-tuple-element.200), channel_id=1, source_target_pairs={{0,8},{4,12},{8,0},{12,4},{16,24},{20,28},{24,16},{28,20},{1,9},{5... | collective-permute-start | bytes 442376 | tf_op jit(solution)/shard_map/ppermute | solution.py:956
  146.6 6.7 %table_grads.7.ver_b = f32[8,32]{1,0:T(8,128)S(1)} custom-call(s32[10]{0:T(128)S(1)} %pad_add_fusion.ids.refs_0_, bf16[3,1024,512]{2,1,0:T(8,128)(2,1)S(1)} %get-tuple-element.193.s_ref, s32[1,1024]{1,0:T(1,128)S(1)} %bitcast.29, s32[1,1024]{1,0:T(1,128)S(1)} %bitcast.30, s32[1,1024]{1,0:T(1,128)S(1)} %bitcast.31), custom_call_target="tpu_custom_call" | custom-call | flops 11500000 | bytes 1 | tf_op jit(solution)/shard_map/table_grads/pallas_call | solution.py:591
  154.0 4.4 %collective-permute-done.29.a2 = bf16[96,768]{1,0:T(8,128)(2,1)} collective-permute-done((bf16[96,768]{1,0:T(8,128)(2,1)}, bf16[96,768]{1,0:T(8,128)(2,1)}, u32[]{:S(2)}, u32[]{:S(2)}) %collective-permute-start.29) | collective-permute-done | bytes 147488 | tf_op jit(solution)/shard_map/ppermute | solution.py:956
  158.4 1.9 %head_final.1 = (f32[96,192]{1,0:T(8,128)}, f32[96,192]{1,0:T(8,128)}, f32[96,192]{1,0:T(8,128)}, f32[192,96]{1,0:T(8,128)}) custom-call(f32[96,768]{1,0:T(8,128)S(1)} %get-tuple-element.198.a0, bf16[96,768]{1,0:T(8,128)(2,1)} %collective-permute-done.28.a1, bf16[96,768]{1,0:T(8,128)(2,1)} %collective-permute-done.29.a2, ...), custom_call_target="tpu_custom_call" | custom-call | flops 1150000000 | bytes 1 | tf_op jit(solution)/shard_map/head_final/pallas_call | solution.py:943
  160.3 2.7 %collective-permute-start.35 = (f32[24,128]{1,0:T(8,128)S(1)}, f32[24,128]{1,0:T(8,128)S(1)}, u32[]{:S(2)}, u32[]{:S(2)}) collective-permute-start(f32[24,128]{1,0:T(8,128)S(1)} %add.17), channel_id=1, source_target_pairs={{0,8},{4,12},{8,0},{12,4},{16,24},{20,28},{24,16},{28,20},{1,9},{5... | collective-permute-start | bytes 36872 | tf_op jit(solution)/shard_map/ppermute | solution.py:956
  163.0 3.6 %join_output.1 = bf16[1024,768]{1,0:T(8,128)(2,1)} custom-call(s32[10]{0:T(128)S(1)} %pad_add_fusion.ids.refs_0_, bf16[2,256,768]{2,1,0:T(8,128)(2,1)} %get-tuple-element.210.b0, bf16[2,256,768]{2,1,0:T(8,128)(2,1)} %collective-permute-done.32.b1, bf16[2,256,768]{2,1,0:T(8,128)(2,1)} %collective-permute-done.33.b2, ...), custom_call_target="tpu_custom_call" | custom-call | flops 11500000256 | bytes 1 | tf_op jit(solution)/shard_map/join_output/pallas_call | solution.py:795
  167.8 4.4 %join_grads.1 = (f32[1024,768]{1,0:T(8,128)}, f32[8,768]{1,0:T(8,128)}) custom-call(s32[10]{0:T(128)S(1)} %pad_add_fusion.ids.refs_0_, bf16[2,256,768]{2,1,0:T(8,128)(2,1)} %get-tuple-element.210.b0, bf16[2,256,768]{2,1,0:T(8,128)(2,1)} %collective-permute-done.32.b1, bf16[2,256,768]{2,1,0:T(8,128)(2,1)} %collective-permute-done.33.b2, ...), custom_call_target="tpu_custom_call" | custom-call | flops 11500000256 | bytes 1 | tf_op jit(solution)/shard_map/join_grads/pallas_call | solution.py:795
  (124 shorter events, 29.8 us)
Async XLA Ops:
  0.6 42.4 %collective-permute-start.7 = (bf16[192,768]{1,0:T(8,128)(2,1)}, bf16[192,768]{1,0:T(8,128)(2,1)S(1)}, u32[]{:S(2)}, u32[]{:S(2)}) collective-permute-start(bf16[192,768]{1,0:T(8,128)(2,1)} %o0.5), channel_id=1, source_target_pairs={{0,1},{1,0},{2,3},{3,2},{4,5},{5,4},{6,7},{7,6},{8,9},{9,8},{10,11... | collective-permute-start | bytes 884744 | tf_op jit(solution)/shard_map/ppermute | solution.py:956
  1.2 14.7 %collective-permute-start = (bf16[192,768]{1,0:T(8,128)(2,1)}, bf16[192,768]{1,0:T(8,128)(2,1)S(1)}, u32[]{:S(2)}, u32[]{:S(2)}) collective-permute-start(bf16[192,768]{1,0:T(8,128)(2,1)} %o0.5), channel_id=1, source_target_pairs={{0,2},{1,3},{2,0},{3,1},{4,6},{5,7},{6,4},{7,5},{8,10},{9,11},{10,... | collective-permute-start | bytes 884744 | tf_op jit(solution)/shard_map/ppermute | solution.py:956
  15.3 14.3 %collective-permute-start.2 = (bf16[768,768]{1,0:T(8,128)(2,1)S(1)}, bf16[768,768]{1,0:T(8,128)(2,1)S(1)}, u32[]{:S(2)}, u32[]{:S(2)}) collective-permute-start(bf16[768,768]{1,0:T(8,128)(2,1)S(1)} %copy-done.15), channel_id=1, source_target_pairs={{0,1},{1,0},{2,3},{3,2},{4,5},{5,4},{6,7},{7,6},{8,9},{9,8},{10,11... | collective-permute-start | bytes 3538952 | tf_op jit(solution)/shard_map/ppermute | solution.py:956
  15.5 14.1 %collective-permute-start.3 = (bf16[768,768]{1,0:T(8,128)(2,1)S(1)}, bf16[768,768]{1,0:T(8,128)(2,1)S(1)}, u32[]{:S(2)}, u32[]{:S(2)}) collective-permute-start(bf16[768,768]{1,0:T(8,128)(2,1)S(1)} %copy-done.16), channel_id=1, source_target_pairs={{0,1},{1,0},{2,3},{3,2},{4,5},{5,4},{6,7},{7,6},{8,9},{9,8},{10,11... | collective-permute-start | bytes 3538952 | tf_op jit(solution)/shard_map/ppermute | solution.py:956
  15.8 11.8 %collective-permute-start.1 = (bf16[192,768]{1,0:T(8,128)(2,1)S(1)}, bf16[192,768]{1,0:T(8,128)(2,1)S(1)}, u32[]{:S(2)}, u32[]{:S(2)}) collective-permute-start(bf16[192,768]{1,0:T(8,128)(2,1)S(1)} %collective-permute-done.o2), channel_id=1, source_target_pairs={{0,1},{1,0},{2,3},{3,2},{4,5},{5,4},{6,7},{7,6},{8,9},{9,8},{10,11... | collective-permute-start | bytes 884744 | tf_op jit(solution)/shard_map/ppermute | solution.py:956
  27.5 13.8 %collective-permute-start.6 = (bf16[192,256]{1,0:T(8,128)(2,1)S(1)}, bf16[192,256]{1,0:T(8,128)(2,1)S(1)}, u32[]{:S(2)}, u32[]{:S(2)}) collective-permute-start(bf16[192,256]{1,0:T(8,128)(2,1)S(1)} %get-tuple-element.136.a1), channel_id=1, source_target_pairs={{0,3},{1,2},{2,1},{3,0},{4,7},{5,6},{6,5},{7,4},{8,11},{9,10},{10,... | collective-permute-start | bytes 294920 | tf_op jit(solution)/shard_map/ppermute | solution.py:956
  27.6 13.8 %collective-permute-start.5 = (bf16[192,256]{1,0:T(8,128)(2,1)S(1)}, bf16[192,256]{1,0:T(8,128)(2,1)S(1)}, u32[]{:S(2)}, u32[]{:S(2)}) collective-permute-start(bf16[192,256]{1,0:T(8,128)(2,1)S(1)} %get-tuple-element.138.a0), channel_id=1, source_target_pairs={{0,2},{1,3},{2,0},{3,1},{4,6},{5,7},{6,4},{7,5},{8,10},{9,11},{10,... | collective-permute-start | bytes 294920 | tf_op jit(solution)/shard_map/ppermute | solution.py:956
  40.8 10.3 %collective-permute-start.8 = (bf16[192,256]{1,0:T(8,128)(2,1)S(1)}, bf16[192,256]{1,0:T(8,128)(2,1)S(1)}, u32[]{:S(2)}, u32[]{:S(2)}) collective-permute-start(bf16[192,256]{1,0:T(8,128)(2,1)S(1)} %get-tuple-element.136.a1), channel_id=1, source_target_pairs={{0,1},{1,0},{2,3},{3,2},{4,5},{5,4},{6,7},{7,6},{8,9},{9,8},{10,11... | collective-permute-start | bytes 294920 | tf_op jit(solution)/shard_map/ppermute | solution.py:956
  41.3 9.8 %collective-permute-start.10 = (bf16[192,256]{1,0:T(8,128)(2,1)S(1)}, bf16[192,256]{1,0:T(8,128)(2,1)S(1)}, u32[]{:S(2)}, u32[]{:S(2)}) collective-permute-start(bf16[192,256]{1,0:T(8,128)(2,1)S(1)} %get-tuple-element.135.a3), channel_id=1, source_target_pairs={{0,3},{1,2},{2,1},{3,0},{4,7},{5,6},{6,5},{7,4},{8,11},{9,10},{10,... | collective-permute-start | bytes 294920 | tf_op jit(solution)/shard_map/ppermute | solution.py:956
  41.4 9.7 %collective-permute-start.9 = (bf16[192,256]{1,0:T(8,128)(2,1)S(1)}, bf16[192,256]{1,0:T(8,128)(2,1)S(1)}, u32[]{:S(2)}, u32[]{:S(2)}) collective-permute-start(bf16[192,256]{1,0:T(8,128)(2,1)S(1)} %get-tuple-element.134.a0.a2), channel_id=1, source_target_pairs={{0,2},{1,3},{2,0},{3,1},{4,6},{5,7},{6,4},{7,5},{8,10},{9,11},{10,... | collective-permute-start | bytes 294920 | tf_op jit(solution)/shard_map/ppermute | solution.py:956
  50.7 11.2 %collective-permute-start.12 = (bf16[256,768]{1,0:T(8,128)(2,1)S(1)}, bf16[256,768]{1,0:T(8,128)(2,1)S(1)}, u32[]{:S(2)}, u32[]{:S(2)}) collective-permute-start(bf16[256,768]{1,0:T(8,128)(2,1)S(1)} %get-tuple-element.142), channel_id=1, source_target_pairs={{0,2},{1,3},{2,0},{3,1},{4,6},{5,7},{6,4},{7,5},{8,10},{9,11},{10,... | collective-permute-start | bytes 1179656 | tf_op jit(solution)/shard_map/ppermute | solution.py:956
  51.1 6.9 %collective-permute-start.11 = (bf16[3,256,768]{2,1,0:T(8,128)(2,1)S(1)}, bf16[3,256,768]{2,1,0:T(8,128)(2,1)S(1)}, u32[]{:S(2)}, u32[]{:S(2)}) collective-permute-start(bf16[3,256,768]{2,1,0:T(8,128)(2,1)S(1)} %get-tuple-element.140.n1), channel_id=1, source_target_pairs={{0,1},{1,0},{2,3},{3,2},{4,5},{5,4},{6,7},{7,6},{8,9},{9,8},{10,11... | collective-permute-start | bytes 3538952 | tf_op jit(solution)/shard_map/ppermute | solution.py:956
  63.6 7.3 %collective-permute-start.15 = (bf16[64,768]{1,0:T(8,128)(2,1)S(1)}, bf16[64,768]{1,0:T(8,128)(2,1)S(1)}, u32[]{:S(2)}, u32[]{:S(2)}) collective-permute-start(bf16[64,768]{1,0:T(8,128)(2,1)S(1)} %get-tuple-element.154), channel_id=1, source_target_pairs={{0,3},{1,2},{2,1},{3,0},{4,7},{5,6},{6,5},{7,4},{8,11},{9,10},{10,... | collective-permute-start | bytes 294920 | tf_op jit(solution)/shard_map/ppermute | solution.py:956
  64.0 18.2 %collective-permute-start.13 = (bf16[320,768]{1,0:T(8,128)(2,1)S(1)}, bf16[320,768]{1,0:T(8,128)(2,1)S(1)}, u32[]{:S(2)}, u32[]{:S(2)}) collective-permute-start(bf16[320,768]{1,0:T(8,128)(2,1)S(1)} %get-tuple-element.144), channel_id=1, source_target_pairs={{0,2},{1,3},{2,0},{3,1},{4,6},{5,7},{6,4},{7,5},{8,10},{9,11},{10,... | collective-permute-start | bytes 1474568 | tf_op jit(solution)/shard_map/ppermute | solution.py:956
  65.7 6.6 %collective-permute-start.16 = (bf16[320,768]{1,0:T(8,128)(2,1)S(1)}, bf16[320,768]{1,0:T(8,128)(2,1)S(1)}, u32[]{:S(2)}, u32[]{:S(2)}) collective-permute-start(bf16[320,768]{1,0:T(8,128)(2,1)S(1)} %get-tuple-element.156.l0), channel_id=1, source_target_pairs={{0,1},{1,0},{2,3},{3,2},{4,5},{5,4},{6,7},{7,6},{8,9},{9,8},{10,11... | collective-permute-start | bytes 1474568 | tf_op jit(solution)/shard_map/ppermute | solution.py:956
  70.8 28.2 %collective-permute-start.19 = (bf16[4,96,1536]{2,1,0:T(8,128)(2,1)}, bf16[4,96,1536]{2,1,0:T(8,128)(2,1)S(1)}, u32[]{:S(2)}, u32[]{:S(2)}) collective-permute-start(bf16[4,96,1536]{2,1,0:T(8,128)(2,1)} %get-tuple-element.167), channel_id=1, source_target_pairs={{0,4},{4,0},{8,12},{12,8},{16,20},{20,16},{24,28},{28,24},{1,5},{5... | collective-permute-start | bytes 3538952 | tf_op jit(solution)/shard_map/ppermute | solution.py:956
  82.2 11.6 %collective-permute-start.17 = (bf16[320,768]{1,0:T(8,128)(2,1)S(1)}, bf16[320,768]{1,0:T(8,128)(2,1)S(1)}, u32[]{:S(2)}, u32[]{:S(2)}) collective-permute-start(bf16[320,768]{1,0:T(8,128)(2,1)S(1)} %collective-permute-done.13.refs_8_.l2), channel_id=1, source_target_pairs={{0,1},{1,0},{2,3},{3,2},{4,5},{5,4},{6,7},{7,6},{8,9},{9,8},{10,11... | collective-permute-start | bytes 1474568 | tf_op jit(solution)/shard_map/ppermute | solution.py:956
  82.3 11.5 %collective-permute-start.18 = (bf16[256,768]{1,0:T(8,128)(2,1)S(1)}, bf16[256,768]{1,0:T(8,128)(2,1)S(1)}, u32[]{:S(2)}, u32[]{:S(2)}) collective-permute-start(bf16[256,768]{1,0:T(8,128)(2,1)S(1)} %get-tuple-element.165), channel_id=1, source_target_pairs={{0,2},{1,3},{2,0},{3,1},{4,6},{5,7},{6,4},{7,5},{8,10},{9,11},{10,... | collective-permute-start | bytes 1179656 | tf_op jit(solution)/shard_map/ppermute | solution.py:956
  94.9 7.9 %collective-permute-start.20 = (bf16[2,256,768]{2,1,0:T(8,128)(2,1)S(1)}, bf16[2,256,768]{2,1,0:T(8,128)(2,1)S(1)}, u32[]{:S(2)}, u32[]{:S(2)}) collective-permute-start(bf16[2,256,768]{2,1,0:T(8,128)(2,1)S(1)} %terms_send.1), channel_id=1, source_target_pairs={{0,1},{1,0},{2,3},{3,2},{4,5},{5,4},{6,7},{7,6},{8,9},{9,8},{10,11... | collective-permute-start | bytes 2359304 | tf_op jit(solution)/shard_map/ppermute | solution.py:956
  101.3 17.8 %collective-permute-start.22 = (bf16[4,96,768]{2,1,0:T(8,128)(2,1)S(1)}, bf16[4,96,768]{2,1,0:T(8,128)(2,1)S(1)}, u32[]{:S(2)}, u32[]{:S(2)}) collective-permute-start(bf16[4,96,768]{2,1,0:T(8,128)(2,1)S(1)} %get-tuple-element.184), channel_id=1, source_target_pairs={{0,4},{4,0},{8,12},{12,8},{16,20},{20,16},{24,28},{28,24},{1,5},{5... | collective-permute-start | bytes 1769480 | tf_op jit(solution)/shard_map/ppermute | solution.py:956
  104.0 12.7 %collective-permute-start.21 = (bf16[256,768]{1,0:T(8,128)(2,1)S(1)}, bf16[256,768]{1,0:T(8,128)(2,1)S(1)}, u32[]{:S(2)}, u32[]{:S(2)}) collective-permute-start(bf16[256,768]{1,0:T(8,128)(2,1)S(1)} %get-tuple-element.177), channel_id=1, source_target_pairs={{0,2},{1,3},{2,0},{3,1},{4,6},{5,7},{6,4},{7,5},{8,10},{9,11},{10,... | collective-permute-start | bytes 1179656 | tf_op jit(solution)/shard_map/ppermute | solution.py:956
  105.3 23.5 %collective-permute-start.23 = (bf16[96,1536]{1,0:T(8,128)(2,1)S(1)}, bf16[96,1536]{1,0:T(8,128)(2,1)S(1)}, u32[]{:S(2)}, u32[]{:S(2)}) collective-permute-start(bf16[96,1536]{1,0:T(8,128)(2,1)S(1)} %get-tuple-element.188), channel_id=1, source_target_pairs={{0,8},{4,12},{8,0},{12,4},{16,24},{20,28},{24,16},{28,20},{1,9},{5... | collective-permute-start | bytes 884744 | tf_op jit(solution)/shard_map/ppermute | solution.py:956
  106.9 23.5 %collective-permute-start.24 = (bf16[96,1536]{1,0:T(8,128)(2,1)S(1)}, bf16[96,1536]{1,0:T(8,128)(2,1)S(1)}, u32[]{:S(2)}, u32[]{:S(2)}) collective-permute-start(bf16[96,1536]{1,0:T(8,128)(2,1)S(1)} %get-tuple-element.189), channel_id=1, source_target_pairs={{0,16},{4,20},{8,24},{12,28},{16,0},{20,4},{24,8},{28,12},{1,17},{... | collective-permute-start | bytes 884744 | tf_op jit(solution)/shard_map/ppermute | solution.py:956
  109.6 20.9 %collective-permute-start.25 = (bf16[96,1536]{1,0:T(8,128)(2,1)S(1)}, bf16[96,1536]{1,0:T(8,128)(2,1)S(1)}, u32[]{:S(2)}, u32[]{:S(2)}) collective-permute-start(bf16[96,1536]{1,0:T(8,128)(2,1)S(1)} %get-tuple-element.190), channel_id=1, source_target_pairs={{0,24},{4,28},{8,16},{12,20},{16,8},{20,12},{24,0},{28,4},{1,25},{... | collective-permute-start | bytes 884744 | tf_op jit(solution)/shard_map/ppermute | solution.py:956
  119.1 12.2 %collective-permute-start.26 = (f32[2,768]{1,0:T(2,128)S(1)}, f32[2,768]{1,0:T(2,128)S(1)}, u32[]{:S(2)}, u32[]{:S(2)}) collective-permute-start(f32[2,768]{1,0:T(2,128)S(1)} %get-tuple-element.192), channel_id=1, source_target_pairs={{0,1},{1,0},{2,3},{3,2},{4,5},{5,4},{6,7},{7,6},{8,9},{9,8},{10,11... | collective-permute-start | bytes 18440 | tf_op jit(solution)/shard_map/ppermute | solution.py:956
  119.1 20.3 %collective-permute-start.33 = (bf16[2,256,768]{2,1,0:T(8,128)(2,1)}, bf16[2,256,768]{2,1,0:T(8,128)(2,1)}, u32[]{:S(2)}, u32[]{:S(2)}) collective-permute-start(bf16[2,256,768]{2,1,0:T(8,128)(2,1)} %get-tuple-element.210.b0), channel_id=1, source_target_pairs={{0,2},{1,3},{2,0},{3,1},{4,6},{5,7},{6,4},{7,5},{8,10},{9,11},{10,... | collective-permute-start | bytes 2359304 | tf_op jit(solution)/shard_map/ppermute | solution.py:956
  128.8 34.3 %collective-permute-start.32 = (bf16[2,256,768]{2,1,0:T(8,128)(2,1)}, bf16[2,256,768]{2,1,0:T(8,128)(2,1)}, u32[]{:S(2)}, u32[]{:S(2)}) collective-permute-start(bf16[2,256,768]{2,1,0:T(8,128)(2,1)} %get-tuple-element.210.b0), channel_id=1, source_target_pairs={{0,1},{1,0},{2,3},{3,2},{4,5},{5,4},{6,7},{7,6},{8,9},{9,8},{10,11... | collective-permute-start | bytes 2359304 | tf_op jit(solution)/shard_map/ppermute | solution.py:956
  139.4 23.7 %collective-permute-start.34 = (bf16[2,256,768]{2,1,0:T(8,128)(2,1)}, bf16[2,256,768]{2,1,0:T(8,128)(2,1)}, u32[]{:S(2)}, u32[]{:S(2)}) collective-permute-start(bf16[2,256,768]{2,1,0:T(8,128)(2,1)} %collective-permute-done.33.b2), channel_id=1, source_target_pairs={{0,1},{1,0},{2,3},{3,2},{4,5},{5,4},{6,7},{7,6},{8,9},{9,8},{10,11... | collective-permute-start | bytes 2359304 | tf_op jit(solution)/shard_map/ppermute | solution.py:956
  140.9 12.5 %collective-permute-start.28 = (bf16[96,768]{1,0:T(8,128)(2,1)}, bf16[96,768]{1,0:T(8,128)(2,1)}, u32[]{:S(2)}, u32[]{:S(2)}) collective-permute-start(bf16[96,768]{1,0:T(8,128)(2,1)} %get-tuple-element.200), channel_id=1, source_target_pairs={{0,8},{4,12},{8,0},{12,4},{16,24},{20,28},{24,16},{28,20},{1,9},{5... | collective-permute-start | bytes 442376 | tf_op jit(solution)/shard_map/ppermute | solution.py:956
  144.1 14.3 %collective-permute-start.29 = (bf16[96,768]{1,0:T(8,128)(2,1)}, bf16[96,768]{1,0:T(8,128)(2,1)}, u32[]{:S(2)}, u32[]{:S(2)}) collective-permute-start(bf16[96,768]{1,0:T(8,128)(2,1)} %get-tuple-element.202), channel_id=1, source_target_pairs={{0,16},{4,20},{8,24},{12,28},{16,0},{20,4},{24,8},{28,12},{1,17},{... | collective-permute-start | bytes 442376 | tf_op jit(solution)/shard_map/ppermute | solution.py:956
  145.1 13.2 %collective-permute-start.30 = (bf16[96,768]{1,0:T(8,128)(2,1)}, bf16[96,768]{1,0:T(8,128)(2,1)}, u32[]{:S(2)}, u32[]{:S(2)}) collective-permute-start(bf16[96,768]{1,0:T(8,128)(2,1)} %get-tuple-element.204), channel_id=1, source_target_pairs={{0,24},{4,28},{8,16},{12,20},{16,8},{20,12},{24,0},{28,4},{1,25},{... | collective-permute-start | bytes 442376 | tf_op jit(solution)/shard_map/ppermute | solution.py:956
  153.4 6.9 %collective-permute-start.31 = (f32[24,128]{1,0:T(8,128)S(1)}, f32[24,128]{1,0:T(8,128)S(1)}, u32[]{:S(2)}, u32[]{:S(2)}) collective-permute-start(f32[24,128]{1,0:T(8,128)S(1)} %pack.1), channel_id=1, source_target_pairs={{0,4},{4,0},{8,12},{12,8},{16,20},{20,16},{24,28},{28,24},{1,5},{5... | collective-permute-start | bytes 36872 | tf_op jit(solution)/shard_map/ppermute | solution.py:956
  (29 other events, 190.2 us)
